TPU v7x, 128 devices: a whole 4x4x4 slice. The times are simulated.
128 devices in a mesh: grp: 2 (over z_lo), ep: 32 (over z_hi, y, x), rep: 2 (over core).
Axes of the slice: x: 4, y: 4, z: 4 (z_hi: 2, z_lo: 2; z = z_hi * 2 + z_lo), core: 2. Of those that a mesh axis runs over, the one named last changes fastest.
Arguments:
- teacher_in: bfloat16 [128, 7168], P('ep'), may hold values from -6 to 6
- teacher_gain: float32 [7168], replicated, may hold values from 0.5 to 1.5
- routes: int32 [128, 8], P('ep'), may hold values from 0 to 31, all different within a row; in each aligned block of 4 rows (0 to 3, 4 to 7, ...) at most 2 rows name the same one
- gates: float32 [128, 8], P('ep'), may hold values from 0.1 to 0.6
- expert_gate: bfloat16 [32, 7168, 1024], P('ep', None, ('grp', 'rep')), may hold values from -0.0625 to 0.0625
- expert_up: bfloat16 [32, 7168, 1024], P('ep', None, ('grp', 'rep')), may hold values from -0.0625 to 0.0625
- expert_down: bfloat16 [32, 1024, 7168], P('ep', ('grp', 'rep')), may hold values from -0.1875 to 0.1875
- projection: bfloat16 [7168, 8192], P(None, ('grp', 'ep', 'rep')), may hold values from -0.0625 to 0.0625
- student_in: bfloat16 [128, 8192], P(None, ('grp', 'ep', 'rep')), may hold values from -6 to 6
- student_gain: float32 [8192], replicated, may hold values from 0.5 to 1.5
- student_gate: bfloat16 [8192, 14336], P(None, ('grp', 'ep', 'rep')), may hold values from -0.0625 to 0.0625
- student_up: bfloat16 [8192, 14336], P(None, ('grp', 'ep', 'rep')), may hold values from -0.0625 to 0.0625
- student_down: bfloat16 [14336, 8192], P(('grp', 'ep', 'rep')), may hold values from -0.1875 to 0.1875
Outputs:
- grad_gate: bfloat16 [8192, 14336], P(None, ('grp', 'ep', 'rep'))
- grad_up: bfloat16 [8192, 14336], P(None, ('grp', 'ep', 'rep'))
- grad_down: bfloat16 [14336, 8192], P(('grp', 'ep', 'rep'))
- mse: float32 [], replicated
Inputs may be any that keep to these rules, and one draw needn't show every extreme that they name: `routes`: each token names 8 different experts. Among the 4 tokens of one index of ep, at most 2 tokens name one expert, and in every draw some expert is named by exactly 2 of them.
All inputs are finite; a program needn't handle non-finite values.
Results may differ from a plain program's by a relative error of at most 0.015.
Values may be sent and summed in bfloat16 or wider, within the bound.
No kernel may reach another device: no remote copies, remote signals or barrier semaphores. Data moves between devices by JAX's collectives and lax.ppermute only.
A program may use at most 128 MiB of HBM per device.

v0:
```python
import math

import jax
import jax.numpy as jnp
from jax import lax
from jax.sharding import PartitionSpec as P


def rms_norm(values, scale_gain):
    floats = values.astype(jnp.float32)
    factor = lax.rsqrt(jnp.mean(floats * floats, axis=-1, keepdims=True) + 1e-05)
    return (floats * factor * scale_gain).astype(jnp.bfloat16)


def local(
    teacher_in,
    teacher_gain,
    routes,
    gates,
    expert_gate,
    expert_up,
    expert_down,
    projection,
    student_in,
    student_gain,
    student_gate,
    student_up,
    student_down,
):
    experts = lax.axis_size("ep")
    rows_here = teacher_in.shape[0]
    route_count = routes.shape[1]
    model_width = teacher_in.shape[1]
    capacity = min(rows_here, max(2, 2 * rows_here * route_count // experts))
    teacher_normed = rms_norm(teacher_in, teacher_gain)
    flat_routes = routes.reshape(-1)
    onehot = (flat_routes[:, None] == jnp.arange(experts, dtype=jnp.int32)[None, :]).astype(
        jnp.int32
    )
    earlier = jnp.cumsum(onehot, axis=0) - onehot
    slot_of = jnp.sum(earlier * onehot, axis=1)
    target_slot = flat_routes * capacity + slot_of
    selector = (
        target_slot[:, None] == jnp.arange(experts * capacity, dtype=jnp.int32)[None, :]
    ).astype(jnp.bfloat16)
    picker = selector.reshape(rows_here, route_count, -1).sum(axis=1)
    outgoing = lax.dot_general(
        picker, teacher_normed, (((0,), (0,)), ((), ())), preferred_element_type=jnp.float32
    )
    outgoing = outgoing.astype(jnp.bfloat16).reshape(experts, capacity, model_width)
    arrived = lax.all_to_all(outgoing, "ep", split_axis=0, concat_axis=0, tiled=True)
    slot_count = arrived.shape[1]
    stacked = arrived.reshape(-1, model_width)
    gate_pre = jnp.dot(stacked, expert_gate[0], preferred_element_type=jnp.float32)
    up_pre = jnp.dot(stacked, expert_up[0], preferred_element_type=jnp.float32)
    hidden = (jax.nn.silu(gate_pre) * up_pre).astype(jnp.bfloat16)
    result = jnp.dot(hidden, expert_down[0], preferred_element_type=jnp.float32).astype(
        jnp.bfloat16
    )
    result = result.reshape(experts, slot_count, model_width)
    returned = lax.all_to_all(result, "ep", split_axis=0, concat_axis=0, tiled=True)
    slot_rows = jnp.take(
        returned.reshape(experts * capacity, model_width), target_slot, axis=0
    ).astype(jnp.float32)
    moe_part = jnp.sum(
        slot_rows.reshape(rows_here, route_count, model_width) * gates[:, :, None], axis=1
    )
    moe = lax.psum(moe_part.astype(jnp.bfloat16), ("grp", "rep")).astype(jnp.float32)
    teacher_out = (teacher_in.astype(jnp.float32) + moe).astype(jnp.bfloat16)
    target = jnp.dot(
        lax.all_gather(teacher_out, "ep", axis=0, tiled=True),
        projection,
        preferred_element_type=jnp.float32,
    )
    whole_in = lax.all_gather(student_in, ("grp", "ep", "rep"), axis=1, tiled=True)
    tokens = whole_in.shape[0]
    student_normed = rms_norm(whole_in, student_gain)
    gate_pre = jnp.dot(student_normed, student_gate, preferred_element_type=jnp.float32)
    up_pre = jnp.dot(student_normed, student_up, preferred_element_type=jnp.float32)
    act = (jax.nn.silu(gate_pre) * up_pre).astype(jnp.bfloat16)
    branch_rows = lax.psum_scatter(
        lax.dot_general(
            student_down, act, (((0,), (1,)), ((), ())), preferred_element_type=jnp.float32
        ),
        ("grp", "ep", "rep"),
        scatter_dimension=0,
        tiled=True,
    )
    diff_rows = student_in.T.astype(jnp.float32) + branch_rows - target.T
    total_sq = lax.psum(jnp.sum(diff_rows * diff_rows), ("grp", "ep", "rep"))
    mse = total_sq / (tokens * whole_in.shape[1])
    delta_rows = (diff_rows / math.sqrt(tokens)).astype(jnp.bfloat16)
    delta_all = lax.all_gather(delta_rows, ("grp", "ep", "rep"), axis=0, tiled=True)
    grad_down = lax.dot_general(
        act, delta_all, (((0,), (1,)), ((), ())), preferred_element_type=jnp.float32
    ).astype(jnp.bfloat16)
    back_act = lax.dot_general(
        delta_all, student_down, (((0,), (1,)), ((), ())), preferred_element_type=jnp.float32
    )
    sigmoid_g = jax.nn.sigmoid(gate_pre)
    d_gate = (back_act * up_pre * sigmoid_g * (1.0 + gate_pre * (1.0 - sigmoid_g))).astype(
        jnp.bfloat16
    )
    d_up = (back_act * gate_pre * sigmoid_g).astype(jnp.bfloat16)
    grad_gate = lax.dot_general(
        student_normed, d_gate, (((0,), (0,)), ((), ())), preferred_element_type=jnp.float32
    ).astype(jnp.bfloat16)
    grad_up = lax.dot_general(
        student_normed, d_up, (((0,), (0,)), ((), ())), preferred_element_type=jnp.float32
    ).astype(jnp.bfloat16)
    return (grad_gate, grad_up, grad_down, mse)


def solution(mesh):
    placed = (
        P("ep", None),
        P(),
        P("ep", None),
        P("ep", None),
        P("ep", None, ("grp", "rep")),
        P("ep", None, ("grp", "rep")),
        P("ep", ("grp", "rep"), None),
        P(None, ("grp", "ep", "rep")),
        P(None, ("grp", "ep", "rep")),
        P(),
        P(None, ("grp", "ep", "rep")),
        P(None, ("grp", "ep", "rep")),
        P(("grp", "ep", "rep"), None),
    )
    return jax.shard_map(
        local,
        mesh=mesh,
        in_specs=placed,
        out_specs=(
            P(None, ("grp", "ep", "rep")),
            P(None, ("grp", "ep", "rep")),
            P(("grp", "ep", "rep"), None),
            P(),
        ),
        check_vma=False,
    )
```

profile of v0, /device:TPU:1, one launch (start us, length us, event | category | flops | bytes accessed | tf_op | source)
XLA Modules:
  0.0 1177.0 jit_solution(18030770418990852681)
XLA Ops:
  7.2 0.0 copy-start
  7.2 0.9 reshape.99
  8.1 0.1 fusion.33
  8.2 0.1 reduce_window_sum.11
  8.2 0.2 select_reduce_fusion
  8.4 0.1 reduce_sum.63
  8.5 0.7 compare_and_fusion
  9.2 0.1 fusion.35
  9.3 1.0 fusion.17
  10.3 1.3 convolution_convert_fusion.3
  11.6 1.3 reshape.100
  12.8 11.3 all-to-all-start
  24.1 0.0 all-gather.5.cloned.1.call-start
  24.2 0.7 all-gather.5.cloned.1.call-update
  24.9 14.8 %all-to-all-done = bf16[32,2,7168]{2,1,0:T(2,128)(2,1)} async-done(((bf16[32,2,7168]{2,1,0:T(2,128)(2,1)}), bf16[32,2,7168]{2,1,0:T(2,128)(2,1)}, u32[]{:S(2)}, u32[]{:S(2)}) %all-to-all-start) | async-done | bytes 917536 | tf_op jit(solution)/shard_map/all_to_all | solution.py:51
  39.6 2.5 reshape.101
  42.1 2.8 fusion.6
  44.9 6.4 convolution_convert_fusion.4
  51.3 3.1 reshape.102
  54.4 4.7 all-to-all-start.1
  59.0 0.0 all-gather.9.cloned.1.call-start
  59.1 0.0 copy-done.7
  59.1 0.1 mul.123
  59.2 14.7 %all-to-all-done.1 = bf16[32,2,7168]{2,1,0:T(2,128)(2,1)} async-done(((bf16[32,2,7168]{2,1,0:T(2,128)(2,1)}), bf16[32,2,7168]{2,1,0:T(2,128)(2,1)}, u32[]{:S(2)}, u32[]{:S(2)}) %all-to-all-start.1) | async-done | bytes 917536 | tf_op jit(solution)/shard_map/all_to_all | solution.py:61
  73.9 2.5 reshape.103
  76.3 0.0 copy-start.8
  76.4 0.0 copy-start.5
  76.4 0.8 gather_fusion
  77.2 0.0 copy-start.10
  77.2 0.0 copy-done.8
  77.2 0.4 multiply_reduce_fusion
  77.6 13.4 %psum.14 = bf16[4,7168]{1,0:T(4,128)(2,1)S(1)} all-reduce(bf16[4,7168]{1,0:T(4,128)(2,1)S(1)} %multiply_reduce_fusion), channel_id=1, replica_groups=mesh['grp'=2,'ep'=32,'rep'=2] {'grp','rep'}, use_global_device_ids=true, to_apply=%region_7.8 | all-reduce | flops 28672 | bytes 114688 | tf_op jit(solution)/shard_map/psum | solution.py:68
  91.1 0.0 copy-done.5
  91.1 0.7 fusion.26
  91.7 0.0 all-gather.9.cloned.1.call-update
  91.8 0.2 reduce-scatter.4.cloned.1.call-start
  92.0 136.3 %all-gather.5.cloned.1.call-done = bf16[128,8192]{0,1:T(8,128)(2,1)} async-done(((bf16[128,64]{0,1:T(8,128)(2,1)}), bf16[128,8192]{0,1:T(8,128)(2,1)}) %all-gather.5.cloned.1.call-update) | async-done | bytes 2097168 | tf_op jit(solution)/shard_map/all_gather | solution.py:75
  228.3 2.8 fusion
  231.1 0.0 copy-done.10
  231.1 0.0 copy-done.2
  231.1 0.0 copy-start.9
  231.1 3.1 fusion.43
  234.3 0.0 copy-done.9
  234.3 1.5 multiply_convert_fusion.2
  235.8 0.0 copy-done
  235.8 2.7 convolution_bitcast_fusion
  238.5 5.6 copy.21
  244.1 0.0 reduce-scatter.4.cloned.1.call-update
  244.1 0.0 copy-start.4
  244.2 0.0 copy-start.6
  244.2 0.0 all-gather.7.cloned.1.call-start
  244.2 55.5 %all-gather.9.cloned.1.call-done = bf16[32,4,7168]{2,1,0:T(4,128)(2,1)} async-done(((bf16[1,4,7168]{2,1,0:T(4,128)(2,1)}), bf16[32,4,7168]{2,1,0:T(4,128)(2,1)}) %all-gather.9.cloned.1.call-update) | async-done | bytes 1835024 | tf_op jit(solution)/shard_map/all_gather | solution.py:71
  299.7 3.9 reshape.113
  303.6 634.5 %reduce-scatter.4.cloned.1.call-done = f32[64,128]{1,0:T(8,128)} async-done(((f32[8192,128]{1,0:T(8,128)}), f32[64,128]{1,0:T(8,128)}) %reduce-scatter.4.cloned.1.call-update) | async-done | bytes 32784 | tf_op jit(solution)/shard_map/reduce_scatter | solution.py:81
  938.1 0.0 copy-done.4
  938.1 0.0 copy-done.6
  938.1 3.5 multiply_reduce_fusion.1
  941.6 0.0 all-gather.7.cloned.1.call-update
  941.6 85.6 %psum.15 = f32[]{:T(128)} all-reduce(f32[]{:T(128)} %get-tuple-element.6), channel_id=1, replica_groups=mesh['grp'=2,'ep'=32,'rep'=2] {'grp','ep','rep'}, use_global_device_ids=true, to_apply=%region_9.10 | all-reduce | flops 1 | bytes 8 | tf_op jit(solution)/shard_map/psum | solution.py:90
  1027.8 127.2 %all-gather.7.cloned.1.call-done = bf16[8192,128]{1,0:T(8,128)(2,1)} async-done(((bf16[64,128]{1,0:T(8,128)(2,1)}), bf16[8192,128]{1,0:T(8,128)(2,1)}) %all-gather.7.cloned.1.call-update) | async-done | bytes 2097168 | tf_op jit(solution)/shard_map/all_gather | solution.py:93
  1155.0 2.4 fusion.48
  1157.4 2.0 convolution_convert_fusion
  1159.4 5.0 convolution_convert_fusion.1
  1164.3 5.0 convolution_convert_fusion.2
  (11 shorter events, 0.0 us)
Async XLA Ops:
  7.2 228.6 %copy-start = (bf16[112,8192]{1,0:T(8,128)(2,1)S(1)}, bf16[112,8192]{1,0:T(8,128)(2,1)}, u32[]{:S(2)}) copy-start(bf16[112,8192]{1,0:T(8,128)(2,1)} %param.25) | copy-start | bytes 5505028
  12.8 26.8 %all-to-all-start = ((bf16[32,2,7168]{2,1,0:T(2,128)(2,1)}), bf16[32,2,7168]{2,1,0:T(2,128)(2,1)}, u32[]{:S(2)}, u32[]{:S(2)}) async-start(bf16[32,2,7168]{2,1,0:T(2,128)(2,1)} %reshape.100), calls=%async_computation | async-start | bytes 1835008 | tf_op jit(solution)/shard_map/all_to_all | solution.py:51
  24.1 204.1 %all-gather.5.cloned.1.call-start = ((), (), s32[]{:S(2)}) async-start(), calls=%async_computation.3 | async-start | bytes 2113536 | tf_op jit(solution)/shard_map/all_gather | solution.py:75
  51.3 7.8 copy-start.7
  54.4 19.5 %all-to-all-start.1 = ((bf16[32,2,7168]{2,1,0:T(2,128)(2,1)}), bf16[32,2,7168]{2,1,0:T(2,128)(2,1)}, u32[]{:S(2)}, u32[]{:S(2)}) async-start(bf16[32,2,7168]{2,1,0:T(2,128)(2,1)} %reshape.102), calls=%async_computation.1 | async-start | bytes 1835008 | tf_op jit(solution)/shard_map/all_to_all | solution.py:61
  59.0 240.7 %all-gather.9.cloned.1.call-start = ((), (), s32[]{:S(2)}) async-start(), calls=%async_computation.5 | async-start | bytes 1892352 | tf_op jit(solution)/shard_map/all_gather | solution.py:71
  76.3 0.9 copy-start.8
  76.4 14.7 %copy-start.5 = (bf16[4,7168]{1,0:T(4,128)(2,1)S(1)}, bf16[4,7168]{1,0:T(4,128)(2,1)}, u32[]{:S(2)}) copy-start(bf16[4,7168]{1,0:T(4,128)(2,1)} %param.13) | copy-start | bytes 172036
  77.2 153.9 %copy-start.10 = (f32[8192]{0:T(1024)S(1)}, f32[8192]{0:T(1024)}, u32[]{:S(2)}) copy-start(f32[8192]{0:T(1024)} %param.22) | copy-start | bytes 98308
  91.8 846.3 %reduce-scatter.4.cloned.1.call-start = ((), (), s32[]{:S(2)}) async-start(), calls=%async_computation.6 | async-start | bytes 4227072 | tf_op jit(solution)/shard_map/reduce_scatter | solution.py:81
  228.3 2.9 copy-start.2
  231.1 3.1 copy-start.9
  244.1 694.0 %copy-start.4 = (bf16[7168,64]{0,1:T(8,128)(2,1)S(1)}, bf16[7168,64]{0,1:T(8,128)(2,1)}, u32[]{:S(2)}) copy-start(bf16[7168,64]{0,1:T(8,128)(2,1)} %param.20) | copy-start | bytes 2752516
  244.2 694.0 %copy-start.6 = (bf16[128,64]{0,1:T(8,128)(2,1)S(1)}, bf16[128,64]{0,1:T(8,128)(2,1)}, u32[]{:S(2)}) copy-start(bf16[128,64]{0,1:T(8,128)(2,1)} %param.21) | copy-start | bytes 49156
  244.2 910.9 %all-gather.7.cloned.1.call-start = ((), (), s32[]{:S(2)}) async-start(), calls=%async_computation.4 | async-start | bytes 2113536 | tf_op jit(solution)/shard_map/all_gather | solution.py:93
  1155.0 2.4 copy-start.1
  1157.4 2.0 copy-start.3
Sparse Core Ops, SparseCore 0:
  26.7 201.5 all-gather.4
  231.8 67.8 all-gather.8
  302.1 635.9 reduce-scatter.3
  941.7 213.2 all-gather.6
where the time goes:
time: 1180 us
  waiting for transfers between devices  984 us (83%)
  blocking collectives  99 us (8%)
  matrix products  35.5 us (3%)
  local copies, waits for them, and re-layouts  20.8 us (2%)
  starting transfers between devices  16.3 us (1%)
  between operations  15.8 us (1%)
    reduce_scatter x1, waiting for transfers between devices, local(): lax.psum_scatter(lax.dot_general(student_down, act, (((0,), (1,)), ((), (...  634 us
    all_gather x1, waiting for transfers between devices, local(): lax.all_gather(student_in, ('grp', 'ep', 'rep'), axis=1, tiled=True)  136 us
    all_gather x1, waiting for transfers between devices, local(): lax.all_gather(delta_rows, ('grp', 'ep', 'rep'), axis=0, tiled=True)  127 us
    psum x1, blocking collectives, local(): total_sq = lax.psum(jnp.sum(diff_rows * diff_rows), ('grp', 'ep', 'rep'))  85.6 us
    all_gather x1, waiting for transfers between devices, local(): lax.all_gather(teacher_out, 'ep', axis=0, tiled=True)  55.5 us
  transfers between devices with their start and end apart: 6, of which 6 were waited for; matrix products, arithmetic and copies ran while one was open for 3% of the time, Pallas kernels for 0%

commit v1 on v0

v1 whole, which is shorter than its diff:
```python
import math

import jax
import jax.numpy as jnp
from jax import lax
from jax.experimental import pallas as pl
from jax.experimental.pallas import tpu as pltpu
from jax.sharding import PartitionSpec as P

CHIPS = ("grp", "ep")
NN = (((1,), (0,)), ((), ()))
NT = (((1,), (1,)), ((), ()))
TN = (((0,), (0,)), ((), ()))
VMEM_BYTES = 56 * 1024 * 1024


def dot(a, b, dims=NN):
    return lax.dot_general(a, b, dims, preferred_element_type=jnp.float32)


def silu(v):
    return v / (1.0 + jnp.exp(-v))


def params():
    return pltpu.CompilerParams(vmem_limit_bytes=VMEM_BYTES)


def vmem():
    return pl.BlockSpec(memory_space=pltpu.VMEM)


def anywhere():
    return pl.BlockSpec(memory_space=pl.ANY)


def exchange(blocks):
    return lax.all_to_all(blocks, CHIPS, split_axis=0, concat_axis=0, tiled=True)


def spread(block):
    chips = lax.axis_size(CHIPS)
    return exchange(jnp.broadcast_to(block[None], (chips,) + block.shape))


def other_core(values):
    return lax.ppermute(values, "rep", [(0, 1), (1, 0)])


def expert_kernel(
    mine, other, gain, weight, gate_hbm, up_hbm, down_hbm, keep, send, gate_w, up_w, down_w, sems
):
    half = mine.shape[1]
    core = lax.axis_index("rep")
    first = pl.multiple_of(core * half, half)
    second = pl.multiple_of((1 - core) * half, half)
    copies = []
    for n, start in enumerate((first, second)):
        rows = pl.ds(start, half)
        for m, (src, dst) in enumerate(((gate_hbm, gate_w), (up_hbm, up_w))):
            copies.append(pltpu.make_async_copy(src.at[rows], dst.at[n], sems.at[2 * n + m]))
    copies.append(pltpu.make_async_copy(down_hbm, down_w, sems.at[4]))
    for copy in copies:
        copy.start()
    floats = [mine[...].astype(jnp.float32), other[...].astype(jnp.float32)]
    squares = sum(jnp.sum(v * v, axis=1, keepdims=True) for v in floats)
    factor = lax.rsqrt(squares / (2 * half) + 1e-05)
    gains = [gain[pl.ds(core, 1), :], gain[pl.ds(1 - core, 1), :]]
    normed = [(v * factor * g).astype(jnp.bfloat16) for v, g in zip(floats, gains)]
    copies[0].wait()
    gate_pre = dot(normed[0], gate_w[0])
    copies[1].wait()
    up_pre = dot(normed[0], up_w[0])
    copies[2].wait()
    gate_pre += dot(normed[1], gate_w[1])
    copies[3].wait()
    up_pre += dot(normed[1], up_w[1])
    hidden = (silu(gate_pre) * up_pre).astype(jnp.bfloat16)
    copies[4].wait()
    scale = weight[...]
    is_first = (lax.axis_index("grp") == 0) & (lax.axis_index("ep") == 0)
    own = jnp.where(is_first, 1.0, 0.0)
    width = 512
    for n in range(half // width):
        here = slice(n * width, (n + 1) * width)
        columns = pl.ds(pl.multiple_of(second + n * width, width), width)
        out = dot(hidden, down_w[:, columns]) * scale
        send[here, :] = out.T.astype(jnp.bfloat16)
    for n in range(half // width):
        here = slice(n * width, (n + 1) * width)
        columns = pl.ds(pl.multiple_of(first + n * width, width), width)
        out = dot(hidden, down_w[:, columns]) * scale
        out += mine[:, here].astype(jnp.float32) * own
        keep[here, :] = out.T


def experts(mine, other, gain, weight, w_gate, w_up, w_down):
    tokens, half = mine.shape
    hidden = w_gate.shape[1]
    return pl.pallas_call(
        expert_kernel,
        out_shape=(
            jax.ShapeDtypeStruct((half, tokens), jnp.float32),
            jax.ShapeDtypeStruct((half, tokens), jnp.bfloat16),
        ),
        in_specs=[vmem()] * 4 + [anywhere()] * 3,
        out_specs=(vmem(), vmem()),
        scratch_shapes=[
            pltpu.VMEM((2, half, hidden), jnp.bfloat16),
            pltpu.VMEM((2, half, hidden), jnp.bfloat16),
            pltpu.VMEM((hidden, 2 * half), jnp.bfloat16),
            pltpu.SemaphoreType.DMA((5,)),
        ],
        compiler_params=params(),
        name="experts",
    )(mine, other, gain, weight, w_gate, w_up, w_down)


def prepare_kernel(gate, up, gain, scaled):
    rows = gate.shape[0]
    scaled[:rows, :] = (gate[...].astype(jnp.float32) * gain[...]).astype(jnp.bfloat16)
    scaled[rows:, :] = (up[...].astype(jnp.float32) * gain[...]).astype(jnp.bfloat16)


def prepare(gate, up, gain):
    rows, width = gate.shape
    return pl.pallas_call(
        prepare_kernel,
        out_shape=jax.ShapeDtypeStruct((2 * rows, width), jnp.bfloat16),
        in_specs=[vmem()] * 3,
        out_specs=vmem(),
        compiler_params=params(),
        name="prepare",
    )(gate, up, gain)


def start_interleaved(mine, other, dst, sems):
    core = lax.axis_index("rep")
    copies = [
        pltpu.make_async_copy(mine, dst.at[:, core], sems.at[0]),
        pltpu.make_async_copy(other, dst.at[:, 1 - core], sems.at[1]),
    ]
    for copy in copies:
        copy.start()
    return copies


def forward_kernel(mine, other, scaled, down, keep, send, act_ref, pre_ref, factor_ref, x, sems):
    core = lax.axis_index("rep")
    chips, _, rows, tokens = x.shape
    features = chips * 2 * rows
    for copy in start_interleaved(mine, other, x, sems):
        copy.wait()
    values = x[...].reshape(features, tokens)
    floats = values.astype(jnp.float32)
    factor = lax.rsqrt(jnp.sum(floats * floats, axis=0, keepdims=True) / features + 1e-05)
    factor_ref[...] = factor
    pre = dot(scaled[...], values) * factor
    pre_ref[...] = pre
    hidden = pre.shape[0] // 2
    act = (silu(pre[:hidden]) * pre[hidden:]).astype(jnp.bfloat16)
    act_ref[...] = act
    step = 8
    width = step * 2 * rows
    for n in range(chips // step):
        part = dot(down[:, n * width : (n + 1) * width], act, TN).reshape(step, 2, rows, tokens)
        here = slice(n * step, (n + 1) * step)
        low, high = part[:, 0], part[:, 1]
        keep[here] = jnp.where(core == 0, low, high)
        send[here] = jnp.where(core == 0, high, low).astype(jnp.bfloat16)


def forward(mine, other, scaled, down):
    chips, rows, tokens = mine.shape
    hidden = down.shape[0]
    return pl.pallas_call(
        forward_kernel,
        out_shape=(
            jax.ShapeDtypeStruct((chips, rows, tokens), jnp.float32),
            jax.ShapeDtypeStruct((chips, rows, tokens), jnp.bfloat16),
            jax.ShapeDtypeStruct((hidden, tokens), jnp.bfloat16),
            jax.ShapeDtypeStruct((2 * hidden, tokens), jnp.float32),
            jax.ShapeDtypeStruct((1, tokens), jnp.float32),
        ),
        in_specs=[anywhere()] * 2 + [vmem()] * 2,
        out_specs=(vmem(),) * 5,
        scratch_shapes=[
            pltpu.VMEM((chips, 2, rows, tokens), jnp.bfloat16),
            pltpu.SemaphoreType.DMA((2,)),
        ],
        compiler_params=params(),
        name="forward",
    )(mine, other, scaled, down)


def delta_kernel(mine, other, projection, partials, student_in, delta):
    core = lax.axis_index("rep")
    half, tokens = mine.shape
    first = pl.multiple_of(core * half, half)
    second = pl.multiple_of((1 - core) * half, half)
    target = dot(projection[:, pl.ds(first, half)], mine[...])
    target += dot(projection[:, pl.ds(second, half)], other[...])
    branch = jnp.sum(partials[...].astype(jnp.float32), axis=0)
    diff = student_in[...].astype(jnp.float32) + branch - target
    scaled = (diff / math.sqrt(tokens)).astype(jnp.bfloat16)
    delta[...] = jnp.broadcast_to(scaled[None], delta.shape)


def deltas(mine, other, projection, partials, student_in):
    return pl.pallas_call(
        delta_kernel,
        out_shape=jax.ShapeDtypeStruct(partials.shape, jnp.bfloat16),
        in_specs=[vmem()] * 5,
        out_specs=vmem(),
        compiler_params=params(),
        name="deltas",
    )(mine, other, projection, partials, student_in)


def backward_kernel(
    d_mine,
    d_other,
    x_mine,
    x_other,
    down,
    act,
    pre,
    factor,
    gain,
    grad_gate,
    grad_up,
    grad_down,
    mse,
    d,
    x,
    sems_d,
    sems_x,
):
    chips, _, rows, tokens = x.shape
    features = chips * 2 * rows
    copies_d = start_interleaved(d_mine, d_other, d, sems_d)
    copies_x = start_interleaved(x_mine, x_other, x, sems_x)
    for copy in copies_d:
        copy.wait()
    hidden = act.shape[0]
    delta = d[...].reshape(features, tokens)
    back = dot(down[...], delta)
    gate_pre, up_pre = pre[:hidden], pre[hidden:]
    sigmoid = 1.0 / (1.0 + jnp.exp(-gate_pre))
    d_gate = back * up_pre * sigmoid * (1.0 + gate_pre * (1.0 - sigmoid))
    d_up = back * gate_pre * sigmoid
    scale = factor[...]
    d_both = jnp.concatenate([d_gate * scale, d_up * scale], axis=0).astype(jnp.bfloat16)
    step = 8
    width = step * 2 * rows
    acts = act[...]
    total = jnp.zeros((1, tokens), jnp.float32)
    for n in range(chips // step):
        here = slice(n * width, (n + 1) * width)
        part = d[n * step : (n + 1) * step].reshape(width, tokens)
        grad_down[:, here] = dot(acts, part, NT).astype(jnp.bfloat16)
        floats = part.astype(jnp.float32)
        total += jnp.sum(floats * floats, axis=0, keepdims=True)
    mse[...] = jnp.sum(total, axis=1, keepdims=True) / features
    for copy in copies_x:
        copy.wait()
    for n in range(chips // step):
        here = slice(n * width, (n + 1) * width)
        part = x[n * step : (n + 1) * step].reshape(width, tokens)
        grads = dot(d_both, part, NT) * gain[:, here]
        grad_gate[:, here] = grads[:hidden].astype(jnp.bfloat16)
        grad_up[:, here] = grads[hidden:].astype(jnp.bfloat16)


def backward(d_mine, d_other, x_mine, x_other, down, act, pre, factor, gain):
    chips, rows, tokens = d_mine.shape
    hidden, features = down.shape
    grad = jax.ShapeDtypeStruct((hidden, features), jnp.bfloat16)
    whole = pltpu.VMEM((chips, 2, rows, tokens), jnp.bfloat16)
    return pl.pallas_call(
        backward_kernel,
        out_shape=(grad, grad, grad, jax.ShapeDtypeStruct((1, 1), jnp.float32)),
        in_specs=[anywhere()] * 4 + [vmem()] * 5,
        out_specs=(vmem(),) * 4,
        scratch_shapes=[
            whole,
            whole,
            pltpu.SemaphoreType.DMA((2,)),
            pltpu.SemaphoreType.DMA((2,)),
        ],
        compiler_params=params(),
        name="backward",
    )(d_mine, d_other, x_mine, x_other, down, act, pre, factor, gain)


def local(
    teacher_in,
    teacher_gain,
    routes,
    gates,
    expert_gate,
    expert_up,
    expert_down,
    projection,
    student_in,
    student_gain,
    student_gate,
    student_up,
    student_down,
):
    groups, experts_in_all, cores = (lax.axis_size(a) for a in ("grp", "ep", "rep"))
    chips = groups * experts_in_all
    group, expert, core = (lax.axis_index(a) for a in ("grp", "ep", "rep"))
    rows_here, model_width = teacher_in.shape
    tokens = rows_here * experts_in_all
    quarter = model_width // (groups * cores)
    lanes = 128

    ids = jnp.arange(experts_in_all, dtype=jnp.int32)
    weights = jnp.sum(
        jnp.where(routes[:, :, None] == ids[None, None, :], gates[:, :, None], 0.0), axis=1
    )
    weights_high = lax.reduce_precision(weights, exponent_bits=8, mantissa_bits=7)
    weights_low = weights - weights_high
    both = jnp.stack([weights_high, weights_low]).astype(jnp.bfloat16).reshape(2, lanes)
    part = lax.dynamic_slice_in_dim(teacher_in, (core * groups + group) * quarter, quarter, axis=1)
    data_rows = rows_here * quarter // lanes
    block = jnp.concatenate([part.reshape(data_rows, lanes), both], axis=0)
    block = jnp.pad(block, ((0, 64 - block.shape[0]), (0, 0)))
    arrived = spread(block)
    arrived_other = other_core(arrived)

    def tokens_of(blocks):
        cut = blocks[:, :data_rows].reshape(groups, experts_in_all, rows_here, quarter)
        return cut.transpose(1, 2, 0, 3).reshape(tokens, groups * quarter)

    weight_rows = arrived[:experts_in_all, data_rows : data_rows + 2].astype(jnp.float32)
    weight_all = weight_rows.sum(axis=1).reshape(tokens, experts_in_all)
    weight_here = lax.dynamic_slice_in_dim(weight_all, expert, 1, axis=1)
    keep, send = experts(
        tokens_of(arrived),
        tokens_of(arrived_other),
        teacher_gain.reshape(cores, -1),
        weight_here,
        expert_gate[0],
        expert_up[0],
        expert_down[0],
    )
    moe = (keep + other_core(send).astype(jnp.float32)).astype(jnp.bfloat16)
    moe = exchange(moe.reshape(chips, -1, tokens))
    teacher_out = jnp.sum(moe.astype(jnp.float32), axis=0).astype(jnp.bfloat16)
    teacher_mine = spread(teacher_out)
    teacher_other = other_core(teacher_mine)

    student_t = student_in.T
    gain_row = student_gain[None, :]
    scaled = prepare(student_gate.T, student_up.T, gain_row)
    x_mine = spread(student_t)
    x_other = other_core(x_mine)
    s_keep, s_send, act, pre, factor = forward(x_mine, x_other, scaled, student_down)
    sums = (s_keep + other_core(s_send).astype(jnp.float32)).astype(jnp.bfloat16)
    partials = exchange(sums)

    delta = deltas(
        teacher_mine.reshape(-1, tokens),
        teacher_other.reshape(-1, tokens),
        projection.T,
        partials,
        student_t,
    )
    d_mine = exchange(delta)
    d_other = other_core(d_mine)
    grad_gate, grad_up, grad_down, mse = backward(
        d_mine, d_other, x_mine, x_other, student_down, act, pre, factor, gain_row
    )
    return (grad_gate.T, grad_up.T, grad_down, mse.reshape(()))


def solution(mesh):
    everything = ("grp", "ep", "rep")
    placed = (
        P("ep", None),
        P(),
        P("ep", None),
        P("ep", None),
        P("ep", None, ("grp", "rep")),
        P("ep", None, ("grp", "rep")),
        P("ep", ("grp", "rep"), None),
        P(None, everything),
        P(None, everything),
        P(),
        P(None, everything),
        P(None, everything),
        P(everything, None),
    )
    return jax.shard_map(
        local,
        mesh=mesh,
        in_specs=placed,
        out_specs=(P(None, everything), P(None, everything), P(everything, None), P()),
        check_vma=False,
    )
```

time: 1180 us -> 178 us (0.15)
  waiting for transfers between devices: 984 us -> 35.9 us
  blocking collectives: 99 us -> 50.2 us
  matrix products: 35.5 us -> 0 us
  Pallas kernels: 0 us -> 32.6 us
  starting transfers between devices: 16.3 us -> 35.8 us
  between operations: 15.8 us -> 0.98 us
    reduce_scatter x1 -> x0, waiting for transfers between devices: 634 us -> none  [local(): lax.psum_scatter(lax.dot_general(student_down, act, (((0,), (1,)), ((), (...]
    all_gather x3 -> x0, waiting for transfers between devices: 319 us -> none  [the longest x1 136 us: local(): lax.all_gather(student_in, ('grp', 'ep', 'rep'), axis=1, tiled=True)]
    psum x2 -> x0, blocking collectives: 99 us -> none  [the longest x1 85.6 us: local(): total_sq = lax.psum(jnp.sum(diff_rows * diff_rows), ('grp', 'ep', 'rep'))]
    all_to_all x0 -> x2, blocking collectives: none -> 50.2 us  [exchange(): lax.all_to_all(blocks, CHIPS, split_axis=0, concat_axis=0, tiled=True)]
    dot_general x11 -> x0, matrix products: 35.5 us -> none  [the longest x1 6.39 us: local(): jnp.dot(hidden, expert_down[0], preferred_element_type=jnp.float32)]
    pallas_call x0 -> x5, Pallas kernels: none -> 32.6 us  [the longest x1 8.66 us: experts(): pl.pallas_call(expert_kernel, out_shape=(jax.ShapeDtypeStruct((half, toke...]
    all_to_all x2 -> x4, starting transfers between devices: 16 us -> 26.2 us  [exchange(): lax.all_to_all(blocks, CHIPS, split_axis=0, concat_axis=0, tiled=True)]
    all_to_all x2 -> x4, waiting for transfers between devices: 29.4 us -> 32.2 us  [exchange(): lax.all_to_all(blocks, CHIPS, split_axis=0, concat_axis=0, tiled=True)]
  transfers between devices with their start and end apart: 6 -> 10, of which waited for: 6 -> 5; matrix products, arithmetic and copies ran while one was open for 3% -> 10% of each run, Pallas kernels for 0% -> 12%
where the time goes in v1:
time: 178 us
  blocking collectives  50.2 us (28%)
  waiting for transfers between devices  35.9 us (20%)
  starting transfers between devices  35.8 us (20%)
  Pallas kernels  32.6 us (18%)
  local copies, waits for them, and re-layouts  15.6 us (9%)
  other arithmetic  6.59 us (4%)
    all_to_all x2, blocking collectives, exchange(): lax.all_to_all(blocks, CHIPS, split_axis=0, concat_axis=0, tiled=True)  50.2 us
    all_to_all x4, waiting for transfers between devices, exchange(): lax.all_to_all(blocks, CHIPS, split_axis=0, concat_axis=0, tiled=True)  32.2 us
    all_to_all x4, starting transfers between devices, exchange(): lax.all_to_all(blocks, CHIPS, split_axis=0, concat_axis=0, tiled=True)  26.2 us
    ppermute x6, starting transfers between devices, other_core(): return lax.ppermute(values, 'rep', [(0, 1), (1, 0)])  9.59 us
    pallas_call x1, Pallas kernels, experts(): pl.pallas_call(expert_kernel, out_shape=(jax.ShapeDtypeStruct((half, toke...  8.66 us
    pallas_call x1, Pallas kernels, backward(): pl.pallas_call(backward_kernel, out_shape=(grad, grad, grad, jax.ShapeDty...  8.17 us
    pallas_call x1, Pallas kernels, forward(): pl.pallas_call(forward_kernel, out_shape=(jax.ShapeDtypeStruct((chips, ro...  7.72 us
    unnamed x22, local copies, waits for them, and re-layouts  5.32 us
  transfers between devices with their start and end apart: 10, of which 5 were waited for; matrix products, arithmetic and copies ran while one was open for 10% of the time, Pallas kernels for 12%

profile of v1, /device:TPU:1, one launch (start us, length us, event | category | flops | bytes accessed | tf_op | source)
XLA Modules:
  0.0 177.6 jit_solution(5619580735601632038)
XLA Ops:
  0.6 0.0 copy-start
  0.6 0.0 copy-start.8
  0.7 0.8 select_reduce_fusion
  1.5 0.1 reduce_sum.33
  1.6 0.0 copy-done
  1.6 0.2 broadcast_in_dim.22
  1.9 29.4 %all_to_all.30 = bf16[64,64,128]{2,1,0:T(8,128)(2,1)S(1)} all-to-all(bf16[64,64,128]{2,1,0:T(8,128)(2,1)S(1)} %broadcast_in_dim.22), channel_id=1, replica_groups=mesh['grp'=2,'ep'=32,'rep'=2] {'grp','ep'}, dimensions={0} | all-to-all | bytes 2097152 | tf_op jit(solution)/shard_map/all_to_all | solution.py:38
  31.3 0.0 copy-start.9
  31.3 2.2 %collective-permute-start = (bf16[64,64,128]{2,1,0:T(8,128)(2,1)S(1)}, bf16[64,64,128]{2,1,0:T(8,128)(2,1)}, u32[]{:S(2)}, u32[]{:S(2)}) collective-permute-start(bf16[64,64,128]{2,1,0:T(8,128)(2,1)S(1)} %all_to_all.30), channel_id=1, source_target_pairs={{0,1},{1,0},{2,3},{3,2},{4,5},{5,4},{6,7},{7,6},{8,9},{9,8},{10,11... | collective-permute-start | bytes 3145736 | tf_op jit(solution)/shard_map/ppermute | solution.py:47
  33.5 0.0 copy-done.8
  33.5 1.2 broadcast_in_dim.40
  34.7 4.7 %all-to-all-start.3 = ((bf16[64,64,128]{2,1,0:T(8,128)(2,1)}), bf16[64,64,128]{2,1,0:T(8,128)(2,1)S(1)}, u32[]{:S(2)}, u32[]{:S(2)}) async-start(bf16[64,64,128]{2,1,0:T(8,128)(2,1)} %broadcast_in_dim.40), calls=%async_computation.3 | async-start | bytes 2097152 | tf_op jit(solution)/shard_map/all_to_all | solution.py:38
  39.4 0.0 copy-done.9
  39.4 0.6 reshape.76.gain
  40.0 0.1 reshape.77
  40.1 1.0 slice.12
  41.1 1.9 %reshape.72 = bf16[2,32,4,1792]{3,2,1,0:T(4,128)(2,1)S(1)} reshape(bf16[64,56,128]{2,1,0:T(8,128)(2,1)} %slice.12) | data formatting | bytes 1835008 | tf_op jit(solution)/shard_map/reshape | solution.py:334
  43.0 0.9 copy.19
  43.9 1.0 copy.21
  45.0 0.7 constant_dynamic-slice_fusion.weight
  45.7 0.0 collective-permute-done
  45.7 1.3 slice.13
  46.9 0.3 reshape.74
  47.2 0.9 copy.20
  48.1 1.1 copy.22
  49.2 8.7 %experts.1 = (f32[3584,128]{1,0:T(8,128)}, bf16[3584,128]{1,0:T(8,128)(2,1)}) custom-call(bf16[128,3584]{1,0:T(8,128)(2,1)} %bitcast.27, bf16[128,3584]{1,0:T(8,128)(2,1)} %bitcast.28, f32[2,3584]{1,0:T(2,128)} %reshape.76.gain, f32[128,1]{1,0:T(8,128)} %constant_dynamic-slice_fusion.weight, bf16[7168,256]{1,0:T(8,128)(2,1)} %bitcast.29, ...), custom_call_target="tpu_custom_call" | custom-call | tf_op jit(solution)/shard_map/experts/pallas_call | solution.py:100
  57.9 0.1 collective-permute-start.1
  57.9 0.0 all-to-all-done.3.mine.x_mine
  58.0 0.0 copy-start.1
  58.0 1.2 collective-permute-start.3
  59.2 1.4 collective-permute-done.1
  60.6 2.6 %add_convert_fusion.1 = bf16[3584,128]{1,0:T(8,128)(2,1)} fusion(f32[3584,128]{1,0:T(8,128)} %get-tuple-element.15, bf16[3584,128]{1,0:T(8,128)(2,1)S(1)} %collective-permute-done.1), kind=kLoop, calls=%fused_computation.1 | loop fusion | flops 1376256 | bytes 3670016 | tf_op jit(solution)/shard_map/convert_element_type | solution.py:349
  63.3 0.0 copy-done.1
  63.3 9.8 %all-to-all-start.1 = ((bf16[64,56,128]{2,1,0:T(8,128)(2,1)}), bf16[64,56,128]{2,1,0:T(8,128)(2,1)S(1)}, u32[]{:S(2)}, u32[]{:S(2)}) async-start(bf16[64,56,128]{2,1,0:T(8,128)(2,1)} %bitcast.5), calls=%async_computation.1 | async-start | bytes 1835008 | tf_op jit(solution)/shard_map/all_to_all | solution.py:38
  73.1 4.4 %prepare.1.scaled = bf16[224,8192]{1,0:T(8,128)(2,1)} custom-call(bf16[112,8192]{1,0:T(8,128)(2,1)} %bitcast.32, bf16[112,8192]{1,0:T(8,128)(2,1)} %bitcast.33, f32[1,8192]{1,0:T(1,128)} %bitcast.36), custom_call_target="tpu_custom_call" | custom-call | tf_op jit(solution)/shard_map/prepare/pallas_call | solution.py:127
  77.5 0.0 collective-permute-done.3.other.x_other
  77.5 0.0 copy-start.4
  77.5 1.0 copy-done.4
  78.5 7.7 %forward.1 = (f32[64,64,128]{2,1,0:T(8,128)}, bf16[64,64,128]{2,1,0:T(8,128)(2,1)}, bf16[112,128]{1,0:T(8,128)(2,1)}, f32[224,128]{1,0:T(8,128)}, f32[1,128]{1,0:T(1,128)}) custom-call(bf16[64,64,128]{2,1,0:T(8,128)(2,1)} %copy-done.1, bf16[64,64,128]{2,1,0:T(8,128)(2,1)} %copy-done.4, bf16[224,8192]{1,0:T(8,128)(2,1)} %prepare.1.scaled, bf16[112,8192]{1,0:T(8,128)(2,1)} %down.3), custom_call_target="tpu_custom_call" | custom-call | tf_op jit(solution)/shard_map/forward/pallas_call | solution.py:176
  86.2 0.6 collective-permute-start.4
  86.9 2.8 %all-to-all-done.1 = bf16[64,56,128]{2,1,0:T(8,128)(2,1)S(1)} async-done(((bf16[64,56,128]{2,1,0:T(8,128)(2,1)}), bf16[64,56,128]{2,1,0:T(8,128)(2,1)S(1)}, u32[]{:S(2)}, u32[]{:S(2)}) %all-to-all-start.1) | async-done | bytes 917536 | tf_op jit(solution)/shard_map/all_to_all | solution.py:38
  89.6 0.2 reduce_sum.35
  89.8 1.0 broadcast_in_dim.23
  90.8 7.0 %all-to-all-start.2 = ((bf16[64,56,128]{2,1,0:T(8,128)(2,1)}), bf16[64,56,128]{2,1,0:T(8,128)(2,1)S(1)}, u32[]{:S(2)}, u32[]{:S(2)}) async-start(bf16[64,56,128]{2,1,0:T(8,128)(2,1)} %broadcast_in_dim.23), calls=%async_computation.2 | async-start | bytes 1835008 | tf_op jit(solution)/shard_map/all_to_all | solution.py:38
  97.9 0.0 collective-permute-done.4
  97.9 2.9 %add_convert_fusion = bf16[64,64,128]{2,1,0:T(8,128)(2,1)} fusion(f32[64,64,128]{2,1,0:T(8,128)} %get-tuple-element.17, bf16[64,64,128]{2,1,0:T(8,128)(2,1)S(1)} %collective-permute-done.4), kind=kLoop, calls=%fused_computation | loop fusion | flops 1572864 | bytes 4194304 | tf_op jit(solution)/shard_map/convert_element_type | solution.py:361
  100.8 14.0 %all-to-all-done.2 = bf16[64,56,128]{2,1,0:T(8,128)(2,1)S(1)} async-done(((bf16[64,56,128]{2,1,0:T(8,128)(2,1)}), bf16[64,56,128]{2,1,0:T(8,128)(2,1)S(1)}, u32[]{:S(2)}, u32[]{:S(2)}) %all-to-all-start.2) | async-done | bytes 917536 | tf_op jit(solution)/shard_map/all_to_all | solution.py:38
  114.8 0.0 copy-start.5
  114.8 4.7 %all-to-all-start.4 = ((bf16[64,64,128]{2,1,0:T(8,128)(2,1)}), bf16[64,64,128]{2,1,0:T(8,128)(2,1)S(1)}, u32[]{:S(2)}, u32[]{:S(2)}) async-start(bf16[64,64,128]{2,1,0:T(8,128)(2,1)} %add_convert_fusion), calls=%async_computation.4 | async-start | bytes 2097152 | tf_op jit(solution)/shard_map/all_to_all | solution.py:38
  119.4 1.6 collective-permute-start.2
  121.1 15.4 %all-to-all-done.4.partials = bf16[64,64,128]{2,1,0:T(8,128)(2,1)S(1)} async-done(((bf16[64,64,128]{2,1,0:T(8,128)(2,1)}), bf16[64,64,128]{2,1,0:T(8,128)(2,1)S(1)}, u32[]{:S(2)}, u32[]{:S(2)}) %all-to-all-start.4) | async-done | bytes 1048608 | tf_op jit(solution)/shard_map/all_to_all | solution.py:38
  136.5 0.0 copy-start.2
  136.5 0.0 collective-permute-done.2
  136.5 0.0 copy-start.7
  136.5 0.0 copy-done.5
  136.5 1.0 copy-done.2
  137.5 0.3 copy-done.7
  137.8 3.6 %deltas.1 = bf16[64,64,128]{2,1,0:T(8,128)(2,1)} custom-call(bf16[3584,128]{1,0:T(8,128)(2,1)} %bitcast.22, bf16[3584,128]{1,0:T(8,128)(2,1)} %bitcast.35, bf16[64,7168]{1,0:T(8,128)(2,1)} %bitcast.34, bf16[64,64,128]{2,1,0:T(8,128)(2,1)} %copy-done.2, bf16[64,128]{1,0:T(8,128)(2,1)} %bitcast.38), custom_call_target="tpu_custom_call" | custom-call | tf_op jit(solution)/shard_map/deltas/pallas_call | solution.py:210
  141.4 20.8 %all_to_all.31.d_mine = bf16[64,64,128]{2,1,0:T(8,128)(2,1)S(1)} all-to-all(bf16[64,64,128]{2,1,0:T(8,128)(2,1)} %deltas.1), channel_id=1, replica_groups=mesh['grp'=2,'ep'=32,'rep'=2] {'grp','ep'}, dimensions={0} | all-to-all | bytes 2097152 | tf_op jit(solution)/shard_map/all_to_all | solution.py:38
  162.2 3.8 %collective-permute-start.5 = (bf16[64,64,128]{2,1,0:T(8,128)(2,1)S(1)}, bf16[64,64,128]{2,1,0:T(8,128)(2,1)S(1)}, u32[]{:S(2)}, u32[]{:S(2)}) collective-permute-start(bf16[64,64,128]{2,1,0:T(8,128)(2,1)S(1)} %all_to_all.31.d_mine), channel_id=1, source_target_pairs={{0,1},{1,0},{2,3},{3,2},{4,5},{5,4},{6,7},{7,6},{8,9},{9,8},{10,11... | collective-permute-start | bytes 3145736 | tf_op jit(solution)/shard_map/ppermute | solution.py:47
  166.0 2.3 %collective-permute-done.5.d_other = bf16[64,64,128]{2,1,0:T(8,128)(2,1)S(1)} collective-permute-done((bf16[64,64,128]{2,1,0:T(8,128)(2,1)S(1)}, bf16[64,64,128]{2,1,0:T(8,128)(2,1)S(1)}, u32[]{:S(2)}, u32[]{:S(2)}) %collective-permute-start.5) | collective-permute-done | bytes 1048608 | tf_op jit(solution)/shard_map/ppermute | solution.py:47
  168.3 0.0 copy-done.3
  168.3 1.0 copy-done.6
  169.3 8.2 %backward.1 = (bf16[112,8192]{1,0:T(8,128)(2,1)}, bf16[112,8192]{1,0:T(8,128)(2,1)}, bf16[112,8192]{1,0:T(8,128)(2,1)}, f32[1,1]{1,0:T(1,128)}) custom-call(bf16[64,64,128]{2,1,0:T(8,128)(2,1)} %copy-done.3, bf16[64,64,128]{2,1,0:T(8,128)(2,1)} %copy-done.6, bf16[64,64,128]{2,1,0:T(8,128)(2,1)} %copy-done.1, bf16[64,64,128]{2,1,0:T(8,128)(2,1)} %copy-done.4, ...), custom_call_target="tpu_custom_call" | custom-call | tf_op jit(solution)/shard_map/backward/pallas_call | solution.py:280
  (7 shorter events, 0.1 us)
Async XLA Ops:
  0.6 0.9 copy-start
  0.6 32.8 %copy-start.8 = (bf16[128,64]{0,1:T(8,128)(2,1)S(1)}, bf16[128,64]{0,1:T(8,128)(2,1)}, u32[]{:S(2)}) copy-start(bf16[128,64]{0,1:T(8,128)(2,1)} %param.21) | copy-start | bytes 49156
  31.3 8.1 %copy-start.9 = (f32[7168]{0:T(1024)S(1)}, f32[7168]{0:T(1024)}, u32[]{:S(2)}) copy-start(f32[7168]{0:T(1024)} %param.14) | copy-start | bytes 86020
  31.3 14.4 %collective-permute-start = (bf16[64,64,128]{2,1,0:T(8,128)(2,1)S(1)}, bf16[64,64,128]{2,1,0:T(8,128)(2,1)}, u32[]{:S(2)}, u32[]{:S(2)}) collective-permute-start(bf16[64,64,128]{2,1,0:T(8,128)(2,1)S(1)} %all_to_all.30), channel_id=1, source_target_pairs={{0,1},{1,0},{2,3},{3,2},{4,5},{5,4},{6,7},{7,6},{8,9},{9,8},{10,11... | collective-permute-start | bytes 3145736 | tf_op jit(solution)/shard_map/ppermute | solution.py:47
  34.7 23.3 %all-to-all-start.3 = ((bf16[64,64,128]{2,1,0:T(8,128)(2,1)}), bf16[64,64,128]{2,1,0:T(8,128)(2,1)S(1)}, u32[]{:S(2)}, u32[]{:S(2)}) async-start(bf16[64,64,128]{2,1,0:T(8,128)(2,1)} %broadcast_in_dim.40), calls=%async_computation.3 | async-start | bytes 2097152 | tf_op jit(solution)/shard_map/all_to_all | solution.py:38
  57.9 2.8 %collective-permute-start.1 = (bf16[3584,128]{1,0:T(8,128)(2,1)}, bf16[3584,128]{1,0:T(8,128)(2,1)S(1)}, u32[]{:S(2)}, u32[]{:S(2)}) collective-permute-start(bf16[3584,128]{1,0:T(8,128)(2,1)} %get-tuple-element.16), channel_id=1, source_target_pairs={{0,1},{1,0},{2,3},{3,2},{4,5},{5,4},{6,7},{7,6},{8,9},{9,8},{10,11... | collective-permute-start | bytes 2752520 | tf_op jit(solution)/shard_map/ppermute | solution.py:47
  58.0 5.3 %copy-start.1 = (bf16[64,64,128]{2,1,0:T(8,128)(2,1)}, bf16[64,64,128]{2,1,0:T(8,128)(2,1)S(1)}, u32[]{:S(2)}) copy-start(bf16[64,64,128]{2,1,0:T(8,128)(2,1)S(1)} %all-to-all-done.3.mine.x_mine) | copy-start | bytes 3145732
  58.0 19.6 %collective-permute-start.3 = (bf16[64,64,128]{2,1,0:T(8,128)(2,1)S(1)}, bf16[64,64,128]{2,1,0:T(8,128)(2,1)S(1)}, u32[]{:S(2)}, u32[]{:S(2)}) collective-permute-start(bf16[64,64,128]{2,1,0:T(8,128)(2,1)S(1)} %all-to-all-done.3.mine.x_mine), channel_id=1, source_target_pairs={{0,1},{1,0},{2,3},{3,2},{4,5},{5,4},{6,7},{7,6},{8,9},{9,8},{10,11... | collective-permute-start | bytes 3145736 | tf_op jit(solution)/shard_map/ppermute | solution.py:47
  63.3 26.4 %all-to-all-start.1 = ((bf16[64,56,128]{2,1,0:T(8,128)(2,1)}), bf16[64,56,128]{2,1,0:T(8,128)(2,1)S(1)}, u32[]{:S(2)}, u32[]{:S(2)}) async-start(bf16[64,56,128]{2,1,0:T(8,128)(2,1)} %bitcast.5), calls=%async_computation.1 | async-start | bytes 1835008 | tf_op jit(solution)/shard_map/all_to_all | solution.py:38
  77.5 1.0 copy-start.4
  86.2 11.6 %collective-permute-start.4 = (bf16[64,64,128]{2,1,0:T(8,128)(2,1)}, bf16[64,64,128]{2,1,0:T(8,128)(2,1)S(1)}, u32[]{:S(2)}, u32[]{:S(2)}) collective-permute-start(bf16[64,64,128]{2,1,0:T(8,128)(2,1)} %get-tuple-element.18), channel_id=1, source_target_pairs={{0,1},{1,0},{2,3},{3,2},{4,5},{5,4},{6,7},{7,6},{8,9},{9,8},{10,11... | collective-permute-start | bytes 3145736 | tf_op jit(solution)/shard_map/ppermute | solution.py:47
  90.8 23.9 %all-to-all-start.2 = ((bf16[64,56,128]{2,1,0:T(8,128)(2,1)}), bf16[64,56,128]{2,1,0:T(8,128)(2,1)S(1)}, u32[]{:S(2)}, u32[]{:S(2)}) async-start(bf16[64,56,128]{2,1,0:T(8,128)(2,1)} %broadcast_in_dim.23), calls=%async_computation.2 | async-start | bytes 1835008 | tf_op jit(solution)/shard_map/all_to_all | solution.py:38
  114.8 21.7 %copy-start.5 = (bf16[64,56,128]{2,1,0:T(8,128)(2,1)}, bf16[64,56,128]{2,1,0:T(8,128)(2,1)S(1)}, u32[]{:S(2)}) copy-start(bf16[64,56,128]{2,1,0:T(8,128)(2,1)S(1)} %all-to-all-done.2) | copy-start | bytes 2752516
  114.8 21.7 %all-to-all-start.4 = ((bf16[64,64,128]{2,1,0:T(8,128)(2,1)}), bf16[64,64,128]{2,1,0:T(8,128)(2,1)S(1)}, u32[]{:S(2)}, u32[]{:S(2)}) async-start(bf16[64,64,128]{2,1,0:T(8,128)(2,1)} %add_convert_fusion), calls=%async_computation.4 | async-start | bytes 2097152 | tf_op jit(solution)/shard_map/all_to_all | solution.py:38
  119.4 17.1 %collective-permute-start.2 = (bf16[64,56,128]{2,1,0:T(8,128)(2,1)S(1)}, bf16[64,56,128]{2,1,0:T(8,128)(2,1)S(1)}, u32[]{:S(2)}, u32[]{:S(2)}) collective-permute-start(bf16[64,56,128]{2,1,0:T(8,128)(2,1)S(1)} %all-to-all-done.2), channel_id=1, source_target_pairs={{0,1},{1,0},{2,3},{3,2},{4,5},{5,4},{6,7},{7,6},{8,9},{9,8},{10,11... | collective-permute-start | bytes 2752520 | tf_op jit(solution)/shard_map/ppermute | solution.py:47
  136.5 1.0 copy-start.2
  136.5 1.3 copy-start.7
  162.2 6.1 %copy-start.3 = (bf16[64,64,128]{2,1,0:T(8,128)(2,1)}, bf16[64,64,128]{2,1,0:T(8,128)(2,1)S(1)}, u32[]{:S(2)}) copy-start(bf16[64,64,128]{2,1,0:T(8,128)(2,1)S(1)} %all_to_all.31.d_mine) | copy-start | bytes 3145732
  162.2 6.1 %collective-permute-start.5 = (bf16[64,64,128]{2,1,0:T(8,128)(2,1)S(1)}, bf16[64,64,128]{2,1,0:T(8,128)(2,1)S(1)}, u32[]{:S(2)}, u32[]{:S(2)}) collective-permute-start(bf16[64,64,128]{2,1,0:T(8,128)(2,1)S(1)} %all_to_all.31.d_mine), channel_id=1, source_target_pairs={{0,1},{1,0},{2,3},{3,2},{4,5},{5,4},{6,7},{7,6},{8,9},{9,8},{10,11... | collective-permute-start | bytes 3145736 | tf_op jit(solution)/shard_map/ppermute | solution.py:47
  168.3 1.0 copy-start.6

commit v2 on v1

v2 whole, which is shorter than its diff:
```python
import math

import jax
import jax.numpy as jnp
from jax import lax
from jax.experimental import pallas as pl
from jax.experimental.pallas import tpu as pltpu
from jax.sharding import PartitionSpec as P

CHIPS = ("grp", "ep")
NN = (((1,), (0,)), ((), ()))
NT = (((1,), (1,)), ((), ()))
TN = (((0,), (0,)), ((), ()))
LANES = 128


def dot(a, b, dims=NN):
    return lax.dot_general(a, b, dims, preferred_element_type=jnp.float32)


def silu(v):
    return v / (1.0 + jnp.exp(-v))


def params(mebibytes):
    return pltpu.CompilerParams(vmem_limit_bytes=mebibytes * 1024 * 1024)


def cost(microseconds):
    size = int(microseconds * 3e6)
    return pl.CostEstimate(flops=0, bytes_accessed=size, transcendentals=0)


def vmem():
    return pl.BlockSpec(memory_space=pltpu.VMEM)


def anywhere():
    return pl.BlockSpec(memory_space=pl.ANY)


def exchange(blocks):
    return lax.all_to_all(blocks, CHIPS, split_axis=0, concat_axis=0, tiled=True)


def other_core(values):
    return lax.ppermute(values, "rep", [(0, 1), (1, 0)])


def slot_weights(routes, gates, experts, copies):
    tokens, _ = routes.shape
    row = lax.broadcasted_iota(jnp.int32, (copies * experts * 2, routes.shape[1]), 0)
    expert, slot = (row // 2) % experts, (row % 2)[:, :1]
    earlier = jnp.zeros(slot.shape, jnp.float32)
    weights = []
    for t in range(tokens):
        hits = routes[t : t + 1, :] == expert
        taken = jnp.sum(jnp.where(hits, 1.0, 0.0), axis=1, keepdims=True)
        value = jnp.sum(jnp.where(hits, gates[t : t + 1, :], 0.0), axis=1, keepdims=True)
        weights.append(jnp.where(earlier == slot.astype(jnp.float32), value, 0.0))
        earlier += taken
    return weights


def padded_pieces(pieces):
    return -(-pieces // 8) * 8


def dispatch_kernel(tokens_hbm, routes_hbm, student_hbm, out, rows, tokens, routes, student, sems):
    pairs = ((routes_hbm, routes), (tokens_hbm, tokens), (student_hbm, student))
    copies_in = [pltpu.make_async_copy(a, b, sems.at[n]) for n, (a, b) in enumerate(pairs)]
    for copy in copies_in:
        copy.start()
    for copy in copies_in:
        copy.wait()
    copies = lax.axis_size("grp")
    experts = lax.axis_size("ep")
    quarter = tokens.shape[1] // (copies * lax.axis_size("rep"))
    place = lax.axis_index("rep") * copies + lax.axis_index("grp")
    start = pl.multiple_of(place * quarter, quarter)
    ids = routes[...]
    chosen = slot_weights(ids, jnp.ones(ids.shape, jnp.float32), experts, 1)
    pieces = quarter // LANES
    stride = padded_pieces(pieces)
    rows[...] = jnp.zeros(rows.shape, jnp.float32)
    for n in range(pieces):
        values = tokens[:, pl.ds(start + n * LANES, LANES)].astype(jnp.float32)
        picked = sum(c * values[t : t + 1, :] for t, c in enumerate(chosen))
        rows[pl.ds(n, 2 * experts, stride=stride), :] = picked
    here = student.shape[0]
    routed = rows[...].astype(jnp.bfloat16).reshape(experts, 2 * stride, LANES)
    for n in range(copies):
        out[n * experts : (n + 1) * experts, here:, :] = routed
    block = student[...]
    out[:, :here, :] = jnp.broadcast_to(block[None], (out.shape[0],) + block.shape)


def dispatch(tokens, routes, student):
    copies, experts = lax.axis_size("grp"), lax.axis_size("ep")
    rows = 2 * padded_pieces(tokens.shape[1] // (copies * lax.axis_size("rep") * LANES))
    shape = (copies * experts, student.shape[0] + rows, LANES)
    return pl.pallas_call(
        dispatch_kernel,
        out_shape=jax.ShapeDtypeStruct(shape, jnp.bfloat16),
        in_specs=[anywhere()] * 3,
        out_specs=vmem(),
        scratch_shapes=[
            pltpu.VMEM((experts * rows, LANES), jnp.float32),
            pltpu.VMEM(tokens.shape, tokens.dtype),
            pltpu.VMEM(routes.shape, routes.dtype),
            pltpu.VMEM(student.shape, student.dtype),
            pltpu.SemaphoreType.DMA((3,)),
        ],
        compiler_params=params(8),
        cost_estimate=cost(2),
        name="dispatch",
    )(tokens, routes, student)


def expert_kernel(
    mine,
    other,
    gain,
    gate_w,
    up_w,
    down_w,
    keep,
    send,
    rows,
    normed,
    result,
):
    half = gain.shape[1] // 2
    groups = lax.axis_size("grp")
    pieces = half // (groups * LANES)
    routed = rows.shape[1]
    stride = padded_pieces(pieces)
    slots = routed // (groups * stride)
    core = lax.axis_index("rep")
    first = pl.multiple_of(core * half, half)
    second = pl.multiple_of((1 - core) * half, half)
    squares = jnp.zeros((slots, LANES), jnp.float32)
    for n, source in enumerate((mine, other)):
        rows[n] = source[...].astype(jnp.float32).reshape(routed, LANES)
        for g in range(groups):
            for m in range(pieces):
                values = rows[n, pl.ds(g * slots * stride + m, slots, stride=stride), :]
                squares += values * values
    factor = lax.rsqrt(jnp.sum(squares, axis=1, keepdims=True) / (2 * half) + 1e-05)
    factor = jnp.broadcast_to(factor, (slots, LANES))
    for n in range(2):
        gains = gain[:, pl.ds((first, second)[n], half)]
        for g in range(groups):
            for m in range(pieces):
                column = (g * pieces + m) * LANES
                columns = slice(column, column + LANES)
                values = rows[n, pl.ds(g * slots * stride + m, slots, stride=stride), :]
                values = values * factor * gains[:, columns]
                normed[n, :, columns] = values.astype(jnp.bfloat16)
    gate_pre = dot(normed[0], gate_w[pl.ds(first, half), :])
    up_pre = dot(normed[0], up_w[pl.ds(first, half), :])
    gate_pre += dot(normed[1], gate_w[pl.ds(second, half), :])
    up_pre += dot(normed[1], up_w[pl.ds(second, half), :])
    hidden = (silu(gate_pre) * up_pre).astype(jnp.bfloat16)
    parts = pieces
    width = half // 2
    result[...] = jnp.zeros(result.shape, jnp.float32)
    for dst, start in ((send, second), (keep, first)):
        for n in range(2):
            columns = pl.ds(pl.multiple_of(start + n * width, width), width)
            out = dot(hidden, down_w[:, columns])
            for m in range(parts):
                place = pl.ds(n * slots * stride + m, slots, stride=stride)
                result[place, :] = out[:, m * LANES : (m + 1) * LANES]
        dst[...] = result[...].astype(dst.dtype)


def experts(mine, other, gain, w_gate, w_up, w_down):
    groups, count = lax.axis_size("grp"), lax.axis_size("ep")
    half = gain.shape[1] // 2
    slots = 2 * count
    result = (groups * slots * padded_pieces(half // (groups * LANES)), LANES)
    return pl.pallas_call(
        expert_kernel,
        out_shape=(
            jax.ShapeDtypeStruct(result, jnp.float32),
            jax.ShapeDtypeStruct(result, jnp.bfloat16),
        ),
        in_specs=[vmem()] * 6,
        out_specs=(vmem(),) * 2,
        scratch_shapes=[
            pltpu.VMEM((2,) + result, jnp.float32),
            pltpu.VMEM((2, slots, half), jnp.bfloat16),
            pltpu.VMEM(result, jnp.float32),
        ],
        compiler_params=params(10),
        cost_estimate=cost(3),
        name="experts",
    )(mine, other, gain, w_gate, w_up, w_down)


def combine_kernel(returned, tokens, routes, gates, keep, received, out, rows, own):
    copies = lax.axis_size("grp")
    experts = lax.axis_size("ep")
    slots = 2 * copies * experts
    stride = returned.shape[0] // slots
    quarter = tokens.shape[1] // (copies * lax.axis_size("rep"))
    pieces = quarter // LANES
    place = lax.axis_index("rep") * copies + lax.axis_index("grp")
    start = pl.multiple_of(place * quarter, quarter)
    count = tokens.shape[0]
    weights = slot_weights(routes[...], gates[...], experts, copies)
    weights = [jnp.broadcast_to(w, (slots, LANES)) for w in weights]
    rows[...] = returned[...].astype(jnp.float32)
    for m in range(pieces):
        values = rows[pl.ds(m, slots, stride=stride), :]
        before = tokens[:, pl.ds(start + m * LANES, LANES)].astype(jnp.float32)
        for t in range(count):
            moe = jnp.sum(values * weights[t], axis=0, keepdims=True)
            own[t * pieces + m : t * pieces + m + 1, :] = before[t : t + 1, :] + moe
    here = keep.shape[1]
    block = own[...].astype(jnp.bfloat16)
    out[:, :here, :] = (keep[...] + received[...].astype(jnp.float32)).astype(jnp.bfloat16)
    out[:, here:, :] = jnp.broadcast_to(block[None], (out.shape[0],) + block.shape)


def combine(returned, tokens, routes, gates, keep, received):
    chips, rows, _ = keep.shape
    own = tokens.size // (lax.axis_size("grp") * lax.axis_size("rep") * LANES)
    return pl.pallas_call(
        combine_kernel,
        out_shape=jax.ShapeDtypeStruct((chips, rows + own, LANES), jnp.bfloat16),
        in_specs=[vmem()] * 6,
        out_specs=vmem(),
        scratch_shapes=[
            pltpu.VMEM(returned.shape, jnp.float32),
            pltpu.VMEM((own, LANES), jnp.float32),
        ],
        compiler_params=params(16),
        cost_estimate=cost(4),
        name="combine",
    )(returned, tokens, routes, gates, keep, received)


def split_kernel(arrived, student, routed):
    rows = student.shape[1]
    routed[...] = arrived[:, rows:, :]
    student[...] = arrived[:, :rows, :]


def split(arrived, rows):
    chips, total, lanes = arrived.shape
    return pl.pallas_call(
        split_kernel,
        out_shape=(
            jax.ShapeDtypeStruct((chips, rows, lanes), arrived.dtype),
            jax.ShapeDtypeStruct((chips, total - rows, lanes), arrived.dtype),
        ),
        in_specs=[vmem()],
        out_specs=(vmem(),) * 2,
        compiler_params=params(4),
        cost_estimate=cost(1),
        name="split",
    )(arrived)


def fetch_kernel(up_hbm, down_hbm, projection, after, up, down, cut, sems):
    half = cut.shape[1]
    start = pl.multiple_of((1 - lax.axis_index("rep")) * half, half)
    pairs = ((up_hbm, up), (down_hbm, down), (projection.at[:, pl.ds(start, half)], cut))
    copies = [pltpu.make_async_copy(a, b, sems.at[n]) for n, (a, b) in enumerate(pairs)]
    for copy in copies:
        copy.start()
    for copy in copies:
        copy.wait()


def fetch(up, down, projection, after):
    rows, width = projection.shape
    return pl.pallas_call(
        fetch_kernel,
        out_shape=(
            pltpu.VMEM(up.shape, up.dtype),
            pltpu.VMEM(down.shape, down.dtype),
            jax.ShapeDtypeStruct((rows, width // 2), projection.dtype),
        ),
        in_specs=[anywhere()] * 4,
        out_specs=(vmem(),) * 3,
        scratch_shapes=[pltpu.SemaphoreType.DMA((3,))],
        compiler_params=params(4),
        cost_estimate=cost(4),
        name="fetch",
    )(up, down, projection, after)


def merge_kernel(keep, received, after, out):
    out[...] = (keep[...] + received[...].astype(jnp.float32)).astype(out.dtype)


def merge(keep, received, after):
    return pl.pallas_call(
        merge_kernel,
        out_shape=jax.ShapeDtypeStruct(received.shape, received.dtype),
        in_specs=[vmem()] * 2 + [anywhere()],
        out_specs=vmem(),
        compiler_params=params(6),
        cost_estimate=cost(1),
        name="merge",
    )(keep, received, after)


def start_interleaved(mine, other, dst, sems):
    core = lax.axis_index("rep")
    copies = [
        pltpu.make_async_copy(mine, dst.at[:, core], sems.at[0]),
        pltpu.make_async_copy(other, dst.at[:, 1 - core], sems.at[1]),
    ]
    for copy in copies:
        copy.start()
    return copies


def forward_kernel(mine, other, gate_hbm, up_hbm, down_hbm, gain, after, keep, *refs):
    send, act_ref, pre_ref, factor_ref, x, raw, scaled, down, sems, sems_x = refs
    core = lax.axis_index("rep")
    chips, cores, rows, tokens = x.shape
    features = chips * cores * rows
    hidden = down.shape[0]
    copies = [
        pltpu.make_async_copy(gate_hbm, raw.at[0], sems.at[0]),
        pltpu.make_async_copy(up_hbm, raw.at[1], sems.at[1]),
        pltpu.make_async_copy(down_hbm, down, sems.at[2]),
    ]
    for copy in copies:
        copy.start()
    copies_x = start_interleaved(mine, other, x, sems_x)
    for n in range(2):
        copies[n].wait()
        part = (raw[n].astype(jnp.float32) * gain[...]).astype(jnp.bfloat16)
        scaled[n * hidden : (n + 1) * hidden, :] = part
    for copy in copies_x:
        copy.wait()
    values = x[...].reshape(features, tokens)
    floats = values.astype(jnp.float32)
    factor = lax.rsqrt(jnp.sum(floats * floats, axis=0, keepdims=True) / features + 1e-05)
    factor_ref[...] = factor
    pre = dot(scaled[...], values) * factor
    pre_ref[...] = pre
    act = (silu(pre[:hidden]) * pre[hidden:]).astype(jnp.bfloat16)
    act_ref[...] = act
    copies[2].wait()
    step = 8
    width = step * 2 * rows
    for n in range(chips // step):
        part = dot(down[:, n * width : (n + 1) * width], act, TN).reshape(step, 2, rows, tokens)
        here = slice(n * step, (n + 1) * step)
        low, high = part[:, 0], part[:, 1]
        keep[here] = jnp.where(core == 0, low, high)
        send[here] = jnp.where(core == 0, high, low).astype(jnp.bfloat16)


def forward(mine, other, gate, up, down, gain, after):
    chips, _, tokens = mine.shape
    hidden, features = down.shape
    rows = features // (2 * chips)
    whole = (chips, 2, rows, tokens)
    return pl.pallas_call(
        forward_kernel,
        out_shape=(
            jax.ShapeDtypeStruct((chips, rows, tokens), jnp.float32),
            jax.ShapeDtypeStruct((chips, rows, tokens), jnp.bfloat16),
            jax.ShapeDtypeStruct((hidden, tokens), jnp.bfloat16),
            jax.ShapeDtypeStruct((2 * hidden, tokens), jnp.float32),
            jax.ShapeDtypeStruct((1, tokens), jnp.float32),
            jax.ShapeDtypeStruct(whole, jnp.bfloat16),
        ),
        in_specs=[anywhere()] * 5 + [vmem(), anywhere()],
        out_specs=(vmem(),) * 6,
        scratch_shapes=[
            pltpu.VMEM((2, hidden, features), jnp.bfloat16),
            pltpu.VMEM((2 * hidden, features), jnp.bfloat16),
            pltpu.VMEM((hidden, features), jnp.bfloat16),
            pltpu.SemaphoreType.DMA((3,)),
            pltpu.SemaphoreType.DMA((2,)),
        ],
        compiler_params=params(28),
        cost_estimate=cost(2),
        name="forward",
    )(mine, other, gate, up, down, gain, after)


def target_kernel(arrived, projection, projection_other, student_in, near, far, rows, tokens):
    here = student_in.shape[0]
    chips, total, lanes = arrived.shape
    count, half = tokens.shape
    groups = lax.axis_size("grp")
    pieces = half // (groups * lanes)
    start = pl.multiple_of(lax.axis_index("rep") * half, half)
    rows[...] = arrived[:, here:, :].astype(jnp.float32).reshape(rows.shape)
    for g in range(groups):
        for m in range(pieces):
            place = pl.ds(g * count * pieces + m, count, stride=pieces)
            columns = slice((g * pieces + m) * lanes, (g * pieces + m + 1) * lanes)
            tokens[:, columns] = rows[place, :].astype(jnp.bfloat16)
    values = tokens[...]
    far[...] = dot(projection_other[...], values, NT)
    branch = jnp.sum(arrived[:, :here, :].astype(jnp.float32), axis=0)
    target = dot(projection[:, pl.ds(start, half)], values, NT)
    near[...] = student_in[...].astype(jnp.float32) + branch - target


def targets(arrived, projection, projection_other, student_in):
    here, count = student_in.shape
    chips, total, lanes = arrived.shape
    half = projection_other.shape[1]
    part = jax.ShapeDtypeStruct((here, count), jnp.float32)
    return pl.pallas_call(
        target_kernel,
        out_shape=(part, part),
        in_specs=[vmem()] * 4,
        out_specs=(vmem(),) * 2,
        scratch_shapes=[
            pltpu.VMEM((chips * (total - here), lanes), jnp.float32),
            pltpu.VMEM((count, half), jnp.bfloat16),
        ],
        compiler_params=params(16),
        cost_estimate=cost(4),
        name="targets",
    )(arrived, projection, projection_other, student_in)


def delta_kernel(near, far, delta):
    tokens = near.shape[1]
    scaled = ((near[...] - far[...]) / math.sqrt(tokens)).astype(jnp.bfloat16)
    delta[...] = jnp.broadcast_to(scaled[None], delta.shape)


def deltas(near, far, chips):
    return pl.pallas_call(
        delta_kernel,
        out_shape=jax.ShapeDtypeStruct((chips,) + near.shape, jnp.bfloat16),
        in_specs=[vmem()] * 2,
        out_specs=vmem(),
        compiler_params=params(4),
        cost_estimate=cost(1),
        name="deltas",
    )(near, far)


def backward_kernel(
    d_mine,
    d_other,
    x,
    down,
    act,
    pre,
    factor,
    gain,
    grad_gate_hbm,
    grad_up_hbm,
    grad_down_hbm,
    mse,
    d,
    grad_gate,
    grad_up,
    grad_down,
    sems_d,
    sems_out,
):
    chips, _, rows, tokens = d.shape
    features = chips * 2 * rows
    copies_d = start_interleaved(d_mine, d_other, d, sems_d)
    for copy in copies_d:
        copy.wait()
    hidden = act.shape[0]
    delta = d[...].reshape(features, tokens)
    back = dot(down[...], delta)
    gate_pre, up_pre = pre[:hidden], pre[hidden:]
    sigmoid = 1.0 / (1.0 + jnp.exp(-gate_pre))
    d_gate = back * up_pre * sigmoid * (1.0 + gate_pre * (1.0 - sigmoid))
    d_up = back * gate_pre * sigmoid
    scale = factor[...]
    d_both = jnp.concatenate([d_gate * scale, d_up * scale], axis=0).astype(jnp.bfloat16)
    step = 8
    width = step * 2 * rows
    acts = act[...]
    copies = []

    def send_out(kind, n, src, dst):
        here = slice(n * width, (n + 1) * width)
        copy = pltpu.make_async_copy(src.at[:, here], dst.at[:, here], sems_out.at[kind, n])
        copy.start()
        copies.append(copy)

    total = jnp.zeros((1, tokens), jnp.float32)
    for n in range(chips // step):
        here = slice(n * width, (n + 1) * width)
        part = d[n * step : (n + 1) * step].reshape(width, tokens)
        grad_down[:, here] = dot(acts, part, NT).astype(jnp.bfloat16)
        send_out(0, n, grad_down, grad_down_hbm)
        floats = part.astype(jnp.float32)
        total += jnp.sum(floats * floats, axis=0, keepdims=True)
    mse[...] = jnp.sum(total, axis=1, keepdims=True) / features
    for n in range(chips // step):
        here = slice(n * width, (n + 1) * width)
        part = x[n * step : (n + 1) * step].reshape(width, tokens)
        grads = dot(d_both, part, NT) * gain[:, here]
        grad_gate[:, here] = grads[:hidden].astype(jnp.bfloat16)
        grad_up[:, here] = grads[hidden:].astype(jnp.bfloat16)
        send_out(1, n, grad_gate, grad_gate_hbm)
        send_out(2, n, grad_up, grad_up_hbm)
    for copy in copies:
        copy.wait()


def backward(d_mine, d_other, x, down, act, pre, factor, gain):
    chips, rows, tokens = d_mine.shape
    hidden, features = down.shape
    grad = jax.ShapeDtypeStruct((hidden, features), jnp.bfloat16)
    whole = pltpu.VMEM((chips, 2, rows, tokens), jnp.bfloat16)
    return pl.pallas_call(
        backward_kernel,
        out_shape=(grad, grad, grad, jax.ShapeDtypeStruct((1, 1), jnp.float32)),
        in_specs=[anywhere()] * 2 + [vmem()] * 6,
        out_specs=(anywhere(),) * 3 + (vmem(),),
        scratch_shapes=[
            whole,
            *[pltpu.VMEM((hidden, features), jnp.bfloat16)] * 3,
            pltpu.SemaphoreType.DMA((2,)),
            pltpu.SemaphoreType.DMA((3, 8)),
        ],
        compiler_params=params(24),
        cost_estimate=cost(8),
        name="backward",
    )(d_mine, d_other, x, down, act, pre, factor, gain)


def local(
    teacher_in,
    teacher_gain,
    routes,
    gates,
    expert_gate,
    expert_up,
    expert_down,
    projection,
    student_in,
    student_gain,
    student_gate,
    student_up,
    student_down,
):
    chips = lax.axis_size(CHIPS)
    projection_t = projection.T
    student_t = student_in.T
    gain_row = student_gain[None, :]

    arrived = exchange(dispatch(teacher_in, routes, student_t))
    x_mine, routed = split(arrived, student_t.shape[0])
    routed_other = other_core(routed)
    x_other = other_core(x_mine)
    up_w, down_w, cut = fetch(expert_up[0], expert_down[0], projection_t, routed)
    projection_other = other_core(cut)
    keep, send = experts(
        routed, routed_other, teacher_gain[None, :], expert_gate[0], up_w, down_w
    )
    outputs = merge(keep, other_core(send), projection_other)
    s_keep, s_send, act, pre, factor, x_all = forward(
        x_mine,
        x_other,
        student_gate.T,
        student_up.T,
        student_down,
        gain_row,
        outputs,
    )
    returned = exchange(outputs)
    joint = combine(returned, teacher_in, routes, gates, s_keep, other_core(s_send))
    near, far = targets(exchange(joint), projection_t, projection_other, student_t)
    d_mine = exchange(deltas(near, other_core(far), chips))
    d_other = other_core(d_mine)
    grad_gate, grad_up, grad_down, mse = backward(
        d_mine, d_other, x_all, student_down, act, pre, factor, gain_row
    )
    return (grad_gate.T, grad_up.T, grad_down, mse.reshape(()))


def solution(mesh):
    everything = ("grp", "ep", "rep")
    placed = (
        P("ep", None),
        P(),
        P("ep", None),
        P("ep", None),
        P("ep", None, ("grp", "rep")),
        P("ep", None, ("grp", "rep")),
        P("ep", ("grp", "rep"), None),
        P(None, everything),
        P(None, everything),
        P(),
        P(None, everything),
        P(None, everything),
        P(everything, None),
    )
    return jax.shard_map(
        local,
        mesh=mesh,
        in_specs=placed,
        out_specs=(P(None, everything), P(None, everything), P(everything, None), P()),
        check_vma=False,
    )
```

time: 178 us -> 141 us (0.79)
  blocking collectives: 50.2 us -> 105 us
  waiting for transfers between devices: 35.9 us -> 5.26 us
  starting transfers between devices: 35.8 us -> 8.58 us
  Pallas kernels: 32.6 us -> 14.4 us
  local copies, waits for them, and re-layouts: 15.6 us -> 5.76 us
  other arithmetic: 6.59 us -> 0 us
    all_to_all x2 -> x4, blocking collectives: 50.2 us -> 105 us  [exchange(): lax.all_to_all(blocks, CHIPS, split_axis=0, concat_axis=0, tiled=True)]
    all_to_all x4 -> x0, waiting for transfers between devices: 32.2 us -> none  [exchange(): lax.all_to_all(blocks, CHIPS, split_axis=0, concat_axis=0, tiled=True)]
    all_to_all x4 -> x0, starting transfers between devices: 26.2 us -> none  [exchange(): lax.all_to_all(blocks, CHIPS, split_axis=0, concat_axis=0, tiled=True)]
    pallas_call x3 -> x8, Pallas kernels: 16.7 us -> 6.41 us  [the longest x1 2.97 us: experts(): pl.pallas_call(expert_kernel, out_shape=(jax.ShapeDtypeStruct(result, jnp...]
    convert_element_type x2 -> x0, other arithmetic: 5.57 us -> none  [the longest x1 2.93 us: local(): (s_keep + other_core(s_send).astype(jnp.float32)).astype(jnp.bfloat16)]
    pallas_call x1, Pallas kernels: 7.72 us -> 3.79 us  [forward(): pl.pallas_call(forward_kernel, out_shape=(jax.ShapeDtypeStruct((chips, ro...]
    pallas_call x1, Pallas kernels: 8.17 us -> 4.24 us  [backward(): pl.pallas_call(backward_kernel, out_shape=(grad, grad, grad, jax.ShapeDty...]
    reshape x5 -> x0, local copies, waits for them, and re-layouts: 2.82 us -> none  [the longest x2 2.11 us: tokens_of(): blocks[:, :data_rows].reshape(groups, experts_in_all, rows_here, quarter)]
  transfers between devices with their start and end apart: 10 -> 7, of which waited for: 5 -> 3; matrix products, arithmetic and copies ran while one was open for 10% -> 0% of each run, Pallas kernels for 12% -> 3%
where the time goes in v2:
time: 141 us; the launch traced here: 140 us
  blocking collectives  105 us (74%)
  Pallas kernels  14.4 us (10%)
  starting transfers between devices  8.58 us (6%)
  local copies, waits for them, and re-layouts  5.76 us (4%)
  waiting for transfers between devices  5.26 us (4%)
    all_to_all x4, blocking collectives, exchange(): lax.all_to_all(blocks, CHIPS, split_axis=0, concat_axis=0, tiled=True)  105 us
    ppermute x7, starting transfers between devices, other_core(): return lax.ppermute(values, 'rep', [(0, 1), (1, 0)])  8.58 us
    unnamed x32, local copies, waits for them, and re-layouts  5.76 us
    ppermute x7, waiting for transfers between devices, other_core(): return lax.ppermute(values, 'rep', [(0, 1), (1, 0)])  5.26 us
    pallas_call x1, Pallas kernels, backward(): pl.pallas_call(backward_kernel, out_shape=(grad, grad, grad, jax.ShapeDty...  4.24 us
    pallas_call x1, Pallas kernels, forward(): pl.pallas_call(forward_kernel, out_shape=(jax.ShapeDtypeStruct((chips, ro...  3.79 us
    pallas_call x1, Pallas kernels, experts(): pl.pallas_call(expert_kernel, out_shape=(jax.ShapeDtypeStruct(result, jnp...  2.97 us
  transfers between devices with their start and end apart: 7, of which 3 were waited for; matrix products, arithmetic and copies ran while one was open for 0% of the time, Pallas kernels for 3%

profile of v2, /device:TPU:1, one launch (start us, length us, event | category | flops | bytes accessed | tf_op | source)
XLA Modules:
  0.0 140.3 jit_solution(4746387263250163377)
XLA Ops:
  0.6 0.0 copy-start.7
  0.6 0.8 copy-done.7
  1.5 0.0 copy-start.10
  1.5 0.7 copy-done.10
  2.2 0.0 copy-start.13
  2.2 0.7 copy-done.13
  2.9 0.6 dispatch.1
  3.4 0.0 copy-start.1
  3.4 0.0 copy-start.2
  3.5 35.0 %all_to_all.26.arrived = bf16[64,96,128]{2,1,0:T(8,128)(2,1)S(1)} all-to-all(bf16[64,96,128]{2,1,0:T(8,128)(2,1)S(1)} %dispatch.1), channel_id=1, replica_groups=mesh['grp'=2,'ep'=32,'rep'=2] {'grp','ep'}, dimensions={0} | all-to-all | bytes 3145728 | tf_op jit(solution)/shard_map/all_to_all | solution.py:43
  38.5 0.1 split.1
  38.6 2.5 %collective-permute-start = (bf16[64,32,128]{2,1,0:T(8,128)(2,1)S(1)}, bf16[64,32,128]{2,1,0:T(8,128)(2,1)S(1)}, u32[]{:S(2)}, u32[]{:S(2)}) collective-permute-start(bf16[64,32,128]{2,1,0:T(8,128)(2,1)S(1)} %get-tuple-element.23.after.mine), channel_id=1, source_target_pairs={{0,1},{1,0},{2,3},{3,2},{4,5},{5,4},{6,7},{7,6},{8,9},{9,8},{10,11... | collective-permute-start | bytes 1572872 | tf_op jit(solution)/shard_map/ppermute | solution.py:47
  41.0 0.1 collective-permute-start.3
  41.1 0.0 copy-done.1
  41.1 0.0 copy-done.2
  41.1 0.0 copy-start.3
  41.1 2.0 %copy-done.3 = bf16[1,256,7168]{2,1,0:T(8,128)(2,1)S(1)} copy-done((bf16[1,256,7168]{2,1,0:T(8,128)(2,1)S(1)}, bf16[1,256,7168]{2,1,0:T(8,128)(2,1)}, u32[]{:S(2)}) %copy-start.3) | copy-done | bytes 3670040
  43.2 0.0 copy-start.4
  43.2 0.0 copy-start.12
  43.2 0.6 fetch.1
  43.8 0.0 collective-permute-done.other
  43.8 1.4 %copy-done.4 = bf16[1,7168,256]{2,1,0:T(8,128)(2,1)S(1)} copy-done((bf16[1,7168,256]{2,1,0:T(8,128)(2,1)S(1)}, bf16[1,7168,256]{2,1,0:T(8,128)(2,1)}, u32[]{:S(2)}) %copy-start.4) | copy-done | bytes 3670040
  45.2 0.0 copy-done.12
  45.2 0.0 copy-start.5
  45.2 0.0 copy-start.6
  45.2 3.0 %experts.1 = (f32[2048,128]{1,0:T(8,128)S(1)}, bf16[2048,128]{1,0:T(8,128)(2,1)S(1)}) custom-call(bf16[64,32,128]{2,1,0:T(8,128)(2,1)S(1)} %get-tuple-element.23.after.mine, bf16[64,32,128]{2,1,0:T(8,128)(2,1)S(1)} %collective-permute-done.other, f32[1,7168]{1,0:T(1,128)S(1)} %bitcast.27, bf16[7168,256]{1,0:T(8,128)(2,1)S(1)} %bitcast.19, ...), custom_call_target="tpu_custom_call" | custom-call | bytes 9000000 | tf_op jit(solution)/shard_map/experts/pallas_call | solution.py:183
  48.2 0.0 copy-start
  48.2 0.0 copy-start.9
  48.2 0.5 collective-permute-start.1
  48.7 0.1 collective-permute-start.2
  48.8 2.1 %collective-permute-done.2.after.projection_other = bf16[64,3584]{1,0:T(8,128)(2,1)S(1)} collective-permute-done((bf16[64,3584]{1,0:T(8,128)(2,1)S(1)}, bf16[64,3584]{1,0:T(8,128)(2,1)S(1)}, u32[]{:S(2)}, u32[]{:S(2)}) %collective-permute-start.2) | collective-permute-done | bytes 458784 | tf_op jit(solution)/shard_map/ppermute | solution.py:47
  50.9 0.0 collective-permute-done.1.received
  50.9 0.1 merge.1.after
  51.0 0.0 collective-permute-done.3.other
  51.0 0.0 copy-done.5
  51.0 0.0 copy-done.6
  51.1 0.0 copy-done
  51.1 0.0 copy-done.9
  51.1 0.0 copy-start.8
  51.1 0.0 copy-start.14
  51.1 0.0 copy-start.15
  51.1 3.8 %forward.1 = (f32[64,64,128]{2,1,0:T(8,128)S(1)}, bf16[64,64,128]{2,1,0:T(8,128)(2,1)S(1)}, bf16[112,128]{1,0:T(8,128)(2,1)S(1)}, f32[224,128]{1,0:T(8,128)S(1)}...) custom-call(bf16[64,64,128]{2,1,0:T(8,128)(2,1)S(1)} %get-tuple-element.29.mine, ...), custom_call_target="tpu_custom_call" | custom-call | bytes 6000000 | tf_op jit(solution)/shard_map/forward/pallas_call | solution.py:367
  54.9 0.5 collective-permute-start.4
  55.4 17.0 %all_to_all.27 = bf16[64,32,128]{2,1,0:T(8,128)(2,1)S(1)} all-to-all(bf16[64,32,128]{2,1,0:T(8,128)(2,1)S(1)} %bitcast.14), channel_id=1, replica_groups=mesh['grp'=2,'ep'=32,'rep'=2] {'grp','ep'}, dimensions={0} | all-to-all | bytes 1048576 | tf_op jit(solution)/shard_map/all_to_all | solution.py:43
  72.4 0.0 collective-permute-done.4.received
  72.4 0.0 copy-done.8
  72.4 0.0 copy-done.14
  72.4 0.0 copy-done.15
  72.4 1.1 combine.1
  73.5 0.0 copy-start.11
  73.5 30.5 %all_to_all.28.arrived = bf16[64,120,128]{2,1,0:T(8,128)(2,1)S(1)} all-to-all(bf16[64,120,128]{2,1,0:T(8,128)(2,1)S(1)} %combine.1), channel_id=1, replica_groups=mesh['grp'=2,'ep'=32,'rep'=2] {'grp','ep'}, dimensions={0} | all-to-all | bytes 3932160 | tf_op jit(solution)/shard_map/all_to_all | solution.py:43
  104.1 0.0 copy-done.11
  104.1 0.9 targets.1
  105.0 3.2 %collective-permute-start.5 = (f32[64,128]{1,0:T(8,128)S(1)}, f32[64,128]{1,0:T(8,128)S(1)}, u32[]{:S(2)}, u32[]{:S(2)}) collective-permute-start(f32[64,128]{1,0:T(8,128)S(1)} %get-tuple-element.33), channel_id=1, source_target_pairs={{0,1},{1,0},{2,3},{3,2},{4,5},{5,4},{6,7},{7,6},{8,9},{9,8},{10,11... | collective-permute-start | bytes 98312 | tf_op jit(solution)/shard_map/ppermute | solution.py:47
  108.2 0.9 collective-permute-done.5.far
  109.0 0.1 deltas.1
  109.1 22.6 %all_to_all.29.d_mine = bf16[64,64,128]{2,1,0:T(8,128)(2,1)S(1)} all-to-all(bf16[64,64,128]{2,1,0:T(8,128)(2,1)S(1)} %deltas.1), channel_id=1, replica_groups=mesh['grp'=2,'ep'=32,'rep'=2] {'grp','ep'}, dimensions={0} | all-to-all | bytes 2097152 | tf_op jit(solution)/shard_map/all_to_all | solution.py:43
  131.7 1.8 %collective-permute-start.6 = (bf16[64,64,128]{2,1,0:T(8,128)(2,1)S(1)}, bf16[64,64,128]{2,1,0:T(8,128)(2,1)S(1)}, u32[]{:S(2)}, u32[]{:S(2)}) collective-permute-start(bf16[64,64,128]{2,1,0:T(8,128)(2,1)S(1)} %all_to_all.29.d_mine), channel_id=1, source_target_pairs={{0,1},{1,0},{2,3},{3,2},{4,5},{5,4},{6,7},{7,6},{8,9},{9,8},{10,11... | collective-permute-start | bytes 3145736 | tf_op jit(solution)/shard_map/ppermute | solution.py:47
  133.6 2.3 %collective-permute-done.6.d_other = bf16[64,64,128]{2,1,0:T(8,128)(2,1)S(1)} collective-permute-done((bf16[64,64,128]{2,1,0:T(8,128)(2,1)S(1)}, bf16[64,64,128]{2,1,0:T(8,128)(2,1)S(1)}, u32[]{:S(2)}, u32[]{:S(2)}) %collective-permute-start.6) | collective-permute-done | bytes 1048608 | tf_op jit(solution)/shard_map/ppermute | solution.py:47
  135.9 4.2 %backward.1 = (bf16[112,8192]{1,0:T(8,128)(2,1)}, bf16[112,8192]{1,0:T(8,128)(2,1)}, bf16[112,8192]{1,0:T(8,128)(2,1)}, f32[1,1]{1,0:T(1,128)}) custom-call(bf16[64,64,128]{2,1,0:T(8,128)(2,1)S(1)} %all_to_all.29.d_mine, bf16[64,64,128]{2,1,0:T(8,128)(2,1)S(1)} %collective-permute-done.6.d_other, bf16[64,2,64,128]{3,2,1,0:T(8,128)(2,1)S(1)} %get-tuple-element.34.x, ...), custom_call_target="tpu_custom_call" | custom-call | bytes 24000000 | tf_op jit(solution)/shard_map/backward/pallas_call | solution.py:521
Async XLA Ops:
  0.6 0.8 copy-start.7
  1.5 0.7 copy-start.10
  2.2 0.7 copy-start.13
  3.4 37.7 %copy-start.1 = (bf16[7168,64]{0,1:T(8,128)(2,1)S(1)}, bf16[7168,64]{0,1:T(8,128)(2,1)}, u32[]{:S(2)}) copy-start(bf16[7168,64]{0,1:T(8,128)(2,1)} %param.20) | copy-start | bytes 2752516
  3.4 37.7 %copy-start.2 = (bf16[1,7168,256]{2,1,0:T(8,128)(2,1)S(1)}, bf16[1,7168,256]{2,1,0:T(8,128)(2,1)}, u32[]{:S(2)}) copy-start(bf16[1,7168,256]{2,1,0:T(8,128)(2,1)} %param.18) | copy-start | bytes 11010052
  38.6 5.2 %collective-permute-start = (bf16[64,32,128]{2,1,0:T(8,128)(2,1)S(1)}, bf16[64,32,128]{2,1,0:T(8,128)(2,1)S(1)}, u32[]{:S(2)}, u32[]{:S(2)}) collective-permute-start(bf16[64,32,128]{2,1,0:T(8,128)(2,1)S(1)} %get-tuple-element.23.after.mine), channel_id=1, source_target_pairs={{0,1},{1,0},{2,3},{3,2},{4,5},{5,4},{6,7},{7,6},{8,9},{9,8},{10,11... | collective-permute-start | bytes 1572872 | tf_op jit(solution)/shard_map/ppermute | solution.py:47
  41.0 10.0 %collective-permute-start.3 = (bf16[64,64,128]{2,1,0:T(8,128)(2,1)S(1)}, bf16[64,64,128]{2,1,0:T(8,128)(2,1)S(1)}, u32[]{:S(2)}, u32[]{:S(2)}) collective-permute-start(bf16[64,64,128]{2,1,0:T(8,128)(2,1)S(1)} %get-tuple-element.29.mine), channel_id=1, source_target_pairs={{0,1},{1,0},{2,3},{3,2},{4,5},{5,4},{6,7},{7,6},{8,9},{9,8},{10,11... | collective-permute-start | bytes 3145736 | tf_op jit(solution)/shard_map/ppermute | solution.py:47
  41.1 2.0 %copy-start.3 = (bf16[1,256,7168]{2,1,0:T(8,128)(2,1)S(1)}, bf16[1,256,7168]{2,1,0:T(8,128)(2,1)}, u32[]{:S(2)}) copy-start(bf16[1,256,7168]{2,1,0:T(8,128)(2,1)} %param.19) | copy-start | bytes 11010052
  43.2 2.0 %copy-start.4 = (bf16[1,7168,256]{2,1,0:T(8,128)(2,1)S(1)}, bf16[1,7168,256]{2,1,0:T(8,128)(2,1)}, u32[]{:S(2)}) copy-start(bf16[1,7168,256]{2,1,0:T(8,128)(2,1)} %param.17) | copy-start | bytes 11010052
  43.2 2.0 %copy-start.12 = (f32[7168]{0:T(1024)S(1)}, f32[7168]{0:T(1024)}, u32[]{:S(2)}) copy-start(f32[7168]{0:T(1024)} %param.14) | copy-start | bytes 86020
  45.2 5.8 %copy-start.5 = (bf16[8192,112]{0,1:T(8,128)(2,1)S(1)}, bf16[8192,112]{0,1:T(8,128)(2,1)}, u32[]{:S(2)}) copy-start(bf16[8192,112]{0,1:T(8,128)(2,1)} %param.23) | copy-start | bytes 5505028
  45.2 5.8 %copy-start.6 = (bf16[8192,112]{0,1:T(8,128)(2,1)S(1)}, bf16[8192,112]{0,1:T(8,128)(2,1)}, u32[]{:S(2)}) copy-start(bf16[8192,112]{0,1:T(8,128)(2,1)} %param.24) | copy-start | bytes 5505028
  48.2 2.8 %copy-start = (bf16[112,8192]{1,0:T(8,128)(2,1)S(1)}, bf16[112,8192]{1,0:T(8,128)(2,1)}, u32[]{:S(2)}) copy-start(bf16[112,8192]{1,0:T(8,128)(2,1)} %down.1) | copy-start | bytes 5505028
  48.2 2.8 %copy-start.9 = (f32[8192]{0:T(1024)S(1)}, f32[8192]{0:T(1024)}, u32[]{:S(2)}) copy-start(f32[8192]{0:T(1024)} %param.22) | copy-start | bytes 98308
  48.2 2.7 %collective-permute-start.1 = (bf16[2048,128]{1,0:T(8,128)(2,1)S(1)}, bf16[2048,128]{1,0:T(8,128)(2,1)S(1)}, u32[]{:S(2)}, u32[]{:S(2)}) collective-permute-start(bf16[2048,128]{1,0:T(8,128)(2,1)S(1)} %get-tuple-element.27), channel_id=1, source_target_pairs={{0,1},{1,0},{2,3},{3,2},{4,5},{5,4},{6,7},{7,6},{8,9},{9,8},{10,11... | collective-permute-start | bytes 1572872 | tf_op jit(solution)/shard_map/ppermute | solution.py:47
  48.7 2.2 %collective-permute-start.2 = (bf16[64,3584]{1,0:T(8,128)(2,1)S(1)}, bf16[64,3584]{1,0:T(8,128)(2,1)S(1)}, u32[]{:S(2)}, u32[]{:S(2)}) collective-permute-start(bf16[64,3584]{1,0:T(8,128)(2,1)S(1)} %get-tuple-element.28), channel_id=1, source_target_pairs={{0,1},{1,0},{2,3},{3,2},{4,5},{5,4},{6,7},{7,6},{8,9},{9,8},{10,11... | collective-permute-start | bytes 1376264 | tf_op jit(solution)/shard_map/ppermute | solution.py:47
  51.1 21.3 %copy-start.8 = (bf16[4,7168]{1,0:T(4,128)(2,1)S(1)}, bf16[4,7168]{1,0:T(4,128)(2,1)}, u32[]{:S(2)}) copy-start(bf16[4,7168]{1,0:T(4,128)(2,1)} %tokens.1) | copy-start | bytes 172036
  51.1 21.3 %copy-start.14 = (s32[4,8]{1,0:T(4,128)S(1)}, s32[4,8]{1,0:T(4,128)}, u32[]{:S(2)}) copy-start(s32[4,8]{1,0:T(4,128)} %routes.1) | copy-start | bytes 388
  51.1 21.3 %copy-start.15 = (f32[4,8]{1,0:T(4,128)S(1)}, f32[4,8]{1,0:T(4,128)}, u32[]{:S(2)}) copy-start(f32[4,8]{1,0:T(4,128)} %gates.1) | copy-start | bytes 388
  54.9 17.5 %collective-permute-start.4 = (bf16[64,64,128]{2,1,0:T(8,128)(2,1)S(1)}, bf16[64,64,128]{2,1,0:T(8,128)(2,1)S(1)}, u32[]{:S(2)}, u32[]{:S(2)}) collective-permute-start(bf16[64,64,128]{2,1,0:T(8,128)(2,1)S(1)} %get-tuple-element.31), channel_id=1, source_target_pairs={{0,1},{1,0},{2,3},{3,2},{4,5},{5,4},{6,7},{7,6},{8,9},{9,8},{10,11... | collective-permute-start | bytes 3145736 | tf_op jit(solution)/shard_map/ppermute | solution.py:47
  73.5 30.6 %copy-start.11 = (bf16[128,64]{0,1:T(8,128)(2,1)S(1)}, bf16[128,64]{0,1:T(8,128)(2,1)}, u32[]{:S(2)}) copy-start(bf16[128,64]{0,1:T(8,128)(2,1)} %param.21) | copy-start | bytes 49156
  105.0 4.0 %collective-permute-start.5 = (f32[64,128]{1,0:T(8,128)S(1)}, f32[64,128]{1,0:T(8,128)S(1)}, u32[]{:S(2)}, u32[]{:S(2)}) collective-permute-start(f32[64,128]{1,0:T(8,128)S(1)} %get-tuple-element.33), channel_id=1, source_target_pairs={{0,1},{1,0},{2,3},{3,2},{4,5},{5,4},{6,7},{7,6},{8,9},{9,8},{10,11... | collective-permute-start | bytes 98312 | tf_op jit(solution)/shard_map/ppermute | solution.py:47
  131.7 4.1 %collective-permute-start.6 = (bf16[64,64,128]{2,1,0:T(8,128)(2,1)S(1)}, bf16[64,64,128]{2,1,0:T(8,128)(2,1)S(1)}, u32[]{:S(2)}, u32[]{:S(2)}) collective-permute-start(bf16[64,64,128]{2,1,0:T(8,128)(2,1)S(1)} %all_to_all.29.d_mine), channel_id=1, source_target_pairs={{0,1},{1,0},{2,3},{3,2},{4,5},{5,4},{6,7},{7,6},{8,9},{9,8},{10,11... | collective-permute-start | bytes 3145736 | tf_op jit(solution)/shard_map/ppermute | solution.py:47

commit v3 on v2

--- a/solution.py
+++ b/solution.py
@@ -27,8 +27,8 @@
 
 
 def cost(microseconds):
-    size = int(microseconds * 3e6)
-    return pl.CostEstimate(flops=0, bytes_accessed=size, transcendentals=0)
+    flops = int(microseconds * 1e9)
+    return pl.CostEstimate(flops=flops, bytes_accessed=0, transcendentals=0)
 
 
 def vmem():
@@ -37,6 +37,10 @@
 
 def anywhere():
     return pl.BlockSpec(memory_space=pl.ANY)
+
+
+def in_hbm():
+    return pl.BlockSpec(memory_space=pltpu.HBM)
 
 
 def exchange(blocks):
@@ -102,7 +106,7 @@
     return pl.pallas_call(
         dispatch_kernel,
         out_shape=jax.ShapeDtypeStruct(shape, jnp.bfloat16),
-        in_specs=[anywhere()] * 3,
+        in_specs=[in_hbm()] * 3,
         out_specs=vmem(),
         scratch_shapes=[
             pltpu.VMEM((experts * rows, LANES), jnp.float32),
@@ -112,91 +116,120 @@
             pltpu.SemaphoreType.DMA((3,)),
         ],
         compiler_params=params(8),
+        cost_estimate=cost(30),
+        name="dispatch",
+    )(*[pltpu.with_memory_space_constraint(a, pltpu.HBM) for a in (tokens, routes, student)])
+
+
+def scaled_tokens(source, gains, rows, scaled):
+    routed = rows.shape[0]
+    groups = lax.axis_size("grp")
+    slots, half = scaled.shape
+    pieces = half // (groups * LANES)
+    stride = padded_pieces(pieces)
+    rows[...] = source.astype(jnp.float32).reshape(routed, LANES)
+    squares = jnp.zeros((slots, LANES), jnp.float32)
+    for g in range(groups):
+        for m in range(pieces):
+            column = (g * pieces + m) * LANES
+            columns = slice(column, column + LANES)
+            values = rows[pl.ds(g * slots * stride + m, slots, stride=stride), :]
+            squares += values * values
+            scaled[:, columns] = (values * gains[:, columns]).astype(jnp.bfloat16)
+    return squares
+
+
+def first_half_kernel(
+    routed, gain, gate_w, up_w, projection, pre, squares, cut, rows, scaled, sem
+):
+    half = scaled.shape[1]
+    core = lax.axis_index("rep")
+    start = pl.multiple_of(core * half, half)
+    cut_start = pl.multiple_of((1 - core) * half, half)
+    copy = pltpu.make_async_copy(projection.at[:, pl.ds(cut_start, half)], cut, sem)
+    copy.start()
+    gains = gain[:, pl.ds(start, half)]
+    squares[...] = scaled_tokens(routed[...], gains, rows, scaled)
+    values = scaled[...]
+    pre[0] = dot(values, gate_w[pl.ds(start, half), :])
+    pre[1] = dot(values, up_w[pl.ds(start, half), :])
+    copy.wait()
+
+
+def first_half(routed, gain, gate, up, projection):
+    slots = 2 * lax.axis_size("ep")
+    half = gain.shape[1] // 2
+    return pl.pallas_call(
+        first_half_kernel,
+        out_shape=(
+            jax.ShapeDtypeStruct((2, slots, gate.shape[1]), jnp.float32),
+            jax.ShapeDtypeStruct((slots, LANES), jnp.float32),
+            jax.ShapeDtypeStruct((projection.shape[0], half), projection.dtype),
+        ),
+        in_specs=[vmem()] * 4 + [in_hbm()],
+        out_specs=(vmem(),) * 3,
+        scratch_shapes=[
+            pltpu.VMEM((routed.shape[0] * routed.shape[1], LANES), jnp.float32),
+            pltpu.VMEM((slots, half), jnp.bfloat16),
+            pltpu.SemaphoreType.DMA,
+        ],
+        compiler_params=params(8),
         cost_estimate=cost(2),
-        name="dispatch",
-    )(tokens, routes, student)
+        name="first_half",
+    )(routed, gain, gate, up, pltpu.with_memory_space_constraint(projection, pltpu.HBM))
 
 
 def expert_kernel(
-    mine,
-    other,
-    gain,
-    gate_w,
-    up_w,
-    down_w,
-    keep,
-    send,
-    rows,
-    normed,
-    result,
+    other, pre, squares, gain, gate_w, up_w, down_w, keep, send, token, rows, scaled, result
 ):
-    half = gain.shape[1] // 2
-    groups = lax.axis_size("grp")
-    pieces = half // (groups * LANES)
-    routed = rows.shape[1]
+    slots, half = scaled.shape
+    pieces = half // (lax.axis_size("grp") * LANES)
     stride = padded_pieces(pieces)
-    slots = routed // (groups * stride)
     core = lax.axis_index("rep")
     first = pl.multiple_of(core * half, half)
     second = pl.multiple_of((1 - core) * half, half)
-    squares = jnp.zeros((slots, LANES), jnp.float32)
-    for n, source in enumerate((mine, other)):
-        rows[n] = source[...].astype(jnp.float32).reshape(routed, LANES)
-        for g in range(groups):
-            for m in range(pieces):
-                values = rows[n, pl.ds(g * slots * stride + m, slots, stride=stride), :]
-                squares += values * values
-    factor = lax.rsqrt(jnp.sum(squares, axis=1, keepdims=True) / (2 * half) + 1e-05)
-    factor = jnp.broadcast_to(factor, (slots, LANES))
-    for n in range(2):
-        gains = gain[:, pl.ds((first, second)[n], half)]
-        for g in range(groups):
-            for m in range(pieces):
-                column = (g * pieces + m) * LANES
-                columns = slice(column, column + LANES)
-                values = rows[n, pl.ds(g * slots * stride + m, slots, stride=stride), :]
-                values = values * factor * gains[:, columns]
-                normed[n, :, columns] = values.astype(jnp.bfloat16)
-    gate_pre = dot(normed[0], gate_w[pl.ds(first, half), :])
-    up_pre = dot(normed[0], up_w[pl.ds(first, half), :])
-    gate_pre += dot(normed[1], gate_w[pl.ds(second, half), :])
-    up_pre += dot(normed[1], up_w[pl.ds(second, half), :])
+    total = squares[...]
+    total += scaled_tokens(other[...], gain[:, pl.ds(second, half)], rows, scaled)
+    factor = lax.rsqrt(jnp.sum(total, axis=1, keepdims=True) / (2 * half) + 1e-05)
+    token[...] = jnp.zeros(token.shape, token.dtype)
+    values = scaled[...]
+    gate_pre = (pre[0] + dot(values, gate_w[pl.ds(second, half), :])) * factor
+    up_pre = (pre[1] + dot(values, up_w[pl.ds(second, half), :])) * factor
     hidden = (silu(gate_pre) * up_pre).astype(jnp.bfloat16)
-    parts = pieces
     width = half // 2
     result[...] = jnp.zeros(result.shape, jnp.float32)
     for dst, start in ((send, second), (keep, first)):
         for n in range(2):
             columns = pl.ds(pl.multiple_of(start + n * width, width), width)
             out = dot(hidden, down_w[:, columns])
-            for m in range(parts):
+            for m in range(pieces):
                 place = pl.ds(n * slots * stride + m, slots, stride=stride)
                 result[place, :] = out[:, m * LANES : (m + 1) * LANES]
         dst[...] = result[...].astype(dst.dtype)
 
 
-def experts(mine, other, gain, w_gate, w_up, w_down):
-    groups, count = lax.axis_size("grp"), lax.axis_size("ep")
+def experts(other, pre, squares, gain, w_gate, w_up, w_down):
+    groups, slots = lax.axis_size("grp"), squares.shape[0]
     half = gain.shape[1] // 2
-    slots = 2 * count
     result = (groups * slots * padded_pieces(half // (groups * LANES)), LANES)
     return pl.pallas_call(
         expert_kernel,
         out_shape=(
             jax.ShapeDtypeStruct(result, jnp.float32),
             jax.ShapeDtypeStruct(result, jnp.bfloat16),
+            jax.ShapeDtypeStruct((8, LANES), jnp.float32),
         ),
-        in_specs=[vmem()] * 6,
-        out_specs=(vmem(),) * 2,
+        in_specs=[vmem()] * 7,
+        out_specs=(vmem(),) * 3,
         scratch_shapes=[
-            pltpu.VMEM((2,) + result, jnp.float32),
-            pltpu.VMEM((2, slots, half), jnp.bfloat16),
+            pltpu.VMEM(result, jnp.float32),
+            pltpu.VMEM((slots, half), jnp.bfloat16),
             pltpu.VMEM(result, jnp.float32),
         ],
-        compiler_params=params(10),
+        compiler_params=params(8),
         cost_estimate=cost(3),
         name="experts",
-    )(mine, other, gain, w_gate, w_up, w_down)
+    )(other, pre, squares, gain, w_gate, w_up, w_down)
 
 
 def combine_kernel(returned, tokens, routes, gates, keep, received, out, rows, own):
@@ -242,55 +275,40 @@
     )(returned, tokens, routes, gates, keep, received)
 
 
-def split_kernel(arrived, student, routed):
-    rows = student.shape[1]
-    routed[...] = arrived[:, rows:, :]
-    student[...] = arrived[:, :rows, :]
-
-
-def split(arrived, rows):
+def split_kernel(arrived, *refs):
+    routed = refs[-1]
+    routed[...] = arrived[:, arrived.shape[1] - routed.shape[1] :, :]
+
+
+def split(arrived, rows, weights):
     chips, total, lanes = arrived.shape
     return pl.pallas_call(
         split_kernel,
-        out_shape=(
-            jax.ShapeDtypeStruct((chips, rows, lanes), arrived.dtype),
-            jax.ShapeDtypeStruct((chips, total - rows, lanes), arrived.dtype),
-        ),
-        in_specs=[vmem()],
-        out_specs=(vmem(),) * 2,
+        out_shape=jax.ShapeDtypeStruct((chips, total - rows, lanes), arrived.dtype),
+        in_specs=[vmem()] * (1 + len(weights)),
+        out_specs=vmem(),
         compiler_params=params(4),
         cost_estimate=cost(1),
         name="split",
-    )(arrived)
-
-
-def fetch_kernel(up_hbm, down_hbm, projection, after, up, down, cut, sems):
-    half = cut.shape[1]
-    start = pl.multiple_of((1 - lax.axis_index("rep")) * half, half)
-    pairs = ((up_hbm, up), (down_hbm, down), (projection.at[:, pl.ds(start, half)], cut))
-    copies = [pltpu.make_async_copy(a, b, sems.at[n]) for n, (a, b) in enumerate(pairs)]
-    for copy in copies:
-        copy.start()
-    for copy in copies:
-        copy.wait()
-
-
-def fetch(up, down, projection, after):
-    rows, width = projection.shape
-    return pl.pallas_call(
-        fetch_kernel,
-        out_shape=(
-            pltpu.VMEM(up.shape, up.dtype),
-            pltpu.VMEM(down.shape, down.dtype),
-            jax.ShapeDtypeStruct((rows, width // 2), projection.dtype),
-        ),
-        in_specs=[anywhere()] * 4,
-        out_specs=(vmem(),) * 3,
-        scratch_shapes=[pltpu.SemaphoreType.DMA((3,))],
+    )(arrived, *weights)
+
+
+def split_student_kernel(arrived, other, squares, student):
+    del other, squares
+    student[...] = arrived[:, : student.shape[1], :]
+
+
+def split_student(arrived, rows, *after):
+    chips, _, lanes = arrived.shape
+    return pl.pallas_call(
+        split_student_kernel,
+        out_shape=jax.ShapeDtypeStruct((chips, rows, lanes), arrived.dtype),
+        in_specs=[vmem()] + [anywhere()] * 2,
+        out_specs=vmem(),
         compiler_params=params(4),
-        cost_estimate=cost(4),
-        name="fetch",
-    )(up, down, projection, after)
+        cost_estimate=cost(1),
+        name="split_student",
+    )(arrived, *after)
 
 
 def merge_kernel(keep, received, after, out):
@@ -320,25 +338,17 @@
     return copies
 
 
-def forward_kernel(mine, other, gate_hbm, up_hbm, down_hbm, gain, after, keep, *refs):
-    send, act_ref, pre_ref, factor_ref, x, raw, scaled, down, sems, sems_x = refs
+def forward_kernel(mine, other, gate, up, down, gain, after, keep, *refs):
+    send, act_ref, pre_ref, factor_ref, x, scaled, sems = refs
     core = lax.axis_index("rep")
     chips, cores, rows, tokens = x.shape
     features = chips * cores * rows
     hidden = down.shape[0]
-    copies = [
-        pltpu.make_async_copy(gate_hbm, raw.at[0], sems.at[0]),
-        pltpu.make_async_copy(up_hbm, raw.at[1], sems.at[1]),
-        pltpu.make_async_copy(down_hbm, down, sems.at[2]),
-    ]
+    copies = start_interleaved(mine, other, x, sems)
+    for n, weights in enumerate((gate, up)):
+        part = (weights[...].astype(jnp.float32) * gain[...]).astype(jnp.bfloat16)
+        scaled[n * hidden : (n + 1) * hidden, :] = part
     for copy in copies:
-        copy.start()
-    copies_x = start_interleaved(mine, other, x, sems_x)
-    for n in range(2):
-        copies[n].wait()
-        part = (raw[n].astype(jnp.float32) * gain[...]).astype(jnp.bfloat16)
-        scaled[n * hidden : (n + 1) * hidden, :] = part
-    for copy in copies_x:
         copy.wait()
     values = x[...].reshape(features, tokens)
     floats = values.astype(jnp.float32)
@@ -348,7 +358,6 @@
     pre_ref[...] = pre
     act = (silu(pre[:hidden]) * pre[hidden:]).astype(jnp.bfloat16)
     act_ref[...] = act
-    copies[2].wait()
     step = 8
     width = step * 2 * rows
     for n in range(chips // step):
@@ -374,17 +383,14 @@
             jax.ShapeDtypeStruct((1, tokens), jnp.float32),
             jax.ShapeDtypeStruct(whole, jnp.bfloat16),
         ),
-        in_specs=[anywhere()] * 5 + [vmem(), anywhere()],
+        in_specs=[anywhere()] * 2 + [vmem()] * 4 + [anywhere()],
         out_specs=(vmem(),) * 6,
         scratch_shapes=[
-            pltpu.VMEM((2, hidden, features), jnp.bfloat16),
             pltpu.VMEM((2 * hidden, features), jnp.bfloat16),
-            pltpu.VMEM((hidden, features), jnp.bfloat16),
-            pltpu.SemaphoreType.DMA((3,)),
             pltpu.SemaphoreType.DMA((2,)),
         ],
-        compiler_params=params(28),
-        cost_estimate=cost(2),
+        compiler_params=params(20),
+        cost_estimate=cost(8),
         name="forward",
     )(mine, other, gate, up, down, gain, after)
 
@@ -473,14 +479,6 @@
     for copy in copies_d:
         copy.wait()
     hidden = act.shape[0]
-    delta = d[...].reshape(features, tokens)
-    back = dot(down[...], delta)
-    gate_pre, up_pre = pre[:hidden], pre[hidden:]
-    sigmoid = 1.0 / (1.0 + jnp.exp(-gate_pre))
-    d_gate = back * up_pre * sigmoid * (1.0 + gate_pre * (1.0 - sigmoid))
-    d_up = back * gate_pre * sigmoid
-    scale = factor[...]
-    d_both = jnp.concatenate([d_gate * scale, d_up * scale], axis=0).astype(jnp.bfloat16)
     step = 8
     width = step * 2 * rows
     acts = act[...]
@@ -501,6 +499,14 @@
         floats = part.astype(jnp.float32)
         total += jnp.sum(floats * floats, axis=0, keepdims=True)
     mse[...] = jnp.sum(total, axis=1, keepdims=True) / features
+    delta = d[...].reshape(features, tokens)
+    back = dot(down[...], delta)
+    gate_pre, up_pre = pre[:hidden], pre[hidden:]
+    sigmoid = 1.0 / (1.0 + jnp.exp(-gate_pre))
+    d_gate = back * up_pre * sigmoid * (1.0 + gate_pre * (1.0 - sigmoid))
+    d_up = back * gate_pre * sigmoid
+    scale = factor[...]
+    d_both = jnp.concatenate([d_gate * scale, d_up * scale], axis=0).astype(jnp.bfloat16)
     for n in range(chips // step):
         here = slice(n * width, (n + 1) * width)
         part = x[n * step : (n + 1) * step].reshape(width, tokens)
@@ -556,24 +562,21 @@
     gain_row = student_gain[None, :]
 
     arrived = exchange(dispatch(teacher_in, routes, student_t))
-    x_mine, routed = split(arrived, student_t.shape[0])
+    expert_weights = (expert_gate[0], expert_up[0], expert_down[0])
+    student_weights = (student_gate.T, student_up.T, student_down)
+    here = student_t.shape[0]
+    routed = split(arrived, here, expert_weights + student_weights)
     routed_other = other_core(routed)
+    teacher_row = teacher_gain[None, :]
+    first_pre, squares, cut = first_half(routed, teacher_row, *expert_weights[:2], projection_t)
+    x_mine = split_student(arrived, here, routed_other, squares)
     x_other = other_core(x_mine)
-    up_w, down_w, cut = fetch(expert_up[0], expert_down[0], projection_t, routed)
     projection_other = other_core(cut)
-    keep, send = experts(
-        routed, routed_other, teacher_gain[None, :], expert_gate[0], up_w, down_w
+    keep, send, token = experts(routed_other, first_pre, squares, teacher_row, *expert_weights)
+    s_keep, s_send, act, pre, factor, x_all = forward(
+        x_mine, x_other, *student_weights, gain_row, token
     )
     outputs = merge(keep, other_core(send), projection_other)
-    s_keep, s_send, act, pre, factor, x_all = forward(
-        x_mine,
-        x_other,
-        student_gate.T,
-        student_up.T,
-        student_down,
-        gain_row,
-        outputs,
-    )
     returned = exchange(outputs)
     joint = combine(returned, teacher_in, routes, gates, s_keep, other_core(s_send))
     near, far = targets(exchange(joint), projection_t, projection_other, student_t)

time: 141 us -> 134 us (0.950)
  local copies, waits for them, and re-layouts: 5.76 us -> 0.07 us
  waiting for transfers between devices: 5.26 us -> 3.16 us
    unnamed x32 -> x26, local copies, waits for them, and re-layouts: 5.76 us -> 0.07 us
    ppermute x7, waiting for transfers between devices: 5.26 us -> 3.16 us  [other_core(): return lax.ppermute(values, 'rep', [(0, 1), (1, 0)])]
  transfers between devices with their start and end apart: 7 -> 7, of which waited for: 3 -> 2; matrix products, arithmetic and copies ran while one was open for 0% -> 0% of each run, Pallas kernels for 3% -> 5%
where the time goes in v3:
time: 134 us
  blocking collectives  105 us (78%)
  Pallas kernels  15.2 us (11%)
  starting transfers between devices  8.97 us (7%)
  waiting for transfers between devices  3.16 us (2%)
    all_to_all x4, blocking collectives, exchange(): lax.all_to_all(blocks, CHIPS, split_axis=0, concat_axis=0, tiled=True)  105 us
    ppermute x7, starting transfers between devices, other_core(): return lax.ppermute(values, 'rep', [(0, 1), (1, 0)])  8.97 us
    pallas_call x1, Pallas kernels, backward(): pl.pallas_call(backward_kernel, out_shape=(grad, grad, grad, jax.ShapeDty...  4.34 us
    pallas_call x1, Pallas kernels, forward(): pl.pallas_call(forward_kernel, out_shape=(jax.ShapeDtypeStruct((chips, ro...  3.42 us
    ppermute x7, waiting for transfers between devices, other_core(): return lax.ppermute(values, 'rep', [(0, 1), (1, 0)])  3.16 us
  transfers between devices with their start and end apart: 7, of which 2 were waited for; matrix products, arithmetic and copies ran while one was open for 0% of the time, Pallas kernels for 5%

profile of v3, /device:TPU:1, one launch (start us, length us, event | category | flops | bytes accessed | tf_op | source)
XLA Modules:
  0.0 133.7 jit_solution(7396394438807289829)
XLA Ops:
  0.6 0.0 copy-start
  0.6 0.0 copy-start.1
  0.7 0.0 copy-start.2
  0.7 0.0 copy-start.4
  0.7 0.0 copy-start.5
  0.7 1.5 %dispatch.1 = bf16[64,96,128]{2,1,0:T(8,128)(2,1)S(1)} custom-call(bf16[4,7168]{1,0:T(4,128)(2,1)} %tokens.1, s32[4,8]{1,0:T(4,128)} %routes.1, bf16[64,128]{1,0:T(8,128)(2,1)} %bitcast.34), custom_call_target="tpu_custom_call" | custom-call | flops 30000001024 | tf_op jit(solution)/shard_map/dispatch/pallas_call | solution.py:106
  2.2 0.0 copy-start.3
  2.2 35.0 %all_to_all.26.arrived = bf16[64,96,128]{2,1,0:T(8,128)(2,1)S(1)} all-to-all(bf16[64,96,128]{2,1,0:T(8,128)(2,1)S(1)} %dispatch.1), channel_id=1, replica_groups=mesh['grp'=2,'ep'=32,'rep'=2] {'grp','ep'}, dimensions={0} | all-to-all | bytes 3145728 | tf_op jit(solution)/shard_map/all_to_all | solution.py:47
  37.2 0.0 copy-done
  37.2 0.0 copy-done.1
  37.2 0.0 copy-done.2
  37.2 0.0 copy-done.4
  37.2 0.0 copy-done.5
  37.3 0.0 copy-done.3
  37.3 0.0 copy-start.7
  37.3 2.5 %collective-permute-start = (bf16[64,32,128]{2,1,0:T(8,128)(2,1)S(1)}, bf16[64,32,128]{2,1,0:T(8,128)(2,1)S(1)}, u32[]{:S(2)}, u32[]{:S(2)}) collective-permute-start(bf16[64,32,128]{2,1,0:T(8,128)(2,1)S(1)} %split.1.routed), channel_id=1, source_target_pairs={{0,1},{1,0},{2,3},{3,2},{4,5},{5,4},{6,7},{7,6},{8,9},{9,8},{10,11... | collective-permute-start | bytes 1572872 | tf_op jit(solution)/shard_map/ppermute | solution.py:51
  39.8 0.0 copy-done.7
  39.8 1.7 %first_half.1 = (f32[2,64,256]{2,1,0:T(8,128)S(1)}, f32[64,128]{1,0:T(8,128)S(1)}, bf16[64,3584]{1,0:T(8,128)(2,1)S(1)}) custom-call(bf16[64,32,128]{2,1,0:T(8,128)(2,1)S(1)} %split.1.routed, f32[1,7168]{1,0:T(1,128)S(1)} %bitcast.30, bf16[7168,256]{1,0:T(8,128)(2,1)S(1)} %bitcast.15, bf16[7168,256]{1,0:T(8,128)(2,1)S(1)} %bitcast.18, bf16[64,7168]{1,0:T(8,128)(2,1)} %bitcast.26), custom_call_target="tpu_custom_call" | custom-call | flops 2000000000 | tf_op jit(solution)/shard_map/first_half/pallas_call | solution.py:162
  41.5 0.0 collective-permute-done.other
  41.5 0.1 split_student.1.mine
  41.6 0.7 collective-permute-start.3
  42.3 0.1 collective-permute-start.2
  42.4 0.0 copy-start.9
  42.4 1.9 %experts.1 = (f32[2048,128]{1,0:T(8,128)S(1)}, bf16[2048,128]{1,0:T(8,128)(2,1)S(1)}, f32[8,128]{1,0:T(8,128)S(1)}) custom-call(bf16[64,32,128]{2,1,0:T(8,128)(2,1)S(1)} %collective-permute-done.other, f32[2,64,256]{2,1,0:T(8,128)S(1)} %get-tuple-element.22.pre, f32[64,128]{1,0:T(8,128)S(1)} %get-tuple-element.23.squares, f32[1,7168]{1,0:T(1,128)S(1)} %bitcast.31, ...), custom_call_target="tpu_custom_call" | custom-call | flops 3000000000 | tf_op jit(solution)/shard_map/experts/pallas_call | solution.py:215
  44.3 0.5 collective-permute-start.1
  44.8 0.0 collective-permute-done.3.other
  44.8 0.0 copy-done.9
  44.8 3.4 %forward.1 = (f32[64,64,128]{2,1,0:T(8,128)S(1)}, bf16[64,64,128]{2,1,0:T(8,128)(2,1)S(1)}, bf16[112,128]{1,0:T(8,128)(2,1)S(1)}, f32[224,128]{1,0:T(8,128)S(1)}...) custom-call(bf16[64,64,128]{2,1,0:T(8,128)(2,1)S(1)} %split_student.1.mine, ...), custom_call_target="tpu_custom_call" | custom-call | flops 8000000000 | tf_op jit(solution)/shard_map/forward/pallas_call | solution.py:376
  48.2 0.2 collective-permute-start.4
  48.4 0.0 collective-permute-done.2.after.projection_other
  48.5 0.0 collective-permute-done.1.received
  48.5 0.0 copy-start.8
  48.5 0.0 copy-start.11
  48.5 0.0 copy-start.12
  48.5 0.1 merge.1
  48.6 16.8 %all_to_all.27 = bf16[64,32,128]{2,1,0:T(8,128)(2,1)S(1)} all-to-all(bf16[64,32,128]{2,1,0:T(8,128)(2,1)S(1)} %bitcast.29), channel_id=1, replica_groups=mesh['grp'=2,'ep'=32,'rep'=2] {'grp','ep'}, dimensions={0} | all-to-all | bytes 1048576 | tf_op jit(solution)/shard_map/all_to_all | solution.py:47
  65.4 0.0 collective-permute-done.4.received
  65.4 0.0 copy-done.8
  65.5 0.0 copy-done.11
  65.5 0.0 copy-done.12
  65.5 1.1 combine.1
  66.6 0.0 copy-start.6
  66.6 0.0 copy-start.10
  66.6 30.9 %all_to_all.28.arrived = bf16[64,120,128]{2,1,0:T(8,128)(2,1)S(1)} all-to-all(bf16[64,120,128]{2,1,0:T(8,128)(2,1)S(1)} %combine.1), channel_id=1, replica_groups=mesh['grp'=2,'ep'=32,'rep'=2] {'grp','ep'}, dimensions={0} | all-to-all | bytes 3932160 | tf_op jit(solution)/shard_map/all_to_all | solution.py:47
  97.5 0.0 copy-done.6
  97.5 0.0 copy-done.10
  97.5 0.9 targets.1
  98.4 3.2 %collective-permute-start.5 = (f32[64,128]{1,0:T(8,128)S(1)}, f32[64,128]{1,0:T(8,128)S(1)}, u32[]{:S(2)}, u32[]{:S(2)}) collective-permute-start(f32[64,128]{1,0:T(8,128)S(1)} %get-tuple-element.31), channel_id=1, source_target_pairs={{0,1},{1,0},{2,3},{3,2},{4,5},{5,4},{6,7},{7,6},{8,9},{9,8},{10,11... | collective-permute-start | bytes 98312 | tf_op jit(solution)/shard_map/ppermute | solution.py:51
  101.6 0.9 collective-permute-done.5.far
  102.4 0.1 deltas.1
  102.6 22.6 %all_to_all.29.d_mine = bf16[64,64,128]{2,1,0:T(8,128)(2,1)S(1)} all-to-all(bf16[64,64,128]{2,1,0:T(8,128)(2,1)S(1)} %deltas.1), channel_id=1, replica_groups=mesh['grp'=2,'ep'=32,'rep'=2] {'grp','ep'}, dimensions={0} | all-to-all | bytes 2097152 | tf_op jit(solution)/shard_map/all_to_all | solution.py:47
  125.1 1.8 %collective-permute-start.6 = (bf16[64,64,128]{2,1,0:T(8,128)(2,1)S(1)}, bf16[64,64,128]{2,1,0:T(8,128)(2,1)S(1)}, u32[]{:S(2)}, u32[]{:S(2)}) collective-permute-start(bf16[64,64,128]{2,1,0:T(8,128)(2,1)S(1)} %all_to_all.29.d_mine), channel_id=1, source_target_pairs={{0,1},{1,0},{2,3},{3,2},{4,5},{5,4},{6,7},{7,6},{8,9},{9,8},{10,11... | collective-permute-start | bytes 3145736 | tf_op jit(solution)/shard_map/ppermute | solution.py:51
  127.0 2.3 %collective-permute-done.6.d_other = bf16[64,64,128]{2,1,0:T(8,128)(2,1)S(1)} collective-permute-done((bf16[64,64,128]{2,1,0:T(8,128)(2,1)S(1)}, bf16[64,64,128]{2,1,0:T(8,128)(2,1)S(1)}, u32[]{:S(2)}, u32[]{:S(2)}) %collective-permute-start.6) | collective-permute-done | bytes 1048608 | tf_op jit(solution)/shard_map/ppermute | solution.py:51
  129.2 4.3 %backward.1 = (bf16[112,8192]{1,0:T(8,128)(2,1)}, bf16[112,8192]{1,0:T(8,128)(2,1)}, bf16[112,8192]{1,0:T(8,128)(2,1)}, f32[1,1]{1,0:T(1,128)}) custom-call(bf16[64,64,128]{2,1,0:T(8,128)(2,1)S(1)} %all_to_all.29.d_mine, bf16[64,64,128]{2,1,0:T(8,128)(2,1)S(1)} %collective-permute-done.6.d_other, bf16[64,2,64,128]{3,2,1,0:T(8,128)(2,1)S(1)} %get-tuple-element.32.x, ...), custom_call_target="tpu_custom_call" | custom-call | flops 8000000000 | tf_op jit(solution)/shard_map/backward/pallas_call | solution.py:527
  (1 shorter events, 0.0 us)
Async XLA Ops:
  0.6 36.6 %copy-start = (bf16[1,7168,256]{2,1,0:T(8,128)(2,1)S(1)}, bf16[1,7168,256]{2,1,0:T(8,128)(2,1)}, u32[]{:S(2)}) copy-start(bf16[1,7168,256]{2,1,0:T(8,128)(2,1)} %param.17) | copy-start | bytes 11010052
  0.6 36.6 %copy-start.1 = (bf16[1,7168,256]{2,1,0:T(8,128)(2,1)S(1)}, bf16[1,7168,256]{2,1,0:T(8,128)(2,1)}, u32[]{:S(2)}) copy-start(bf16[1,7168,256]{2,1,0:T(8,128)(2,1)} %param.18) | copy-start | bytes 11010052
  0.7 36.6 %copy-start.2 = (bf16[1,256,7168]{2,1,0:T(8,128)(2,1)S(1)}, bf16[1,256,7168]{2,1,0:T(8,128)(2,1)}, u32[]{:S(2)}) copy-start(bf16[1,256,7168]{2,1,0:T(8,128)(2,1)} %param.19) | copy-start | bytes 11010052
  0.7 36.6 %copy-start.4 = (bf16[8192,112]{0,1:T(8,128)(2,1)S(1)}, bf16[8192,112]{0,1:T(8,128)(2,1)}, u32[]{:S(2)}) copy-start(bf16[8192,112]{0,1:T(8,128)(2,1)} %param.24) | copy-start | bytes 5505028
  0.7 36.6 %copy-start.5 = (bf16[112,8192]{1,0:T(8,128)(2,1)S(1)}, bf16[112,8192]{1,0:T(8,128)(2,1)}, u32[]{:S(2)}) copy-start(bf16[112,8192]{1,0:T(8,128)(2,1)} %down.3) | copy-start | bytes 5505028
  2.2 35.1 %copy-start.3 = (bf16[8192,112]{0,1:T(8,128)(2,1)S(1)}, bf16[8192,112]{0,1:T(8,128)(2,1)}, u32[]{:S(2)}) copy-start(bf16[8192,112]{0,1:T(8,128)(2,1)} %param.23) | copy-start | bytes 5505028
  37.3 2.5 %copy-start.7 = (f32[7168]{0:T(1024)S(1)}, f32[7168]{0:T(1024)}, u32[]{:S(2)}) copy-start(f32[7168]{0:T(1024)} %param.14) | copy-start | bytes 86020
  37.3 4.2 %collective-permute-start = (bf16[64,32,128]{2,1,0:T(8,128)(2,1)S(1)}, bf16[64,32,128]{2,1,0:T(8,128)(2,1)S(1)}, u32[]{:S(2)}, u32[]{:S(2)}) collective-permute-start(bf16[64,32,128]{2,1,0:T(8,128)(2,1)S(1)} %split.1.routed), channel_id=1, source_target_pairs={{0,1},{1,0},{2,3},{3,2},{4,5},{5,4},{6,7},{7,6},{8,9},{9,8},{10,11... | collective-permute-start | bytes 1572872 | tf_op jit(solution)/shard_map/ppermute | solution.py:51
  41.6 3.2 %collective-permute-start.3 = (bf16[64,64,128]{2,1,0:T(8,128)(2,1)S(1)}, bf16[64,64,128]{2,1,0:T(8,128)(2,1)S(1)}, u32[]{:S(2)}, u32[]{:S(2)}) collective-permute-start(bf16[64,64,128]{2,1,0:T(8,128)(2,1)S(1)} %split_student.1.mine), channel_id=1, source_target_pairs={{0,1},{1,0},{2,3},{3,2},{4,5},{5,4},{6,7},{7,6},{8,9},{9,8},{10,11... | collective-permute-start | bytes 3145736 | tf_op jit(solution)/shard_map/ppermute | solution.py:51
  42.3 6.2 %collective-permute-start.2 = (bf16[64,3584]{1,0:T(8,128)(2,1)S(1)}, bf16[64,3584]{1,0:T(8,128)(2,1)S(1)}, u32[]{:S(2)}, u32[]{:S(2)}) collective-permute-start(bf16[64,3584]{1,0:T(8,128)(2,1)S(1)} %get-tuple-element.26), channel_id=1, source_target_pairs={{0,1},{1,0},{2,3},{3,2},{4,5},{5,4},{6,7},{7,6},{8,9},{9,8},{10,11... | collective-permute-start | bytes 1376264 | tf_op jit(solution)/shard_map/ppermute | solution.py:51
  42.4 2.4 %copy-start.9 = (f32[8192]{0:T(1024)S(1)}, f32[8192]{0:T(1024)}, u32[]{:S(2)}) copy-start(f32[8192]{0:T(1024)} %param.22) | copy-start | bytes 98308
  44.3 4.2 %collective-permute-start.1 = (bf16[2048,128]{1,0:T(8,128)(2,1)S(1)}, bf16[2048,128]{1,0:T(8,128)(2,1)S(1)}, u32[]{:S(2)}, u32[]{:S(2)}) collective-permute-start(bf16[2048,128]{1,0:T(8,128)(2,1)S(1)} %get-tuple-element.25), channel_id=1, source_target_pairs={{0,1},{1,0},{2,3},{3,2},{4,5},{5,4},{6,7},{7,6},{8,9},{9,8},{10,11... | collective-permute-start | bytes 1572872 | tf_op jit(solution)/shard_map/ppermute | solution.py:51
  48.2 17.2 %collective-permute-start.4 = (bf16[64,64,128]{2,1,0:T(8,128)(2,1)S(1)}, bf16[64,64,128]{2,1,0:T(8,128)(2,1)S(1)}, u32[]{:S(2)}, u32[]{:S(2)}) collective-permute-start(bf16[64,64,128]{2,1,0:T(8,128)(2,1)S(1)} %get-tuple-element.29), channel_id=1, source_target_pairs={{0,1},{1,0},{2,3},{3,2},{4,5},{5,4},{6,7},{7,6},{8,9},{9,8},{10,11... | collective-permute-start | bytes 3145736 | tf_op jit(solution)/shard_map/ppermute | solution.py:51
  48.5 17.0 %copy-start.8 = (bf16[4,7168]{1,0:T(4,128)(2,1)S(1)}, bf16[4,7168]{1,0:T(4,128)(2,1)}, u32[]{:S(2)}) copy-start(bf16[4,7168]{1,0:T(4,128)(2,1)} %tokens.1) | copy-start | bytes 172036
  48.5 17.0 %copy-start.11 = (s32[4,8]{1,0:T(4,128)S(1)}, s32[4,8]{1,0:T(4,128)}, u32[]{:S(2)}) copy-start(s32[4,8]{1,0:T(4,128)} %routes.1) | copy-start | bytes 388
  48.5 17.0 %copy-start.12 = (f32[4,8]{1,0:T(4,128)S(1)}, f32[4,8]{1,0:T(4,128)}, u32[]{:S(2)}) copy-start(f32[4,8]{1,0:T(4,128)} %gates.1) | copy-start | bytes 388
  66.6 30.9 %copy-start.6 = (bf16[7168,64]{0,1:T(8,128)(2,1)S(1)}, bf16[7168,64]{0,1:T(8,128)(2,1)}, u32[]{:S(2)}) copy-start(bf16[7168,64]{0,1:T(8,128)(2,1)} %param.20) | copy-start | bytes 2752516
  66.6 30.9 %copy-start.10 = (bf16[128,64]{0,1:T(8,128)(2,1)S(1)}, bf16[128,64]{0,1:T(8,128)(2,1)}, u32[]{:S(2)}) copy-start(bf16[128,64]{0,1:T(8,128)(2,1)} %param.21) | copy-start | bytes 49156
  98.4 4.0 %collective-permute-start.5 = (f32[64,128]{1,0:T(8,128)S(1)}, f32[64,128]{1,0:T(8,128)S(1)}, u32[]{:S(2)}, u32[]{:S(2)}) collective-permute-start(f32[64,128]{1,0:T(8,128)S(1)} %get-tuple-element.31), channel_id=1, source_target_pairs={{0,1},{1,0},{2,3},{3,2},{4,5},{5,4},{6,7},{7,6},{8,9},{9,8},{10,11... | collective-permute-start | bytes 98312 | tf_op jit(solution)/shard_map/ppermute | solution.py:51
  125.1 4.1 %collective-permute-start.6 = (bf16[64,64,128]{2,1,0:T(8,128)(2,1)S(1)}, bf16[64,64,128]{2,1,0:T(8,128)(2,1)S(1)}, u32[]{:S(2)}, u32[]{:S(2)}) collective-permute-start(bf16[64,64,128]{2,1,0:T(8,128)(2,1)S(1)} %all_to_all.29.d_mine), channel_id=1, source_target_pairs={{0,1},{1,0},{2,3},{3,2},{4,5},{5,4},{6,7},{7,6},{8,9},{9,8},{10,11... | collective-permute-start | bytes 3145736 | tf_op jit(solution)/shard_map/ppermute | solution.py:51

commit v4 on v3

--- a/solution.py
+++ b/solution.py
@@ -70,8 +70,27 @@
     return -(-pieces // 8) * 8
 
 
-def dispatch_kernel(tokens_hbm, routes_hbm, student_hbm, out, rows, tokens, routes, student, sems):
-    pairs = ((routes_hbm, routes), (tokens_hbm, tokens), (student_hbm, student))
+def dispatch_kernel(
+    tokens_hbm,
+    routes_hbm,
+    student_hbm,
+    gain_hbm,
+    out,
+    rows,
+    tokens,
+    routes,
+    student,
+    gain,
+    sems,
+):
+    chip = lax.axis_index("grp") * lax.axis_size("ep") + lax.axis_index("ep")
+    mine = pl.ds(pl.multiple_of(chip * LANES, LANES), LANES)
+    pairs = (
+        (routes_hbm, routes),
+        (tokens_hbm, tokens),
+        (student_hbm, student),
+        (gain_hbm.at[:, mine], gain),
+    )
     copies_in = [pltpu.make_async_copy(a, b, sems.at[n]) for n, (a, b) in enumerate(pairs)]
     for copy in copies_in:
         copy.start()
@@ -92,33 +111,47 @@
         picked = sum(c * values[t : t + 1, :] for t, c in enumerate(chosen))
         rows[pl.ds(n, 2 * experts, stride=stride), :] = picked
     here = student.shape[0]
+    values = student[...].astype(jnp.float32)
+    squares = jnp.sum(values * values, axis=0, keepdims=True)
+    high = squares.astype(jnp.bfloat16).astype(jnp.float32)
+    for n, part in enumerate((high, squares - high)):
+        place = pl.ds(pieces + n, 2 * experts, stride=stride)
+        rows[place, :] = jnp.broadcast_to(part, (2 * experts, LANES))
     routed = rows[...].astype(jnp.bfloat16).reshape(experts, 2 * stride, LANES)
     for n in range(copies):
         out[n * experts : (n + 1) * experts, here:, :] = routed
-    block = student[...]
+    columns = jnp.broadcast_to(gain[...], (LANES, LANES)).T
+    columns = jnp.where(lax.axis_index("rep") == 0, columns[:here], columns[here:])
+    block = (values * columns).astype(jnp.bfloat16)
     out[:, :here, :] = jnp.broadcast_to(block[None], (out.shape[0],) + block.shape)
 
 
-def dispatch(tokens, routes, student):
+def dispatch(tokens, routes, student, gain):
     copies, experts = lax.axis_size("grp"), lax.axis_size("ep")
     rows = 2 * padded_pieces(tokens.shape[1] // (copies * lax.axis_size("rep") * LANES))
     shape = (copies * experts, student.shape[0] + rows, LANES)
     return pl.pallas_call(
         dispatch_kernel,
         out_shape=jax.ShapeDtypeStruct(shape, jnp.bfloat16),
-        in_specs=[in_hbm()] * 3,
+        in_specs=[in_hbm()] * 4,
         out_specs=vmem(),
         scratch_shapes=[
             pltpu.VMEM((experts * rows, LANES), jnp.float32),
             pltpu.VMEM(tokens.shape, tokens.dtype),
             pltpu.VMEM(routes.shape, routes.dtype),
             pltpu.VMEM(student.shape, student.dtype),
-            pltpu.SemaphoreType.DMA((3,)),
+            pltpu.VMEM((1, LANES), gain.dtype),
+            pltpu.SemaphoreType.DMA((4,)),
         ],
         compiler_params=params(8),
         cost_estimate=cost(30),
         name="dispatch",
-    )(*[pltpu.with_memory_space_constraint(a, pltpu.HBM) for a in (tokens, routes, student)])
+    )(
+        *[
+            pltpu.with_memory_space_constraint(a, pltpu.HBM)
+            for a in (tokens, routes, student, gain)
+        ]
+    )
 
 
 def scaled_tokens(source, gains, rows, scaled):
@@ -338,24 +371,26 @@
     return copies
 
 
-def forward_kernel(mine, other, gate, up, down, gain, after, keep, *refs):
-    send, act_ref, pre_ref, factor_ref, x, scaled, sems = refs
+def forward_kernel(mine, other, routed, routed_other, gate, up, down, after, keep, *refs):
+    send, act_ref, pre_ref, factor_ref, x, sems = refs
     core = lax.axis_index("rep")
     chips, cores, rows, tokens = x.shape
     features = chips * cores * rows
     hidden = down.shape[0]
     copies = start_interleaved(mine, other, x, sems)
-    for n, weights in enumerate((gate, up)):
-        part = (weights[...].astype(jnp.float32) * gain[...]).astype(jnp.bfloat16)
-        scaled[n * hidden : (n + 1) * hidden, :] = part
+    stride = routed.shape[1] // 2
+    sums = jnp.zeros((1, tokens), jnp.float32)
+    for part in (routed, routed_other):
+        rows_of = part[:, stride - 2 : stride, :].astype(jnp.float32)
+        sums += jnp.sum(jnp.sum(rows_of, axis=0), axis=0, keepdims=True)
+    factor = lax.rsqrt(sums / features + 1e-05)
+    factor_ref[...] = factor
     for copy in copies:
         copy.wait()
     values = x[...].reshape(features, tokens)
-    floats = values.astype(jnp.float32)
-    factor = lax.rsqrt(jnp.sum(floats * floats, axis=0, keepdims=True) / features + 1e-05)
-    factor_ref[...] = factor
-    pre = dot(scaled[...], values) * factor
-    pre_ref[...] = pre
+    pre_ref[:hidden, :] = dot(gate[...], values) * factor
+    pre_ref[hidden:, :] = dot(up[...], values) * factor
+    pre = pre_ref[...]
     act = (silu(pre[:hidden]) * pre[hidden:]).astype(jnp.bfloat16)
     act_ref[...] = act
     step = 8
@@ -368,7 +403,7 @@
         send[here] = jnp.where(core == 0, high, low).astype(jnp.bfloat16)
 
 
-def forward(mine, other, gate, up, down, gain, after):
+def forward(mine, other, routed, routed_other, gate, up, down, after):
     chips, _, tokens = mine.shape
     hidden, features = down.shape
     rows = features // (2 * chips)
@@ -383,16 +418,13 @@
             jax.ShapeDtypeStruct((1, tokens), jnp.float32),
             jax.ShapeDtypeStruct(whole, jnp.bfloat16),
         ),
-        in_specs=[anywhere()] * 2 + [vmem()] * 4 + [anywhere()],
+        in_specs=[anywhere()] * 2 + [vmem()] * 5 + [anywhere()],
         out_specs=(vmem(),) * 6,
-        scratch_shapes=[
-            pltpu.VMEM((2 * hidden, features), jnp.bfloat16),
-            pltpu.SemaphoreType.DMA((2,)),
-        ],
+        scratch_shapes=[pltpu.SemaphoreType.DMA((2,))],
         compiler_params=params(20),
         cost_estimate=cost(8),
         name="forward",
-    )(mine, other, gate, up, down, gain, after)
+    )(mine, other, routed, routed_other, gate, up, down, after)
 
 
 def target_kernel(arrived, projection, projection_other, student_in, near, far, rows, tokens):
@@ -461,7 +493,6 @@
     act,
     pre,
     factor,
-    gain,
     grad_gate_hbm,
     grad_up_hbm,
     grad_down_hbm,
@@ -479,6 +510,14 @@
     for copy in copies_d:
         copy.wait()
     hidden = act.shape[0]
+    delta = d[...].reshape(features, tokens)
+    back = dot(down[...], delta)
+    gate_pre, up_pre = pre[:hidden], pre[hidden:]
+    sigmoid = 1.0 / (1.0 + jnp.exp(-gate_pre))
+    d_gate = back * up_pre * sigmoid * (1.0 + gate_pre * (1.0 - sigmoid))
+    d_up = back * gate_pre * sigmoid
+    scale = factor[...]
+    d_both = jnp.concatenate([d_gate * scale, d_up * scale], axis=0).astype(jnp.bfloat16)
     step = 8
     width = step * 2 * rows
     acts = act[...]
@@ -499,18 +538,10 @@
         floats = part.astype(jnp.float32)
         total += jnp.sum(floats * floats, axis=0, keepdims=True)
     mse[...] = jnp.sum(total, axis=1, keepdims=True) / features
-    delta = d[...].reshape(features, tokens)
-    back = dot(down[...], delta)
-    gate_pre, up_pre = pre[:hidden], pre[hidden:]
-    sigmoid = 1.0 / (1.0 + jnp.exp(-gate_pre))
-    d_gate = back * up_pre * sigmoid * (1.0 + gate_pre * (1.0 - sigmoid))
-    d_up = back * gate_pre * sigmoid
-    scale = factor[...]
-    d_both = jnp.concatenate([d_gate * scale, d_up * scale], axis=0).astype(jnp.bfloat16)
     for n in range(chips // step):
         here = slice(n * width, (n + 1) * width)
         part = x[n * step : (n + 1) * step].reshape(width, tokens)
-        grads = dot(d_both, part, NT) * gain[:, here]
+        grads = dot(d_both, part, NT)
         grad_gate[:, here] = grads[:hidden].astype(jnp.bfloat16)
         grad_up[:, here] = grads[hidden:].astype(jnp.bfloat16)
         send_out(1, n, grad_gate, grad_gate_hbm)
@@ -519,7 +550,7 @@
         copy.wait()
 
 
-def backward(d_mine, d_other, x, down, act, pre, factor, gain):
+def backward(d_mine, d_other, x, down, act, pre, factor):
     chips, rows, tokens = d_mine.shape
     hidden, features = down.shape
     grad = jax.ShapeDtypeStruct((hidden, features), jnp.bfloat16)
@@ -527,7 +558,7 @@
     return pl.pallas_call(
         backward_kernel,
         out_shape=(grad, grad, grad, jax.ShapeDtypeStruct((1, 1), jnp.float32)),
-        in_specs=[anywhere()] * 2 + [vmem()] * 6,
+        in_specs=[anywhere()] * 2 + [vmem()] * 5,
         out_specs=(anywhere(),) * 3 + (vmem(),),
         scratch_shapes=[
             whole,
@@ -538,7 +569,7 @@
         compiler_params=params(24),
         cost_estimate=cost(8),
         name="backward",
-    )(d_mine, d_other, x, down, act, pre, factor, gain)
+    )(d_mine, d_other, x, down, act, pre, factor)
 
 
 def local(
@@ -559,22 +590,21 @@
     chips = lax.axis_size(CHIPS)
     projection_t = projection.T
     student_t = student_in.T
-    gain_row = student_gain[None, :]
-
-    arrived = exchange(dispatch(teacher_in, routes, student_t))
+
+    arrived = exchange(dispatch(teacher_in, routes, student_t, student_gain[None, :]))
     expert_weights = (expert_gate[0], expert_up[0], expert_down[0])
     student_weights = (student_gate.T, student_up.T, student_down)
     here = student_t.shape[0]
-    routed = split(arrived, here, expert_weights + student_weights)
+    teacher_row = teacher_gain[None, :]
+    routed = split(arrived, here, expert_weights + student_weights + (teacher_row,))
     routed_other = other_core(routed)
-    teacher_row = teacher_gain[None, :]
     first_pre, squares, cut = first_half(routed, teacher_row, *expert_weights[:2], projection_t)
     x_mine = split_student(arrived, here, routed_other, squares)
     x_other = other_core(x_mine)
     projection_other = other_core(cut)
     keep, send, token = experts(routed_other, first_pre, squares, teacher_row, *expert_weights)
     s_keep, s_send, act, pre, factor, x_all = forward(
-        x_mine, x_other, *student_weights, gain_row, token
+        x_mine, x_other, routed, routed_other, *student_weights, token
     )
     outputs = merge(keep, other_core(send), projection_other)
     returned = exchange(outputs)
@@ -583,7 +613,7 @@
     d_mine = exchange(deltas(near, other_core(far), chips))
     d_other = other_core(d_mine)
     grad_gate, grad_up, grad_down, mse = backward(
-        d_mine, d_other, x_all, student_down, act, pre, factor, gain_row
+        d_mine, d_other, x_all, student_down, act, pre, factor
     )
     return (grad_gate.T, grad_up.T, grad_down, mse.reshape(()))
 

time: 134 us -> 133 us (level)
  no operation moved by 1% of the time
where the time goes in v4:
time: 133 us; the launch traced here: 132 us
  blocking collectives  105 us (79%)
  Pallas kernels  14.2 us (11%)
  starting transfers between devices  8.66 us (7%)
  waiting for transfers between devices  3.18 us (2%)
    all_to_all x4, blocking collectives, exchange(): lax.all_to_all(blocks, CHIPS, split_axis=0, concat_axis=0, tiled=True)  105 us
    ppermute x7, starting transfers between devices, other_core(): return lax.ppermute(values, 'rep', [(0, 1), (1, 0)])  8.66 us
    pallas_call x1, Pallas kernels, backward(): pl.pallas_call(backward_kernel, out_shape=(grad, grad, grad, jax.ShapeDty...  4.28 us
    ppermute x7, waiting for transfers between devices, other_core(): return lax.ppermute(values, 'rep', [(0, 1), (1, 0)])  3.18 us
  transfers between devices with their start and end apart: 7, of which 2 were waited for; matrix products, arithmetic and copies ran while one was open for 0% of the time, Pallas kernels for 5%

profile of v4, /device:TPU:1, one launch (start us, length us, event | category | flops | bytes accessed | tf_op | source)
XLA Modules:
  0.0 132.4 jit_solution(10678886957110624183)
XLA Ops:
  0.6 0.0 copy-start
  0.6 0.0 copy-start.1
  0.7 0.0 copy-start.2
  0.7 0.0 copy-start.4
  0.7 0.0 copy-start.5
  0.7 1.5 %dispatch.1 = bf16[64,96,128]{2,1,0:T(8,128)(2,1)S(1)} custom-call(bf16[4,7168]{1,0:T(4,128)(2,1)} %tokens.1, s32[4,8]{1,0:T(4,128)} %routes.1, bf16[64,128]{1,0:T(8,128)(2,1)} %bitcast.33, f32[1,8192]{1,0:T(1,128)} %bitcast.35), custom_call_target="tpu_custom_call" | custom-call | flops 30000001024 | tf_op jit(solution)/shard_map/dispatch/pallas_call | solution.py:133
  2.2 0.0 copy-start.3
  2.2 0.0 copy-start.7
  2.2 35.0 %all_to_all.26.arrived = bf16[64,96,128]{2,1,0:T(8,128)(2,1)S(1)} all-to-all(bf16[64,96,128]{2,1,0:T(8,128)(2,1)S(1)} %dispatch.1), channel_id=1, replica_groups=mesh['grp'=2,'ep'=32,'rep'=2] {'grp','ep'}, dimensions={0} | all-to-all | bytes 3145728 | tf_op jit(solution)/shard_map/all_to_all | solution.py:47
  37.3 0.0 copy-done
  37.3 0.0 copy-done.1
  37.3 0.0 copy-done.2
  37.3 0.0 copy-done.4
  37.3 0.0 copy-done.5
  37.3 0.0 copy-done.3
  37.3 0.0 copy-done.7
  37.4 2.5 %collective-permute-start = (bf16[64,32,128]{2,1,0:T(8,128)(2,1)S(1)}, bf16[64,32,128]{2,1,0:T(8,128)(2,1)S(1)}, u32[]{:S(2)}, u32[]{:S(2)}) collective-permute-start(bf16[64,32,128]{2,1,0:T(8,128)(2,1)S(1)} %split.1.routed), channel_id=1, source_target_pairs={{0,1},{1,0},{2,3},{3,2},{4,5},{5,4},{6,7},{7,6},{8,9},{9,8},{10,11... | collective-permute-start | bytes 1572872 | tf_op jit(solution)/shard_map/ppermute | solution.py:51
  39.8 1.8 %first_half.1 = (f32[2,64,256]{2,1,0:T(8,128)S(1)}, f32[64,128]{1,0:T(8,128)S(1)}, bf16[64,3584]{1,0:T(8,128)(2,1)S(1)}) custom-call(bf16[64,32,128]{2,1,0:T(8,128)(2,1)S(1)} %split.1.routed, f32[1,7168]{1,0:T(1,128)S(1)} %bitcast.31, bf16[7168,256]{1,0:T(8,128)(2,1)S(1)} %bitcast.15, bf16[7168,256]{1,0:T(8,128)(2,1)S(1)} %bitcast.18, bf16[64,7168]{1,0:T(8,128)(2,1)} %bitcast.26), custom_call_target="tpu_custom_call" | custom-call | flops 2000000000 | tf_op jit(solution)/shard_map/first_half/pallas_call | solution.py:195
  41.6 0.0 collective-permute-done.other.routed_other
  41.6 0.1 split_student.1.mine
  41.7 0.2 collective-permute-start.3
  41.9 0.4 collective-permute-start.2
  42.3 1.9 %experts.1 = (f32[2048,128]{1,0:T(8,128)S(1)}, bf16[2048,128]{1,0:T(8,128)(2,1)S(1)}, f32[8,128]{1,0:T(8,128)S(1)}) custom-call(bf16[64,32,128]{2,1,0:T(8,128)(2,1)S(1)} %collective-permute-done.other.routed_other, f32[2,64,256]{2,1,0:T(8,128)S(1)} %get-tuple-element.22.pre, f32[64,128]{1,0:T(8,128)S(1)} %get-tuple-element.23.squares, ...), custom_call_target="tpu_custom_call" | custom-call | flops 3000000000 | tf_op jit(solution)/shard_map/experts/pallas_call | solution.py:248
  44.2 0.2 collective-permute-start.1
  44.4 0.0 collective-permute-done.3.other
  44.4 2.3 %forward.1 = (f32[64,64,128]{2,1,0:T(8,128)S(1)}, bf16[64,64,128]{2,1,0:T(8,128)(2,1)S(1)}, bf16[112,128]{1,0:T(8,128)(2,1)S(1)}, f32[224,128]{1,0:T(8,128)S(1)}...) custom-call(bf16[64,64,128]{2,1,0:T(8,128)(2,1)S(1)} %split_student.1.mine, ...), custom_call_target="tpu_custom_call" | custom-call | flops 8000000000 | tf_op jit(solution)/shard_map/forward/pallas_call | solution.py:411
  46.8 0.4 collective-permute-start.4
  47.2 0.0 collective-permute-done.2.after.projection_other
  47.2 0.0 collective-permute-done.1.received
  47.2 0.0 copy-start.8
  47.2 0.0 copy-start.10
  47.2 0.0 copy-start.11
  47.2 0.1 merge.1
  47.3 17.0 %all_to_all.27 = bf16[64,32,128]{2,1,0:T(8,128)(2,1)S(1)} all-to-all(bf16[64,32,128]{2,1,0:T(8,128)(2,1)S(1)} %bitcast.29), channel_id=1, replica_groups=mesh['grp'=2,'ep'=32,'rep'=2] {'grp','ep'}, dimensions={0} | all-to-all | bytes 1048576 | tf_op jit(solution)/shard_map/all_to_all | solution.py:47
  64.4 0.0 collective-permute-done.4.received
  64.4 0.0 copy-done.8
  64.4 0.0 copy-done.10
  64.4 0.0 copy-done.11
  64.4 1.1 combine.1
  65.5 0.0 copy-start.6
  65.6 0.0 copy-start.9
  65.6 30.7 %all_to_all.28.arrived = bf16[64,120,128]{2,1,0:T(8,128)(2,1)S(1)} all-to-all(bf16[64,120,128]{2,1,0:T(8,128)(2,1)S(1)} %combine.1), channel_id=1, replica_groups=mesh['grp'=2,'ep'=32,'rep'=2] {'grp','ep'}, dimensions={0} | all-to-all | bytes 3932160 | tf_op jit(solution)/shard_map/all_to_all | solution.py:47
  96.2 0.0 copy-done.6
  96.2 0.0 copy-done.9
  96.3 0.9 targets.1
  97.2 3.2 %collective-permute-start.5 = (f32[64,128]{1,0:T(8,128)S(1)}, f32[64,128]{1,0:T(8,128)S(1)}, u32[]{:S(2)}, u32[]{:S(2)}) collective-permute-start(f32[64,128]{1,0:T(8,128)S(1)} %get-tuple-element.31), channel_id=1, source_target_pairs={{0,1},{1,0},{2,3},{3,2},{4,5},{5,4},{6,7},{7,6},{8,9},{9,8},{10,11... | collective-permute-start | bytes 98312 | tf_op jit(solution)/shard_map/ppermute | solution.py:51
  100.3 0.9 collective-permute-done.5.far
  101.2 0.1 deltas.1
  101.3 22.6 %all_to_all.29.d_mine = bf16[64,64,128]{2,1,0:T(8,128)(2,1)S(1)} all-to-all(bf16[64,64,128]{2,1,0:T(8,128)(2,1)S(1)} %deltas.1), channel_id=1, replica_groups=mesh['grp'=2,'ep'=32,'rep'=2] {'grp','ep'}, dimensions={0} | all-to-all | bytes 2097152 | tf_op jit(solution)/shard_map/all_to_all | solution.py:47
  123.9 1.8 %collective-permute-start.6 = (bf16[64,64,128]{2,1,0:T(8,128)(2,1)S(1)}, bf16[64,64,128]{2,1,0:T(8,128)(2,1)S(1)}, u32[]{:S(2)}, u32[]{:S(2)}) collective-permute-start(bf16[64,64,128]{2,1,0:T(8,128)(2,1)S(1)} %all_to_all.29.d_mine), channel_id=1, source_target_pairs={{0,1},{1,0},{2,3},{3,2},{4,5},{5,4},{6,7},{7,6},{8,9},{9,8},{10,11... | collective-permute-start | bytes 3145736 | tf_op jit(solution)/shard_map/ppermute | solution.py:51
  125.7 2.3 %collective-permute-done.6.d_other = bf16[64,64,128]{2,1,0:T(8,128)(2,1)S(1)} collective-permute-done((bf16[64,64,128]{2,1,0:T(8,128)(2,1)S(1)}, bf16[64,64,128]{2,1,0:T(8,128)(2,1)S(1)}, u32[]{:S(2)}, u32[]{:S(2)}) %collective-permute-start.6) | collective-permute-done | bytes 1048608 | tf_op jit(solution)/shard_map/ppermute | solution.py:51
  128.0 4.3 %backward.1 = (bf16[112,8192]{1,0:T(8,128)(2,1)}, bf16[112,8192]{1,0:T(8,128)(2,1)}, bf16[112,8192]{1,0:T(8,128)(2,1)}, f32[1,1]{1,0:T(1,128)}) custom-call(bf16[64,64,128]{2,1,0:T(8,128)(2,1)S(1)} %all_to_all.29.d_mine, bf16[64,64,128]{2,1,0:T(8,128)(2,1)S(1)} %collective-permute-done.6.d_other, bf16[64,2,64,128]{3,2,1,0:T(8,128)(2,1)S(1)} %get-tuple-element.32.x, ...), custom_call_target="tpu_custom_call" | custom-call | flops 8000000000 | tf_op jit(solution)/shard_map/backward/pallas_call | solution.py:558
  (1 shorter events, 0.0 us)
Async XLA Ops:
  0.6 36.6 %copy-start = (bf16[1,7168,256]{2,1,0:T(8,128)(2,1)S(1)}, bf16[1,7168,256]{2,1,0:T(8,128)(2,1)}, u32[]{:S(2)}) copy-start(bf16[1,7168,256]{2,1,0:T(8,128)(2,1)} %param.17) | copy-start | bytes 11010052
  0.6 36.6 %copy-start.1 = (bf16[1,7168,256]{2,1,0:T(8,128)(2,1)S(1)}, bf16[1,7168,256]{2,1,0:T(8,128)(2,1)}, u32[]{:S(2)}) copy-start(bf16[1,7168,256]{2,1,0:T(8,128)(2,1)} %param.18) | copy-start | bytes 11010052
  0.7 36.6 %copy-start.2 = (bf16[1,256,7168]{2,1,0:T(8,128)(2,1)S(1)}, bf16[1,256,7168]{2,1,0:T(8,128)(2,1)}, u32[]{:S(2)}) copy-start(bf16[1,256,7168]{2,1,0:T(8,128)(2,1)} %param.19) | copy-start | bytes 11010052
  0.7 36.6 %copy-start.4 = (bf16[8192,112]{0,1:T(8,128)(2,1)S(1)}, bf16[8192,112]{0,1:T(8,128)(2,1)}, u32[]{:S(2)}) copy-start(bf16[8192,112]{0,1:T(8,128)(2,1)} %param.24) | copy-start | bytes 5505028
  0.7 36.6 %copy-start.5 = (bf16[112,8192]{1,0:T(8,128)(2,1)S(1)}, bf16[112,8192]{1,0:T(8,128)(2,1)}, u32[]{:S(2)}) copy-start(bf16[112,8192]{1,0:T(8,128)(2,1)} %down.3) | copy-start | bytes 5505028
  2.2 35.1 %copy-start.3 = (bf16[8192,112]{0,1:T(8,128)(2,1)S(1)}, bf16[8192,112]{0,1:T(8,128)(2,1)}, u32[]{:S(2)}) copy-start(bf16[8192,112]{0,1:T(8,128)(2,1)} %param.23) | copy-start | bytes 5505028
  2.2 35.1 %copy-start.7 = (f32[7168]{0:T(1024)S(1)}, f32[7168]{0:T(1024)}, u32[]{:S(2)}) copy-start(f32[7168]{0:T(1024)} %param.14) | copy-start | bytes 86020
  37.4 4.2 %collective-permute-start = (bf16[64,32,128]{2,1,0:T(8,128)(2,1)S(1)}, bf16[64,32,128]{2,1,0:T(8,128)(2,1)S(1)}, u32[]{:S(2)}, u32[]{:S(2)}) collective-permute-start(bf16[64,32,128]{2,1,0:T(8,128)(2,1)S(1)} %split.1.routed), channel_id=1, source_target_pairs={{0,1},{1,0},{2,3},{3,2},{4,5},{5,4},{6,7},{7,6},{8,9},{9,8},{10,11... | collective-permute-start | bytes 1572872 | tf_op jit(solution)/shard_map/ppermute | solution.py:51
  41.7 2.7 %collective-permute-start.3 = (bf16[64,64,128]{2,1,0:T(8,128)(2,1)S(1)}, bf16[64,64,128]{2,1,0:T(8,128)(2,1)S(1)}, u32[]{:S(2)}, u32[]{:S(2)}) collective-permute-start(bf16[64,64,128]{2,1,0:T(8,128)(2,1)S(1)} %split_student.1.mine), channel_id=1, source_target_pairs={{0,1},{1,0},{2,3},{3,2},{4,5},{5,4},{6,7},{7,6},{8,9},{9,8},{10,11... | collective-permute-start | bytes 3145736 | tf_op jit(solution)/shard_map/ppermute | solution.py:51
  41.9 5.3 %collective-permute-start.2 = (bf16[64,3584]{1,0:T(8,128)(2,1)S(1)}, bf16[64,3584]{1,0:T(8,128)(2,1)S(1)}, u32[]{:S(2)}, u32[]{:S(2)}) collective-permute-start(bf16[64,3584]{1,0:T(8,128)(2,1)S(1)} %get-tuple-element.26), channel_id=1, source_target_pairs={{0,1},{1,0},{2,3},{3,2},{4,5},{5,4},{6,7},{7,6},{8,9},{9,8},{10,11... | collective-permute-start | bytes 1376264 | tf_op jit(solution)/shard_map/ppermute | solution.py:51
  44.2 3.0 %collective-permute-start.1 = (bf16[2048,128]{1,0:T(8,128)(2,1)S(1)}, bf16[2048,128]{1,0:T(8,128)(2,1)S(1)}, u32[]{:S(2)}, u32[]{:S(2)}) collective-permute-start(bf16[2048,128]{1,0:T(8,128)(2,1)S(1)} %get-tuple-element.25), channel_id=1, source_target_pairs={{0,1},{1,0},{2,3},{3,2},{4,5},{5,4},{6,7},{7,6},{8,9},{9,8},{10,11... | collective-permute-start | bytes 1572872 | tf_op jit(solution)/shard_map/ppermute | solution.py:51
  46.8 17.6 %collective-permute-start.4 = (bf16[64,64,128]{2,1,0:T(8,128)(2,1)S(1)}, bf16[64,64,128]{2,1,0:T(8,128)(2,1)S(1)}, u32[]{:S(2)}, u32[]{:S(2)}) collective-permute-start(bf16[64,64,128]{2,1,0:T(8,128)(2,1)S(1)} %get-tuple-element.29), channel_id=1, source_target_pairs={{0,1},{1,0},{2,3},{3,2},{4,5},{5,4},{6,7},{7,6},{8,9},{9,8},{10,11... | collective-permute-start | bytes 3145736 | tf_op jit(solution)/shard_map/ppermute | solution.py:51
  47.2 17.2 %copy-start.8 = (bf16[4,7168]{1,0:T(4,128)(2,1)S(1)}, bf16[4,7168]{1,0:T(4,128)(2,1)}, u32[]{:S(2)}) copy-start(bf16[4,7168]{1,0:T(4,128)(2,1)} %tokens.1) | copy-start | bytes 172036
  47.2 17.2 %copy-start.10 = (s32[4,8]{1,0:T(4,128)S(1)}, s32[4,8]{1,0:T(4,128)}, u32[]{:S(2)}) copy-start(s32[4,8]{1,0:T(4,128)} %routes.1) | copy-start | bytes 388
  47.2 17.2 %copy-start.11 = (f32[4,8]{1,0:T(4,128)S(1)}, f32[4,8]{1,0:T(4,128)}, u32[]{:S(2)}) copy-start(f32[4,8]{1,0:T(4,128)} %gates.1) | copy-start | bytes 388
  65.5 30.7 %copy-start.6 = (bf16[7168,64]{0,1:T(8,128)(2,1)S(1)}, bf16[7168,64]{0,1:T(8,128)(2,1)}, u32[]{:S(2)}) copy-start(bf16[7168,64]{0,1:T(8,128)(2,1)} %param.20) | copy-start | bytes 2752516
  65.6 30.7 %copy-start.9 = (bf16[128,64]{0,1:T(8,128)(2,1)S(1)}, bf16[128,64]{0,1:T(8,128)(2,1)}, u32[]{:S(2)}) copy-start(bf16[128,64]{0,1:T(8,128)(2,1)} %param.21) | copy-start | bytes 49156
  97.2 4.0 %collective-permute-start.5 = (f32[64,128]{1,0:T(8,128)S(1)}, f32[64,128]{1,0:T(8,128)S(1)}, u32[]{:S(2)}, u32[]{:S(2)}) collective-permute-start(f32[64,128]{1,0:T(8,128)S(1)} %get-tuple-element.31), channel_id=1, source_target_pairs={{0,1},{1,0},{2,3},{3,2},{4,5},{5,4},{6,7},{7,6},{8,9},{9,8},{10,11... | collective-permute-start | bytes 98312 | tf_op jit(solution)/shard_map/ppermute | solution.py:51
  123.9 4.1 %collective-permute-start.6 = (bf16[64,64,128]{2,1,0:T(8,128)(2,1)S(1)}, bf16[64,64,128]{2,1,0:T(8,128)(2,1)S(1)}, u32[]{:S(2)}, u32[]{:S(2)}) collective-permute-start(bf16[64,64,128]{2,1,0:T(8,128)(2,1)S(1)} %all_to_all.29.d_mine), channel_id=1, source_target_pairs={{0,1},{1,0},{2,3},{3,2},{4,5},{5,4},{6,7},{7,6},{8,9},{9,8},{10,11... | collective-permute-start | bytes 3145736 | tf_op jit(solution)/shard_map/ppermute | solution.py:51

commit v5 on v4

--- a/solution.py
+++ b/solution.py
@@ -12,6 +12,8 @@
 NT = (((1,), (1,)), ((), ()))
 TN = (((0,), (0,)), ((), ()))
 LANES = 128
+PIECES = 4
+SPARE = 16
 
 
 def dot(a, b, dims=NN):
@@ -94,36 +96,39 @@
     copies_in = [pltpu.make_async_copy(a, b, sems.at[n]) for n, (a, b) in enumerate(pairs)]
     for copy in copies_in:
         copy.start()
-    for copy in copies_in:
-        copy.wait()
     copies = lax.axis_size("grp")
     experts = lax.axis_size("ep")
     quarter = tokens.shape[1] // (copies * lax.axis_size("rep"))
     place = lax.axis_index("rep") * copies + lax.axis_index("grp")
     start = pl.multiple_of(place * quarter, quarter)
-    ids = routes[...]
-    chosen = slot_weights(ids, jnp.ones(ids.shape, jnp.float32), experts, 1)
     pieces = quarter // LANES
     stride = padded_pieces(pieces)
-    rows[...] = jnp.zeros(rows.shape, jnp.float32)
-    for n in range(pieces):
-        values = tokens[:, pl.ds(start + n * LANES, LANES)].astype(jnp.float32)
-        picked = sum(c * values[t : t + 1, :] for t, c in enumerate(chosen))
-        rows[pl.ds(n, 2 * experts, stride=stride), :] = picked
+    copies_in[2].wait()
+    copies_in[3].wait()
     here = student.shape[0]
     values = student[...].astype(jnp.float32)
     squares = jnp.sum(values * values, axis=0, keepdims=True)
     high = squares.astype(jnp.bfloat16).astype(jnp.float32)
     for n, part in enumerate((high, squares - high)):
-        place = pl.ds(pieces + n, 2 * experts, stride=stride)
-        rows[place, :] = jnp.broadcast_to(part, (2 * experts, LANES))
-    routed = rows[...].astype(jnp.bfloat16).reshape(experts, 2 * stride, LANES)
-    for n in range(copies):
-        out[n * experts : (n + 1) * experts, here:, :] = routed
+        rows[pl.ds(pieces + n, 2 * experts, stride=stride), :] = jnp.broadcast_to(
+            part, (2 * experts, LANES)
+        )
     columns = jnp.broadcast_to(gain[...], (LANES, LANES)).T
     columns = jnp.where(lax.axis_index("rep") == 0, columns[:here], columns[here:])
     block = (values * columns).astype(jnp.bfloat16)
     out[:, :here, :] = jnp.broadcast_to(block[None], (out.shape[0],) + block.shape)
+    copies_in[0].wait()
+    copies_in[1].wait()
+    ids = routes[...]
+    chosen = slot_weights(ids, jnp.ones(ids.shape, jnp.float32), experts, 1)
+    for n in range(pieces):
+        values = tokens[:, pl.ds(start + n * LANES, LANES)].astype(jnp.float32)
+        picked = sum(c * values[t : t + 1, :] for t, c in enumerate(chosen))
+        rows[pl.ds(n, 2 * experts, stride=stride), :] = picked
+    whole = rows[: 2 * experts * stride, :]
+    routed = whole.astype(jnp.bfloat16).reshape(experts, 2 * stride, LANES)
+    for n in range(copies):
+        out[n * experts : (n + 1) * experts, here:, :] = routed
 
 
 def dispatch(tokens, routes, student, gain):
@@ -136,7 +141,7 @@
         in_specs=[in_hbm()] * 4,
         out_specs=vmem(),
         scratch_shapes=[
-            pltpu.VMEM((experts * rows, LANES), jnp.float32),
+            pltpu.VMEM((experts * rows + SPARE, LANES), jnp.float32),
             pltpu.VMEM(tokens.shape, tokens.dtype),
             pltpu.VMEM(routes.shape, routes.dtype),
             pltpu.VMEM(student.shape, student.dtype),
@@ -155,12 +160,12 @@
 
 
 def scaled_tokens(source, gains, rows, scaled):
-    routed = rows.shape[0]
+    routed = source.shape[0] * source.shape[1]
     groups = lax.axis_size("grp")
     slots, half = scaled.shape
     pieces = half // (groups * LANES)
     stride = padded_pieces(pieces)
-    rows[...] = source.astype(jnp.float32).reshape(routed, LANES)
+    rows[:routed, :] = source.astype(jnp.float32).reshape(routed, LANES)
     squares = jnp.zeros((slots, LANES), jnp.float32)
     for g in range(groups):
         for m in range(pieces):
@@ -202,7 +207,7 @@
         in_specs=[vmem()] * 4 + [in_hbm()],
         out_specs=(vmem(),) * 3,
         scratch_shapes=[
-            pltpu.VMEM((routed.shape[0] * routed.shape[1], LANES), jnp.float32),
+            pltpu.VMEM((routed.shape[0] * routed.shape[1] + SPARE, LANES), jnp.float32),
             pltpu.VMEM((slots, half), jnp.bfloat16),
             pltpu.SemaphoreType.DMA,
         ],
@@ -238,7 +243,7 @@
             for m in range(pieces):
                 place = pl.ds(n * slots * stride + m, slots, stride=stride)
                 result[place, :] = out[:, m * LANES : (m + 1) * LANES]
-        dst[...] = result[...].astype(dst.dtype)
+        dst[...] = result[: dst.shape[0], :].astype(dst.dtype)
 
 
 def experts(other, pre, squares, gain, w_gate, w_up, w_down):
@@ -255,9 +260,9 @@
         in_specs=[vmem()] * 7,
         out_specs=(vmem(),) * 3,
         scratch_shapes=[
-            pltpu.VMEM(result, jnp.float32),
+            pltpu.VMEM((result[0] + SPARE, LANES), jnp.float32),
             pltpu.VMEM((slots, half), jnp.bfloat16),
-            pltpu.VMEM(result, jnp.float32),
+            pltpu.VMEM((result[0] + SPARE, LANES), jnp.float32),
         ],
         compiler_params=params(8),
         cost_estimate=cost(3),
@@ -277,7 +282,7 @@
     count = tokens.shape[0]
     weights = slot_weights(routes[...], gates[...], experts, copies)
     weights = [jnp.broadcast_to(w, (slots, LANES)) for w in weights]
-    rows[...] = returned[...].astype(jnp.float32)
+    rows[: returned.shape[0], :] = returned[...].astype(jnp.float32)
     for m in range(pieces):
         values = rows[pl.ds(m, slots, stride=stride), :]
         before = tokens[:, pl.ds(start + m * LANES, LANES)].astype(jnp.float32)
@@ -299,7 +304,7 @@
         in_specs=[vmem()] * 6,
         out_specs=vmem(),
         scratch_shapes=[
-            pltpu.VMEM(returned.shape, jnp.float32),
+            pltpu.VMEM((returned.shape[0] + SPARE, LANES), jnp.float32),
             pltpu.VMEM((own, LANES), jnp.float32),
         ],
         compiler_params=params(16),
@@ -362,10 +367,12 @@
 
 def start_interleaved(mine, other, dst, sems):
     core = lax.axis_index("rep")
-    copies = [
-        pltpu.make_async_copy(mine, dst.at[:, core], sems.at[0]),
-        pltpu.make_async_copy(other, dst.at[:, 1 - core], sems.at[1]),
-    ]
+    size = dst.shape[0] // PIECES
+    copies = []
+    for n in range(PIECES):
+        here = pl.ds(n * size, size)
+        for m, (src, to) in enumerate(((mine, core), (other, 1 - core))):
+            copies.append(pltpu.make_async_copy(src.at[here], dst.at[here, to], sems.at[m, n]))
     for copy in copies:
         copy.start()
     return copies
@@ -420,7 +427,7 @@
         ),
         in_specs=[anywhere()] * 2 + [vmem()] * 5 + [anywhere()],
         out_specs=(vmem(),) * 6,
-        scratch_shapes=[pltpu.SemaphoreType.DMA((2,))],
+        scratch_shapes=[pltpu.SemaphoreType.DMA((2, PIECES))],
         compiler_params=params(20),
         cost_estimate=cost(8),
         name="forward",
@@ -434,7 +441,8 @@
     groups = lax.axis_size("grp")
     pieces = half // (groups * lanes)
     start = pl.multiple_of(lax.axis_index("rep") * half, half)
-    rows[...] = arrived[:, here:, :].astype(jnp.float32).reshape(rows.shape)
+    whole = chips * (total - here)
+    rows[:whole, :] = arrived[:, here:, :].astype(jnp.float32).reshape(whole, lanes)
     for g in range(groups):
         for m in range(pieces):
             place = pl.ds(g * count * pieces + m, count, stride=pieces)
@@ -458,7 +466,7 @@
         in_specs=[vmem()] * 4,
         out_specs=(vmem(),) * 2,
         scratch_shapes=[
-            pltpu.VMEM((chips * (total - here), lanes), jnp.float32),
+            pltpu.VMEM((chips * (total - here) + SPARE, lanes), jnp.float32),
             pltpu.VMEM((count, half), jnp.bfloat16),
         ],
         compiler_params=params(16),
@@ -563,7 +571,7 @@
         scratch_shapes=[
             whole,
             *[pltpu.VMEM((hidden, features), jnp.bfloat16)] * 3,
-            pltpu.SemaphoreType.DMA((2,)),
+            pltpu.SemaphoreType.DMA((2, PIECES)),
             pltpu.SemaphoreType.DMA((3, 8)),
         ],
         compiler_params=params(24),

time: 133 us -> 132 us (level)
  transfers between devices with their start and end apart: 7 -> 7, of which waited for: 2 -> 2; matrix products, arithmetic and copies ran while one was open for 0% -> 0% of each run, Pallas kernels for 5% -> 4%
where the time goes in v5:
time: 132 us
  blocking collectives  105 us (80%)
  Pallas kernels  13.7 us (10%)
  starting transfers between devices  8.67 us (7%)
  waiting for transfers between devices  3.2 us (2%)
    all_to_all x4, blocking collectives, exchange(): lax.all_to_all(blocks, CHIPS, split_axis=0, concat_axis=0, tiled=True)  105 us
    ppermute x7, starting transfers between devices, other_core(): return lax.ppermute(values, 'rep', [(0, 1), (1, 0)])  8.67 us
    pallas_call x1, Pallas kernels, backward(): pl.pallas_call(backward_kernel, out_shape=(grad, grad, grad, jax.ShapeDty...  4.1 us
    ppermute x7, waiting for transfers between devices, other_core(): return lax.ppermute(values, 'rep', [(0, 1), (1, 0)])  3.2 us
  transfers between devices with their start and end apart: 7, of which 2 were waited for; matrix products, arithmetic and copies ran while one was open for 0% of the time, Pallas kernels for 4%

profile of v5, /device:TPU:1, one launch (start us, length us, event | category | flops | bytes accessed | tf_op | source)
XLA Modules:
  0.0 132.0 jit_solution(7121351253151605358)
XLA Ops:
  0.6 0.0 copy-start
  0.6 0.0 copy-start.1
  0.7 0.0 copy-start.2
  0.7 0.0 copy-start.4
  0.7 0.0 copy-start.5
  0.7 1.5 %dispatch.1 = bf16[64,96,128]{2,1,0:T(8,128)(2,1)S(1)} custom-call(bf16[4,7168]{1,0:T(4,128)(2,1)} %tokens.1, s32[4,8]{1,0:T(4,128)} %routes.1, bf16[64,128]{1,0:T(8,128)(2,1)} %bitcast.33, f32[1,8192]{1,0:T(1,128)} %bitcast.35), custom_call_target="tpu_custom_call" | custom-call | flops 30000001024 | tf_op jit(solution)/shard_map/dispatch/pallas_call | solution.py:138
  2.2 0.0 copy-start.3
  2.2 0.0 copy-start.7
  2.2 35.0 %all_to_all.26.arrived = bf16[64,96,128]{2,1,0:T(8,128)(2,1)S(1)} all-to-all(bf16[64,96,128]{2,1,0:T(8,128)(2,1)S(1)} %dispatch.1), channel_id=1, replica_groups=mesh['grp'=2,'ep'=32,'rep'=2] {'grp','ep'}, dimensions={0} | all-to-all | bytes 3145728 | tf_op jit(solution)/shard_map/all_to_all | solution.py:49
  37.2 0.0 copy-done
  37.2 0.0 copy-done.1
  37.2 0.0 copy-done.2
  37.2 0.0 copy-done.4
  37.2 0.0 copy-done.5
  37.2 0.0 copy-done.3
  37.3 0.0 copy-done.7
  37.3 2.5 %collective-permute-start = (bf16[64,32,128]{2,1,0:T(8,128)(2,1)S(1)}, bf16[64,32,128]{2,1,0:T(8,128)(2,1)S(1)}, u32[]{:S(2)}, u32[]{:S(2)}) collective-permute-start(bf16[64,32,128]{2,1,0:T(8,128)(2,1)S(1)} %split.1.routed), channel_id=1, source_target_pairs={{0,1},{1,0},{2,3},{3,2},{4,5},{5,4},{6,7},{7,6},{8,9},{9,8},{10,11... | collective-permute-start | bytes 1572872 | tf_op jit(solution)/shard_map/ppermute | solution.py:53
  39.8 1.8 %first_half.1 = (f32[2,64,256]{2,1,0:T(8,128)S(1)}, f32[64,128]{1,0:T(8,128)S(1)}, bf16[64,3584]{1,0:T(8,128)(2,1)S(1)}) custom-call(bf16[64,32,128]{2,1,0:T(8,128)(2,1)S(1)} %split.1.routed, f32[1,7168]{1,0:T(1,128)S(1)} %bitcast.31, bf16[7168,256]{1,0:T(8,128)(2,1)S(1)} %bitcast.15, bf16[7168,256]{1,0:T(8,128)(2,1)S(1)} %bitcast.18, bf16[64,7168]{1,0:T(8,128)(2,1)} %bitcast.26), custom_call_target="tpu_custom_call" | custom-call | flops 2000000000 | tf_op jit(solution)/shard_map/first_half/pallas_call | solution.py:200
  41.5 0.0 collective-permute-done.other.routed_other
  41.5 0.1 split_student.1.mine
  41.6 0.2 collective-permute-start.3
  41.8 0.4 collective-permute-start.2
  42.2 1.9 %experts.1 = (f32[2048,128]{1,0:T(8,128)S(1)}, bf16[2048,128]{1,0:T(8,128)(2,1)S(1)}, f32[8,128]{1,0:T(8,128)S(1)}) custom-call(bf16[64,32,128]{2,1,0:T(8,128)(2,1)S(1)} %collective-permute-done.other.routed_other, f32[2,64,256]{2,1,0:T(8,128)S(1)} %get-tuple-element.22.pre, f32[64,128]{1,0:T(8,128)S(1)} %get-tuple-element.23.squares, ...), custom_call_target="tpu_custom_call" | custom-call | flops 3000000000 | tf_op jit(solution)/shard_map/experts/pallas_call | solution.py:253
  44.1 0.2 collective-permute-start.1
  44.3 0.0 collective-permute-done.3.other
  44.4 2.2 %forward.1 = (f32[64,64,128]{2,1,0:T(8,128)S(1)}, bf16[64,64,128]{2,1,0:T(8,128)(2,1)S(1)}, bf16[112,128]{1,0:T(8,128)(2,1)S(1)}, f32[224,128]{1,0:T(8,128)S(1)}...) custom-call(bf16[64,64,128]{2,1,0:T(8,128)(2,1)S(1)} %split_student.1.mine, ...), custom_call_target="tpu_custom_call" | custom-call | flops 8000000000 | tf_op jit(solution)/shard_map/forward/pallas_call | solution.py:418
  46.5 0.4 collective-permute-start.4
  47.0 0.0 collective-permute-done.2.after.projection_other
  47.0 0.0 collective-permute-done.1.received
  47.0 0.0 copy-start.8
  47.0 0.0 copy-start.10
  47.0 0.0 copy-start.11
  47.0 0.1 merge.1
  47.1 17.0 %all_to_all.27 = bf16[64,32,128]{2,1,0:T(8,128)(2,1)S(1)} all-to-all(bf16[64,32,128]{2,1,0:T(8,128)(2,1)S(1)} %bitcast.29), channel_id=1, replica_groups=mesh['grp'=2,'ep'=32,'rep'=2] {'grp','ep'}, dimensions={0} | all-to-all | bytes 1048576 | tf_op jit(solution)/shard_map/all_to_all | solution.py:49
  64.1 0.0 collective-permute-done.4.received
  64.1 0.0 copy-done.8
  64.1 0.0 copy-done.10
  64.2 0.0 copy-done.11
  64.2 1.1 combine.1
  65.3 0.0 copy-start.6
  65.3 0.0 copy-start.9
  65.3 30.7 %all_to_all.28.arrived = bf16[64,120,128]{2,1,0:T(8,128)(2,1)S(1)} all-to-all(bf16[64,120,128]{2,1,0:T(8,128)(2,1)S(1)} %combine.1), channel_id=1, replica_groups=mesh['grp'=2,'ep'=32,'rep'=2] {'grp','ep'}, dimensions={0} | all-to-all | bytes 3932160 | tf_op jit(solution)/shard_map/all_to_all | solution.py:49
  96.0 0.0 copy-done.6
  96.0 0.0 copy-done.9
  96.0 0.9 targets.1
  96.9 3.2 %collective-permute-start.5 = (f32[64,128]{1,0:T(8,128)S(1)}, f32[64,128]{1,0:T(8,128)S(1)}, u32[]{:S(2)}, u32[]{:S(2)}) collective-permute-start(f32[64,128]{1,0:T(8,128)S(1)} %get-tuple-element.31), channel_id=1, source_target_pairs={{0,1},{1,0},{2,3},{3,2},{4,5},{5,4},{6,7},{7,6},{8,9},{9,8},{10,11... | collective-permute-start | bytes 98312 | tf_op jit(solution)/shard_map/ppermute | solution.py:53
  100.1 0.9 collective-permute-done.5.far
  100.9 0.1 deltas.1
  101.1 22.6 %all_to_all.29.d_mine = bf16[64,64,128]{2,1,0:T(8,128)(2,1)S(1)} all-to-all(bf16[64,64,128]{2,1,0:T(8,128)(2,1)S(1)} %deltas.1), channel_id=1, replica_groups=mesh['grp'=2,'ep'=32,'rep'=2] {'grp','ep'}, dimensions={0} | all-to-all | bytes 2097152 | tf_op jit(solution)/shard_map/all_to_all | solution.py:49
  123.7 1.8 %collective-permute-start.6 = (bf16[64,64,128]{2,1,0:T(8,128)(2,1)S(1)}, bf16[64,64,128]{2,1,0:T(8,128)(2,1)S(1)}, u32[]{:S(2)}, u32[]{:S(2)}) collective-permute-start(bf16[64,64,128]{2,1,0:T(8,128)(2,1)S(1)} %all_to_all.29.d_mine), channel_id=1, source_target_pairs={{0,1},{1,0},{2,3},{3,2},{4,5},{5,4},{6,7},{7,6},{8,9},{9,8},{10,11... | collective-permute-start | bytes 3145736 | tf_op jit(solution)/shard_map/ppermute | solution.py:53
  125.5 2.3 %collective-permute-done.6.d_other = bf16[64,64,128]{2,1,0:T(8,128)(2,1)S(1)} collective-permute-done((bf16[64,64,128]{2,1,0:T(8,128)(2,1)S(1)}, bf16[64,64,128]{2,1,0:T(8,128)(2,1)S(1)}, u32[]{:S(2)}, u32[]{:S(2)}) %collective-permute-start.6) | collective-permute-done | bytes 1048608 | tf_op jit(solution)/shard_map/ppermute | solution.py:53
  127.8 4.1 %backward.1 = (bf16[112,8192]{1,0:T(8,128)(2,1)}, bf16[112,8192]{1,0:T(8,128)(2,1)}, bf16[112,8192]{1,0:T(8,128)(2,1)}, f32[1,1]{1,0:T(1,128)}) custom-call(bf16[64,64,128]{2,1,0:T(8,128)(2,1)S(1)} %all_to_all.29.d_mine, bf16[64,64,128]{2,1,0:T(8,128)(2,1)S(1)} %collective-permute-done.6.d_other, bf16[64,2,64,128]{3,2,1,0:T(8,128)(2,1)S(1)} %get-tuple-element.32.x, ...), custom_call_target="tpu_custom_call" | custom-call | flops 8000000000 | tf_op jit(solution)/shard_map/backward/pallas_call | solution.py:566
  (1 shorter events, 0.0 us)
Async XLA Ops:
  0.6 36.6 %copy-start = (bf16[1,7168,256]{2,1,0:T(8,128)(2,1)S(1)}, bf16[1,7168,256]{2,1,0:T(8,128)(2,1)}, u32[]{:S(2)}) copy-start(bf16[1,7168,256]{2,1,0:T(8,128)(2,1)} %param.17) | copy-start | bytes 11010052
  0.6 36.6 %copy-start.1 = (bf16[1,7168,256]{2,1,0:T(8,128)(2,1)S(1)}, bf16[1,7168,256]{2,1,0:T(8,128)(2,1)}, u32[]{:S(2)}) copy-start(bf16[1,7168,256]{2,1,0:T(8,128)(2,1)} %param.18) | copy-start | bytes 11010052
  0.7 36.6 %copy-start.2 = (bf16[1,256,7168]{2,1,0:T(8,128)(2,1)S(1)}, bf16[1,256,7168]{2,1,0:T(8,128)(2,1)}, u32[]{:S(2)}) copy-start(bf16[1,256,7168]{2,1,0:T(8,128)(2,1)} %param.19) | copy-start | bytes 11010052
  0.7 36.6 %copy-start.4 = (bf16[8192,112]{0,1:T(8,128)(2,1)S(1)}, bf16[8192,112]{0,1:T(8,128)(2,1)}, u32[]{:S(2)}) copy-start(bf16[8192,112]{0,1:T(8,128)(2,1)} %param.24) | copy-start | bytes 5505028
  0.7 36.6 %copy-start.5 = (bf16[112,8192]{1,0:T(8,128)(2,1)S(1)}, bf16[112,8192]{1,0:T(8,128)(2,1)}, u32[]{:S(2)}) copy-start(bf16[112,8192]{1,0:T(8,128)(2,1)} %down.3) | copy-start | bytes 5505028
  2.2 35.1 %copy-start.3 = (bf16[8192,112]{0,1:T(8,128)(2,1)S(1)}, bf16[8192,112]{0,1:T(8,128)(2,1)}, u32[]{:S(2)}) copy-start(bf16[8192,112]{0,1:T(8,128)(2,1)} %param.23) | copy-start | bytes 5505028
  2.2 35.1 %copy-start.7 = (f32[7168]{0:T(1024)S(1)}, f32[7168]{0:T(1024)}, u32[]{:S(2)}) copy-start(f32[7168]{0:T(1024)} %param.14) | copy-start | bytes 86020
  37.3 4.2 %collective-permute-start = (bf16[64,32,128]{2,1,0:T(8,128)(2,1)S(1)}, bf16[64,32,128]{2,1,0:T(8,128)(2,1)S(1)}, u32[]{:S(2)}, u32[]{:S(2)}) collective-permute-start(bf16[64,32,128]{2,1,0:T(8,128)(2,1)S(1)} %split.1.routed), channel_id=1, source_target_pairs={{0,1},{1,0},{2,3},{3,2},{4,5},{5,4},{6,7},{7,6},{8,9},{9,8},{10,11... | collective-permute-start | bytes 1572872 | tf_op jit(solution)/shard_map/ppermute | solution.py:53
  41.6 2.7 %collective-permute-start.3 = (bf16[64,64,128]{2,1,0:T(8,128)(2,1)S(1)}, bf16[64,64,128]{2,1,0:T(8,128)(2,1)S(1)}, u32[]{:S(2)}, u32[]{:S(2)}) collective-permute-start(bf16[64,64,128]{2,1,0:T(8,128)(2,1)S(1)} %split_student.1.mine), channel_id=1, source_target_pairs={{0,1},{1,0},{2,3},{3,2},{4,5},{5,4},{6,7},{7,6},{8,9},{9,8},{10,11... | collective-permute-start | bytes 3145736 | tf_op jit(solution)/shard_map/ppermute | solution.py:53
  41.8 5.1 %collective-permute-start.2 = (bf16[64,3584]{1,0:T(8,128)(2,1)S(1)}, bf16[64,3584]{1,0:T(8,128)(2,1)S(1)}, u32[]{:S(2)}, u32[]{:S(2)}) collective-permute-start(bf16[64,3584]{1,0:T(8,128)(2,1)S(1)} %get-tuple-element.26), channel_id=1, source_target_pairs={{0,1},{1,0},{2,3},{3,2},{4,5},{5,4},{6,7},{7,6},{8,9},{9,8},{10,11... | collective-permute-start | bytes 1376264 | tf_op jit(solution)/shard_map/ppermute | solution.py:53
  44.1 2.8 %collective-permute-start.1 = (bf16[2048,128]{1,0:T(8,128)(2,1)S(1)}, bf16[2048,128]{1,0:T(8,128)(2,1)S(1)}, u32[]{:S(2)}, u32[]{:S(2)}) collective-permute-start(bf16[2048,128]{1,0:T(8,128)(2,1)S(1)} %get-tuple-element.25), channel_id=1, source_target_pairs={{0,1},{1,0},{2,3},{3,2},{4,5},{5,4},{6,7},{7,6},{8,9},{9,8},{10,11... | collective-permute-start | bytes 1572872 | tf_op jit(solution)/shard_map/ppermute | solution.py:53
  46.5 17.6 %collective-permute-start.4 = (bf16[64,64,128]{2,1,0:T(8,128)(2,1)S(1)}, bf16[64,64,128]{2,1,0:T(8,128)(2,1)S(1)}, u32[]{:S(2)}, u32[]{:S(2)}) collective-permute-start(bf16[64,64,128]{2,1,0:T(8,128)(2,1)S(1)} %get-tuple-element.29), channel_id=1, source_target_pairs={{0,1},{1,0},{2,3},{3,2},{4,5},{5,4},{6,7},{7,6},{8,9},{9,8},{10,11... | collective-permute-start | bytes 3145736 | tf_op jit(solution)/shard_map/ppermute | solution.py:53
  47.0 17.2 %copy-start.8 = (bf16[4,7168]{1,0:T(4,128)(2,1)S(1)}, bf16[4,7168]{1,0:T(4,128)(2,1)}, u32[]{:S(2)}) copy-start(bf16[4,7168]{1,0:T(4,128)(2,1)} %tokens.1) | copy-start | bytes 172036
  47.0 17.2 %copy-start.10 = (s32[4,8]{1,0:T(4,128)S(1)}, s32[4,8]{1,0:T(4,128)}, u32[]{:S(2)}) copy-start(s32[4,8]{1,0:T(4,128)} %routes.1) | copy-start | bytes 388
  47.0 17.2 %copy-start.11 = (f32[4,8]{1,0:T(4,128)S(1)}, f32[4,8]{1,0:T(4,128)}, u32[]{:S(2)}) copy-start(f32[4,8]{1,0:T(4,128)} %gates.1) | copy-start | bytes 388
  65.3 30.7 %copy-start.6 = (bf16[7168,64]{0,1:T(8,128)(2,1)S(1)}, bf16[7168,64]{0,1:T(8,128)(2,1)}, u32[]{:S(2)}) copy-start(bf16[7168,64]{0,1:T(8,128)(2,1)} %param.20) | copy-start | bytes 2752516
  65.3 30.7 %copy-start.9 = (bf16[128,64]{0,1:T(8,128)(2,1)S(1)}, bf16[128,64]{0,1:T(8,128)(2,1)}, u32[]{:S(2)}) copy-start(bf16[128,64]{0,1:T(8,128)(2,1)} %param.21) | copy-start | bytes 49156
  96.9 4.0 %collective-permute-start.5 = (f32[64,128]{1,0:T(8,128)S(1)}, f32[64,128]{1,0:T(8,128)S(1)}, u32[]{:S(2)}, u32[]{:S(2)}) collective-permute-start(f32[64,128]{1,0:T(8,128)S(1)} %get-tuple-element.31), channel_id=1, source_target_pairs={{0,1},{1,0},{2,3},{3,2},{4,5},{5,4},{6,7},{7,6},{8,9},{9,8},{10,11... | collective-permute-start | bytes 98312 | tf_op jit(solution)/shard_map/ppermute | solution.py:53
  123.7 4.1 %collective-permute-start.6 = (bf16[64,64,128]{2,1,0:T(8,128)(2,1)S(1)}, bf16[64,64,128]{2,1,0:T(8,128)(2,1)S(1)}, u32[]{:S(2)}, u32[]{:S(2)}) collective-permute-start(bf16[64,64,128]{2,1,0:T(8,128)(2,1)S(1)} %all_to_all.29.d_mine), channel_id=1, source_target_pairs={{0,1},{1,0},{2,3},{3,2},{4,5},{5,4},{6,7},{7,6},{8,9},{9,8},{10,11... | collective-permute-start | bytes 3145736 | tf_op jit(solution)/shard_map/ppermute | solution.py:53

commit v6 on v5

--- a/solution.py
+++ b/solution.py
@@ -12,7 +12,7 @@
 NT = (((1,), (1,)), ((), ()))
 TN = (((0,), (0,)), ((), ()))
 LANES = 128
-PIECES = 4
+PIECES = 8
 SPARE = 16
 
 

time: 132 us -> 133 us (level)
  transfers between devices with their start and end apart: 7 -> 7, of which waited for: 2 -> 2; matrix products, arithmetic and copies ran while one was open for 0% -> 0% of each run, Pallas kernels for 4% -> 5%
where the time goes in v6:
time: 133 us
  blocking collectives  105 us (79%)
  Pallas kernels  14.3 us (11%)
  starting transfers between devices  8.66 us (7%)
  waiting for transfers between devices  3.2 us (2%)
    all_to_all x4, blocking collectives, exchange(): lax.all_to_all(blocks, CHIPS, split_axis=0, concat_axis=0, tiled=True)  105 us
    ppermute x7, starting transfers between devices, other_core(): return lax.ppermute(values, 'rep', [(0, 1), (1, 0)])  8.66 us
    pallas_call x1, Pallas kernels, backward(): pl.pallas_call(backward_kernel, out_shape=(grad, grad, grad, jax.ShapeDty...  4.39 us
    ppermute x7, waiting for transfers between devices, other_core(): return lax.ppermute(values, 'rep', [(0, 1), (1, 0)])  3.2 us
  transfers between devices with their start and end apart: 7, of which 2 were waited for; matrix products, arithmetic and copies ran while one was open for 0% of the time, Pallas kernels for 5%

profile of v6, /device:TPU:1, one launch (start us, length us, event | category | flops | bytes accessed | tf_op | source)
XLA Modules:
  0.0 132.6 jit_solution(979353114770623327)
XLA Ops:
  0.6 0.0 copy-start
  0.6 0.0 copy-start.1
  0.7 0.0 copy-start.2
  0.7 0.0 copy-start.4
  0.7 0.0 copy-start.5
  0.7 1.5 %dispatch.1 = bf16[64,96,128]{2,1,0:T(8,128)(2,1)S(1)} custom-call(bf16[4,7168]{1,0:T(4,128)(2,1)} %tokens.1, s32[4,8]{1,0:T(4,128)} %routes.1, bf16[64,128]{1,0:T(8,128)(2,1)} %bitcast.33, f32[1,8192]{1,0:T(1,128)} %bitcast.35), custom_call_target="tpu_custom_call" | custom-call | flops 30000001024 | tf_op jit(solution)/shard_map/dispatch/pallas_call | solution.py:138
  2.2 0.0 copy-start.3
  2.2 0.0 copy-start.7
  2.2 35.0 %all_to_all.26.arrived = bf16[64,96,128]{2,1,0:T(8,128)(2,1)S(1)} all-to-all(bf16[64,96,128]{2,1,0:T(8,128)(2,1)S(1)} %dispatch.1), channel_id=1, replica_groups=mesh['grp'=2,'ep'=32,'rep'=2] {'grp','ep'}, dimensions={0} | all-to-all | bytes 3145728 | tf_op jit(solution)/shard_map/all_to_all | solution.py:49
  37.2 0.0 copy-done
  37.2 0.0 copy-done.1
  37.2 0.0 copy-done.2
  37.2 0.0 copy-done.4
  37.2 0.0 copy-done.5
  37.2 0.0 copy-done.3
  37.3 0.0 copy-done.7
  37.3 2.5 %collective-permute-start = (bf16[64,32,128]{2,1,0:T(8,128)(2,1)S(1)}, bf16[64,32,128]{2,1,0:T(8,128)(2,1)S(1)}, u32[]{:S(2)}, u32[]{:S(2)}) collective-permute-start(bf16[64,32,128]{2,1,0:T(8,128)(2,1)S(1)} %split.1.routed), channel_id=1, source_target_pairs={{0,1},{1,0},{2,3},{3,2},{4,5},{5,4},{6,7},{7,6},{8,9},{9,8},{10,11... | collective-permute-start | bytes 1572872 | tf_op jit(solution)/shard_map/ppermute | solution.py:53
  39.8 1.8 %first_half.1 = (f32[2,64,256]{2,1,0:T(8,128)S(1)}, f32[64,128]{1,0:T(8,128)S(1)}, bf16[64,3584]{1,0:T(8,128)(2,1)S(1)}) custom-call(bf16[64,32,128]{2,1,0:T(8,128)(2,1)S(1)} %split.1.routed, f32[1,7168]{1,0:T(1,128)S(1)} %bitcast.31, bf16[7168,256]{1,0:T(8,128)(2,1)S(1)} %bitcast.15, bf16[7168,256]{1,0:T(8,128)(2,1)S(1)} %bitcast.18, bf16[64,7168]{1,0:T(8,128)(2,1)} %bitcast.26), custom_call_target="tpu_custom_call" | custom-call | flops 2000000000 | tf_op jit(solution)/shard_map/first_half/pallas_call | solution.py:200
  41.5 0.0 collective-permute-done.other.routed_other
  41.5 0.1 split_student.1.mine
  41.6 0.2 collective-permute-start.3
  41.8 0.4 collective-permute-start.2
  42.2 1.9 %experts.1 = (f32[2048,128]{1,0:T(8,128)S(1)}, bf16[2048,128]{1,0:T(8,128)(2,1)S(1)}, f32[8,128]{1,0:T(8,128)S(1)}) custom-call(bf16[64,32,128]{2,1,0:T(8,128)(2,1)S(1)} %collective-permute-done.other.routed_other, f32[2,64,256]{2,1,0:T(8,128)S(1)} %get-tuple-element.22.pre, f32[64,128]{1,0:T(8,128)S(1)} %get-tuple-element.23.squares, ...), custom_call_target="tpu_custom_call" | custom-call | flops 3000000000 | tf_op jit(solution)/shard_map/experts/pallas_call | solution.py:253
  44.1 0.2 collective-permute-start.1
  44.3 0.0 collective-permute-done.3.other
  44.4 2.4 %forward.1 = (f32[64,64,128]{2,1,0:T(8,128)S(1)}, bf16[64,64,128]{2,1,0:T(8,128)(2,1)S(1)}, bf16[112,128]{1,0:T(8,128)(2,1)S(1)}, f32[224,128]{1,0:T(8,128)S(1)}...) custom-call(bf16[64,64,128]{2,1,0:T(8,128)(2,1)S(1)} %split_student.1.mine, ...), custom_call_target="tpu_custom_call" | custom-call | flops 8000000000 | tf_op jit(solution)/shard_map/forward/pallas_call | solution.py:418
  46.8 0.4 collective-permute-start.4
  47.2 0.0 collective-permute-done.2.after.projection_other
  47.3 0.0 collective-permute-done.1.received
  47.3 0.0 copy-start.8
  47.3 0.0 copy-start.10
  47.3 0.0 copy-start.11
  47.3 0.1 merge.1
  47.4 17.0 %all_to_all.27 = bf16[64,32,128]{2,1,0:T(8,128)(2,1)S(1)} all-to-all(bf16[64,32,128]{2,1,0:T(8,128)(2,1)S(1)} %bitcast.29), channel_id=1, replica_groups=mesh['grp'=2,'ep'=32,'rep'=2] {'grp','ep'}, dimensions={0} | all-to-all | bytes 1048576 | tf_op jit(solution)/shard_map/all_to_all | solution.py:49
  64.4 0.0 collective-permute-done.4.received
  64.4 0.0 copy-done.8
  64.4 0.0 copy-done.10
  64.4 0.0 copy-done.11
  64.5 1.1 combine.1
  65.6 0.0 copy-start.6
  65.6 0.0 copy-start.9
  65.6 30.7 %all_to_all.28.arrived = bf16[64,120,128]{2,1,0:T(8,128)(2,1)S(1)} all-to-all(bf16[64,120,128]{2,1,0:T(8,128)(2,1)S(1)} %combine.1), channel_id=1, replica_groups=mesh['grp'=2,'ep'=32,'rep'=2] {'grp','ep'}, dimensions={0} | all-to-all | bytes 3932160 | tf_op jit(solution)/shard_map/all_to_all | solution.py:49
  96.3 0.0 copy-done.6
  96.3 0.0 copy-done.9
  96.3 0.9 targets.1
  97.2 3.2 %collective-permute-start.5 = (f32[64,128]{1,0:T(8,128)S(1)}, f32[64,128]{1,0:T(8,128)S(1)}, u32[]{:S(2)}, u32[]{:S(2)}) collective-permute-start(f32[64,128]{1,0:T(8,128)S(1)} %get-tuple-element.31), channel_id=1, source_target_pairs={{0,1},{1,0},{2,3},{3,2},{4,5},{5,4},{6,7},{7,6},{8,9},{9,8},{10,11... | collective-permute-start | bytes 98312 | tf_op jit(solution)/shard_map/ppermute | solution.py:53
  100.4 0.9 collective-permute-done.5.far
  101.3 0.1 deltas.1
  101.4 22.6 %all_to_all.29.d_mine = bf16[64,64,128]{2,1,0:T(8,128)(2,1)S(1)} all-to-all(bf16[64,64,128]{2,1,0:T(8,128)(2,1)S(1)} %deltas.1), channel_id=1, replica_groups=mesh['grp'=2,'ep'=32,'rep'=2] {'grp','ep'}, dimensions={0} | all-to-all | bytes 2097152 | tf_op jit(solution)/shard_map/all_to_all | solution.py:49
  124.0 1.8 %collective-permute-start.6 = (bf16[64,64,128]{2,1,0:T(8,128)(2,1)S(1)}, bf16[64,64,128]{2,1,0:T(8,128)(2,1)S(1)}, u32[]{:S(2)}, u32[]{:S(2)}) collective-permute-start(bf16[64,64,128]{2,1,0:T(8,128)(2,1)S(1)} %all_to_all.29.d_mine), channel_id=1, source_target_pairs={{0,1},{1,0},{2,3},{3,2},{4,5},{5,4},{6,7},{7,6},{8,9},{9,8},{10,11... | collective-permute-start | bytes 3145736 | tf_op jit(solution)/shard_map/ppermute | solution.py:53
  125.8 2.3 %collective-permute-done.6.d_other = bf16[64,64,128]{2,1,0:T(8,128)(2,1)S(1)} collective-permute-done((bf16[64,64,128]{2,1,0:T(8,128)(2,1)S(1)}, bf16[64,64,128]{2,1,0:T(8,128)(2,1)S(1)}, u32[]{:S(2)}, u32[]{:S(2)}) %collective-permute-start.6) | collective-permute-done | bytes 1048608 | tf_op jit(solution)/shard_map/ppermute | solution.py:53
  128.1 4.4 %backward.1 = (bf16[112,8192]{1,0:T(8,128)(2,1)}, bf16[112,8192]{1,0:T(8,128)(2,1)}, bf16[112,8192]{1,0:T(8,128)(2,1)}, f32[1,1]{1,0:T(1,128)}) custom-call(bf16[64,64,128]{2,1,0:T(8,128)(2,1)S(1)} %all_to_all.29.d_mine, bf16[64,64,128]{2,1,0:T(8,128)(2,1)S(1)} %collective-permute-done.6.d_other, bf16[64,2,64,128]{3,2,1,0:T(8,128)(2,1)S(1)} %get-tuple-element.32.x, ...), custom_call_target="tpu_custom_call" | custom-call | flops 8000000000 | tf_op jit(solution)/shard_map/backward/pallas_call | solution.py:566
  (1 shorter events, 0.0 us)
Async XLA Ops:
  0.6 36.6 %copy-start = (bf16[1,7168,256]{2,1,0:T(8,128)(2,1)S(1)}, bf16[1,7168,256]{2,1,0:T(8,128)(2,1)}, u32[]{:S(2)}) copy-start(bf16[1,7168,256]{2,1,0:T(8,128)(2,1)} %param.17) | copy-start | bytes 11010052
  0.6 36.6 %copy-start.1 = (bf16[1,7168,256]{2,1,0:T(8,128)(2,1)S(1)}, bf16[1,7168,256]{2,1,0:T(8,128)(2,1)}, u32[]{:S(2)}) copy-start(bf16[1,7168,256]{2,1,0:T(8,128)(2,1)} %param.18) | copy-start | bytes 11010052
  0.7 36.6 %copy-start.2 = (bf16[1,256,7168]{2,1,0:T(8,128)(2,1)S(1)}, bf16[1,256,7168]{2,1,0:T(8,128)(2,1)}, u32[]{:S(2)}) copy-start(bf16[1,256,7168]{2,1,0:T(8,128)(2,1)} %param.19) | copy-start | bytes 11010052
  0.7 36.6 %copy-start.4 = (bf16[8192,112]{0,1:T(8,128)(2,1)S(1)}, bf16[8192,112]{0,1:T(8,128)(2,1)}, u32[]{:S(2)}) copy-start(bf16[8192,112]{0,1:T(8,128)(2,1)} %param.24) | copy-start | bytes 5505028
  0.7 36.6 %copy-start.5 = (bf16[112,8192]{1,0:T(8,128)(2,1)S(1)}, bf16[112,8192]{1,0:T(8,128)(2,1)}, u32[]{:S(2)}) copy-start(bf16[112,8192]{1,0:T(8,128)(2,1)} %down.3) | copy-start | bytes 5505028
  2.2 35.1 %copy-start.3 = (bf16[8192,112]{0,1:T(8,128)(2,1)S(1)}, bf16[8192,112]{0,1:T(8,128)(2,1)}, u32[]{:S(2)}) copy-start(bf16[8192,112]{0,1:T(8,128)(2,1)} %param.23) | copy-start | bytes 5505028
  2.2 35.1 %copy-start.7 = (f32[7168]{0:T(1024)S(1)}, f32[7168]{0:T(1024)}, u32[]{:S(2)}) copy-start(f32[7168]{0:T(1024)} %param.14) | copy-start | bytes 86020
  37.3 4.2 %collective-permute-start = (bf16[64,32,128]{2,1,0:T(8,128)(2,1)S(1)}, bf16[64,32,128]{2,1,0:T(8,128)(2,1)S(1)}, u32[]{:S(2)}, u32[]{:S(2)}) collective-permute-start(bf16[64,32,128]{2,1,0:T(8,128)(2,1)S(1)} %split.1.routed), channel_id=1, source_target_pairs={{0,1},{1,0},{2,3},{3,2},{4,5},{5,4},{6,7},{7,6},{8,9},{9,8},{10,11... | collective-permute-start | bytes 1572872 | tf_op jit(solution)/shard_map/ppermute | solution.py:53
  41.6 2.7 %collective-permute-start.3 = (bf16[64,64,128]{2,1,0:T(8,128)(2,1)S(1)}, bf16[64,64,128]{2,1,0:T(8,128)(2,1)S(1)}, u32[]{:S(2)}, u32[]{:S(2)}) collective-permute-start(bf16[64,64,128]{2,1,0:T(8,128)(2,1)S(1)} %split_student.1.mine), channel_id=1, source_target_pairs={{0,1},{1,0},{2,3},{3,2},{4,5},{5,4},{6,7},{7,6},{8,9},{9,8},{10,11... | collective-permute-start | bytes 3145736 | tf_op jit(solution)/shard_map/ppermute | solution.py:53
  41.8 5.4 %collective-permute-start.2 = (bf16[64,3584]{1,0:T(8,128)(2,1)S(1)}, bf16[64,3584]{1,0:T(8,128)(2,1)S(1)}, u32[]{:S(2)}, u32[]{:S(2)}) collective-permute-start(bf16[64,3584]{1,0:T(8,128)(2,1)S(1)} %get-tuple-element.26), channel_id=1, source_target_pairs={{0,1},{1,0},{2,3},{3,2},{4,5},{5,4},{6,7},{7,6},{8,9},{9,8},{10,11... | collective-permute-start | bytes 1376264 | tf_op jit(solution)/shard_map/ppermute | solution.py:53
  44.1 3.1 %collective-permute-start.1 = (bf16[2048,128]{1,0:T(8,128)(2,1)S(1)}, bf16[2048,128]{1,0:T(8,128)(2,1)S(1)}, u32[]{:S(2)}, u32[]{:S(2)}) collective-permute-start(bf16[2048,128]{1,0:T(8,128)(2,1)S(1)} %get-tuple-element.25), channel_id=1, source_target_pairs={{0,1},{1,0},{2,3},{3,2},{4,5},{5,4},{6,7},{7,6},{8,9},{9,8},{10,11... | collective-permute-start | bytes 1572872 | tf_op jit(solution)/shard_map/ppermute | solution.py:53
  46.8 17.6 %collective-permute-start.4 = (bf16[64,64,128]{2,1,0:T(8,128)(2,1)S(1)}, bf16[64,64,128]{2,1,0:T(8,128)(2,1)S(1)}, u32[]{:S(2)}, u32[]{:S(2)}) collective-permute-start(bf16[64,64,128]{2,1,0:T(8,128)(2,1)S(1)} %get-tuple-element.29), channel_id=1, source_target_pairs={{0,1},{1,0},{2,3},{3,2},{4,5},{5,4},{6,7},{7,6},{8,9},{9,8},{10,11... | collective-permute-start | bytes 3145736 | tf_op jit(solution)/shard_map/ppermute | solution.py:53
  47.3 17.2 %copy-start.8 = (bf16[4,7168]{1,0:T(4,128)(2,1)S(1)}, bf16[4,7168]{1,0:T(4,128)(2,1)}, u32[]{:S(2)}) copy-start(bf16[4,7168]{1,0:T(4,128)(2,1)} %tokens.1) | copy-start | bytes 172036
  47.3 17.2 %copy-start.10 = (s32[4,8]{1,0:T(4,128)S(1)}, s32[4,8]{1,0:T(4,128)}, u32[]{:S(2)}) copy-start(s32[4,8]{1,0:T(4,128)} %routes.1) | copy-start | bytes 388
  47.3 17.2 %copy-start.11 = (f32[4,8]{1,0:T(4,128)S(1)}, f32[4,8]{1,0:T(4,128)}, u32[]{:S(2)}) copy-start(f32[4,8]{1,0:T(4,128)} %gates.1) | copy-start | bytes 388
  65.6 30.7 %copy-start.6 = (bf16[7168,64]{0,1:T(8,128)(2,1)S(1)}, bf16[7168,64]{0,1:T(8,128)(2,1)}, u32[]{:S(2)}) copy-start(bf16[7168,64]{0,1:T(8,128)(2,1)} %param.20) | copy-start | bytes 2752516
  65.6 30.7 %copy-start.9 = (bf16[128,64]{0,1:T(8,128)(2,1)S(1)}, bf16[128,64]{0,1:T(8,128)(2,1)}, u32[]{:S(2)}) copy-start(bf16[128,64]{0,1:T(8,128)(2,1)} %param.21) | copy-start | bytes 49156
  97.2 4.0 %collective-permute-start.5 = (f32[64,128]{1,0:T(8,128)S(1)}, f32[64,128]{1,0:T(8,128)S(1)}, u32[]{:S(2)}, u32[]{:S(2)}) collective-permute-start(f32[64,128]{1,0:T(8,128)S(1)} %get-tuple-element.31), channel_id=1, source_target_pairs={{0,1},{1,0},{2,3},{3,2},{4,5},{5,4},{6,7},{7,6},{8,9},{9,8},{10,11... | collective-permute-start | bytes 98312 | tf_op jit(solution)/shard_map/ppermute | solution.py:53
  124.0 4.1 %collective-permute-start.6 = (bf16[64,64,128]{2,1,0:T(8,128)(2,1)S(1)}, bf16[64,64,128]{2,1,0:T(8,128)(2,1)S(1)}, u32[]{:S(2)}, u32[]{:S(2)}) collective-permute-start(bf16[64,64,128]{2,1,0:T(8,128)(2,1)S(1)} %all_to_all.29.d_mine), channel_id=1, source_target_pairs={{0,1},{1,0},{2,3},{3,2},{4,5},{5,4},{6,7},{7,6},{8,9},{9,8},{10,11... | collective-permute-start | bytes 3145736 | tf_op jit(solution)/shard_map/ppermute | solution.py:53
